TPU v7x, 32 devices: a whole 2x2x4 slice. The times are simulated.
32 devices in a mesh: ctx: 2 (over y), exp: 4 (over z), dp: 4 (over x, core).
Axes of the slice: x: 2, y: 2, z: 4, core: 2. Of those that a mesh axis runs over, the one named last changes fastest.
Arguments:
- block_in: bfloat16 [16, 256, 1024], P(('exp', 'dp'), 'ctx'), may hold values from -6 to 6
- seg_ids: int32 [16, 256], P(('exp', 'dp')), may hold values from 0 to 6, as said below
- routes: int32 [16, 256, 2], P(('exp', 'dp'), 'ctx'), may hold values from 0 to 3, all different within a row; in each aligned block of 128 rows (0 to 127, 128 to 255, ..., all dimensions but the last counted through in order) at most 96 rows name the same one
- gates: float32 [16, 256, 2], P(('exp', 'dp'), 'ctx'), may hold values from 0.25 to 1
- buckets: int32 [256], replicated, may hold values from 0 to 31, as said below
- norm_attn: float32 [1024], replicated, may hold values from 0.5 to 1.5
- norm_ffn: float32 [1024], replicated, may hold values from 0.5 to 1.5
- w_query: bfloat16 [1024, 1024], replicated, may hold values from -0.1875 to 0.1875
- w_key: bfloat16 [1024, 1024], replicated, may hold values from -0.1875 to 0.1875
- w_value: bfloat16 [1024, 1024], replicated, may hold values from -0.1875 to 0.1875
- w_out_attn: bfloat16 [1024, 1024], replicated, may hold values from -1.5 to 1.5
- rel_bias: float32 [512], replicated, may hold values from -4 to 4
- clip_level: float32 [16], replicated, may hold values from 2 to 6
- w_in: bfloat16 [4, 1024, 5632], P('exp'), may hold values from -0.1875 to 0.1875
- w_down: bfloat16 [4, 2816, 1024], P('exp'), may hold values from -0.109375 to 0.109375
- cotangent: bfloat16 [16, 256, 1024], P(('exp', 'dp'), 'ctx'), may hold values from -6 to 6
Outputs:
- block_out: bfloat16 [16, 256, 1024], P(('exp', 'dp'), 'ctx')
- grad_in: float32 [16, 256, 1024], P(('exp', 'dp'), 'ctx')
- grad_norm_attn: float32 [1024], P(('ctx', 'exp', 'dp'))
- grad_norm_ffn: float32 [1024], P(('ctx', 'exp', 'dp'))
- grad_query: float32 [1024, 1024], P(('ctx', 'exp', 'dp'))
- grad_key: float32 [1024, 1024], P(('ctx', 'exp', 'dp'))
- grad_value: float32 [1024, 1024], P(('ctx', 'exp', 'dp'))
- grad_out_attn: float32 [1024, 1024], P(('ctx', 'exp', 'dp'))
- grad_rel_bias: float32 [512], P(('ctx', 'exp', 'dp'))
- grad_w_in: float32 [4, 1024, 5632], P('exp', ('ctx', 'dp'))
- grad_w_down: float32 [4, 2816, 1024], P('exp', ('ctx', 'dp'))
- clipped_query: float32 [1024, 1024], replicated
- clipped_key: float32 [1024, 1024], replicated
- clip_factor: float32 [16], replicated
Inputs may be any that keep to these rules, and one draw needn't show every extreme that they name: `seg_ids`: numbers never fall along a sequence; the first document ends and the last begins within the first and the last 128 positions; between them one document covers the sequence. In the 128 rows of one device no expert is named by more than 96 routes. `buckets`: never falls as the distance grows; 0 at distance 0 and 31 at the largest distance.
All inputs are finite; a program needn't handle non-finite values.
Results may differ from a plain program's by a relative error of at most 0.012.
The roundings to bfloat16 on the way count: a program that leaves them out, or rounds other values in their place, can miss the bound.
Values may be sent and summed in bfloat16 or wider, within the bound.
No kernel may reach another device: no remote copies, remote signals or barrier semaphores. Data moves between devices by JAX's collectives and lax.ppermute only.
A program may use at most 192 MiB of HBM per device.

v0:
```python
import jax
import jax.numpy as jnp
from jax import lax
from jax.sharding import PartitionSpec as P

HDIM = 64
NB = 32


EPSILON = 1e-06
FULL_PRECISION = lax.Precision.HIGHEST


def rms_norm(block_inputs, scale_gain):
    return (
        block_inputs
        * lax.rsqrt(jnp.mean(block_inputs * block_inputs, axis=-1, keepdims=True) + EPSILON)
        * scale_gain
    )


def gated_unit(gate_part, up_part):
    return jax.nn.gelu(gate_part, approximate=True) * up_part


def transpose_dot(left_rows, right_rows):
    return lax.dot_general(
        left_rows, right_rows, (((0,), (0,)), ((), ())), preferred_element_type=jnp.float32
    )


def dot_back(left_rows, weight_matrix):
    return lax.dot_general(
        left_rows, weight_matrix, (((1,), (1,)), ((), ())), preferred_element_type=jnp.float32
    )


def bias_block(bucket_index, table):
    bucket_count = table.shape[0]
    hot = (
        bucket_index[:, :, None] == jnp.arange(bucket_count, dtype=jnp.int32)[None, None, :]
    ).astype(jnp.float32)
    return jnp.einsum("qkb,bh->hqk", hot, table, precision=FULL_PRECISION)


def head_scores(q_part, k_part, bias_part, allowed, score_scale):
    raw_logits = (
        jnp.einsum("qhd,khd->hqk", q_part, k_part, preferred_element_type=jnp.float32) * score_scale
    )
    return (raw_logits, jnp.where(allowed[None], raw_logits + bias_part, -1e30))


def diagonal_sums(grad_scores, row_start):
    groups, rows, keys = grad_scores.shape
    width = keys + rows
    padded = jnp.concatenate([jnp.zeros((groups, rows, rows), jnp.float32), grad_scores], axis=2)
    flat = jnp.concatenate(
        [padded.reshape(groups, rows * width), jnp.zeros((groups, rows), jnp.float32)], axis=1
    )
    skewed = flat.reshape(groups, rows, width + 1)
    column_sums = jnp.sum(skewed, axis=1)
    extended = jnp.concatenate([jnp.zeros((groups, keys), jnp.float32), column_sums], axis=1)
    flipped = extended[:, ::-1]
    return lax.dynamic_slice_in_dim(flipped, keys - row_start, keys, 1).T


def local(
    block_in,
    seg_ids,
    routes,
    gates,
    buckets,
    norm_attn,
    norm_ffn,
    w_query,
    w_key,
    w_value,
    w_out_attn,
    rel_bias,
    clip_level,
    w_in,
    w_down,
    cotangent,
):
    block_inputs = block_in[0].astype(jnp.float32)
    tok_count, model_width = block_inputs.shape
    head_count = model_width // HDIM
    length = buckets.shape[0]
    score_scale = HDIM ** (-0.5)
    head_group = 2
    ctx_start = lax.axis_index("ctx") * tok_count
    q_pos = ctx_start + jnp.arange(tok_count, dtype=jnp.int32)
    all_pos = jnp.arange(length, dtype=jnp.int32)
    seg_all = seg_ids[0]
    seg_own = lax.dynamic_slice_in_dim(seg_all, ctx_start, tok_count)
    normalized_rows, norm_pull = jax.vjp(rms_norm, block_inputs, norm_attn)
    normed_low = normalized_rows.astype(jnp.bfloat16)
    queries = jnp.dot(normed_low, w_query, preferred_element_type=jnp.float32).astype(jnp.bfloat16)
    key_rows = jnp.dot(normed_low, w_key, preferred_element_type=jnp.float32).astype(jnp.bfloat16)
    value_rows = jnp.dot(normed_low, w_value, preferred_element_type=jnp.float32).astype(
        jnp.bfloat16
    )
    key_all, value_all = (
        lax.all_gather(key_rows, "ctx", axis=0, tiled=True),
        lax.all_gather(value_rows, "ctx", axis=0, tiled=True),
    )
    bucket_hot = (buckets[:, None] == jnp.arange(NB, dtype=jnp.int32)[None, :]).astype(jnp.float32)
    bias_table = rel_bias.reshape(NB, head_count)
    distance = jnp.clip(q_pos[:, None] - all_pos[None, :], 0, length - 1)
    bias_fwd = bias_block(buckets[distance], bias_table)
    allowed = (all_pos[None, :] <= q_pos[:, None]) & (seg_own[:, None] == seg_all[None, :])
    q_heads = queries.reshape(tok_count, head_count, HDIM)
    k_heads = key_all.reshape(length, head_count, HDIM)
    v_heads = value_all.reshape(length, head_count, HDIM)
    outputs, log_parts, peak_parts = ([], [], [])
    for head_start in range(0, head_count, head_group):
        head_cut = slice(head_start, head_start + head_group)
        raw_logits, scores = head_scores(
            q_heads[:, head_cut], k_heads[:, head_cut], bias_fwd[head_cut], allowed, score_scale
        )
        peak_parts.append(jnp.max(jnp.where(allowed[None], raw_logits, -1e30), axis=(1, 2)))
        row_max = jnp.max(scores, axis=-1, keepdims=True)
        exp_scores = jnp.exp(scores - row_max)
        row_sum = jnp.sum(exp_scores, axis=-1, keepdims=True)
        weights_low = (exp_scores / row_sum).astype(jnp.bfloat16)
        outputs.append(
            jnp.einsum(
                "hqk,khd->qhd",
                weights_low,
                v_heads[:, head_cut],
                preferred_element_type=jnp.float32,
            )
        )
        log_parts.append((row_max + jnp.log(row_sum))[:, :, 0])
    attention_output = (
        jnp.concatenate(outputs, axis=1).reshape(tok_count, model_width).astype(jnp.bfloat16)
    )
    log_sums = jnp.concatenate(log_parts, axis=0)
    peak_all = lax.pmax(jnp.concatenate(peak_parts), ("ctx", "exp", "dp"))
    residual_after_attention = block_inputs + jnp.dot(
        attention_output, w_out_attn, preferred_element_type=jnp.float32
    )
    normed_ffn, ffn_pull = jax.vjp(rms_norm, residual_after_attention, norm_ffn)
    sent_rows = normed_ffn.astype(jnp.bfloat16)
    experts = lax.axis_size("exp")
    top_count = routes.shape[-1]
    capacity = tok_count * top_count * 3 // (2 * experts)
    flat_routes = routes[0].reshape(-1)
    one_hot = (flat_routes[:, None] == jnp.arange(experts, dtype=jnp.int32)[None, :]).astype(
        jnp.int32
    )
    slot_index = jnp.sum((jnp.cumsum(one_hot, axis=0) - 1) * one_hot, axis=1)
    outgoing = (
        jnp.zeros((experts, capacity, model_width), jnp.bfloat16)
        .at[flat_routes, slot_index]
        .set(jnp.repeat(sent_rows, top_count, axis=0))
    )
    incoming = lax.all_to_all(outgoing, "exp", split_axis=0, concat_axis=0, tiled=True)
    expert_rows = incoming.reshape(-1, model_width)
    weight_first = w_in[0]
    weight_second = w_down[0]
    ffn_width = weight_second.shape[0]
    gate_up = jnp.dot(expert_rows, weight_first, preferred_element_type=jnp.float32)
    hidden, glu_pull = jax.vjp(gated_unit, gate_up[:, :ffn_width], gate_up[:, ffn_width:])
    hidden_low = hidden.astype(jnp.bfloat16)
    expert_out = (
        jnp.dot(hidden_low, weight_second, preferred_element_type=jnp.float32)
        .astype(jnp.bfloat16)
        .reshape(experts, capacity, model_width)
    )
    returned = lax.all_to_all(expert_out, "exp", split_axis=0, concat_axis=0, tiled=True)
    picked = (
        returned[flat_routes, slot_index]
        .astype(jnp.float32)
        .reshape(tok_count, top_count, model_width)
    )
    mixed = residual_after_attention + jnp.sum(gates[0][:, :, None] * picked, axis=1)
    grad_mix = cotangent[0].astype(jnp.float32)
    grad_routes = (
        (gates[0][:, :, None] * grad_mix[:, None, :]).astype(jnp.bfloat16).reshape(-1, model_width)
    )
    grad_outgoing = (
        jnp.zeros((experts, capacity, model_width), jnp.bfloat16)
        .at[flat_routes, slot_index]
        .set(grad_routes)
    )
    grad_incoming = lax.all_to_all(
        grad_outgoing, "exp", split_axis=0, concat_axis=0, tiled=True
    ).reshape(-1, model_width)
    grad_hidden = dot_back(grad_incoming, weight_second)
    grad_gate, grad_up = glu_pull(grad_hidden)
    grad_gate_up = jnp.concatenate([grad_gate, grad_up], axis=1).astype(jnp.bfloat16)
    grad_second = transpose_dot(hidden_low, grad_incoming)
    grad_first = transpose_dot(expert_rows, grad_gate_up)
    grad_rows = (
        dot_back(grad_gate_up, weight_first)
        .astype(jnp.bfloat16)
        .reshape(experts, capacity, model_width)
    )
    grad_back = lax.all_to_all(grad_rows, "exp", split_axis=0, concat_axis=0, tiled=True)
    grad_normed_ffn = jnp.sum(
        grad_back[flat_routes, slot_index]
        .astype(jnp.float32)
        .reshape(tok_count, top_count, model_width),
        axis=1,
    )
    grad_after, grad_gain_ffn = ffn_pull(grad_normed_ffn)
    grad_after = grad_after + grad_mix
    grad_branch = grad_after.astype(jnp.bfloat16)
    grad_wo = transpose_dot(attention_output, grad_branch)
    grad_att_flat = dot_back(grad_branch, w_out_attn).astype(jnp.bfloat16)
    grad_heads = grad_att_flat.reshape(tok_count, head_count, HDIM)
    grad_q_parts, grad_k_parts, grad_v_parts, dist_parts, delta_parts = ([], [], [], [], [])
    for head_start in range(0, head_count, head_group):
        head_cut = slice(head_start, head_start + head_group)
        raw_logits, scores = head_scores(
            q_heads[:, head_cut], k_heads[:, head_cut], bias_fwd[head_cut], allowed, score_scale
        )
        probs_full = jnp.exp(scores - log_sums[head_cut][:, :, None])
        att_cut = grad_heads[:, head_cut]
        grad_probs = jnp.einsum(
            "qhd,khd->hqk", att_cut, v_heads[:, head_cut], preferred_element_type=jnp.float32
        )
        row_delta = jnp.sum(probs_full * grad_probs, axis=-1, keepdims=True)
        grad_scores = probs_full * (grad_probs - row_delta)
        grad_low = grad_scores.astype(jnp.bfloat16)
        grad_q_parts.append(
            jnp.einsum(
                "hqk,khd->qhd", grad_low, k_heads[:, head_cut], preferred_element_type=jnp.float32
            )
            * score_scale
        )
        dist_parts.append(diagonal_sums(grad_scores, ctx_start))
        delta_parts.append(row_delta[:, :, 0])
        grad_k_parts.append(
            jnp.einsum(
                "hqk,qhd->khd", grad_low, q_heads[:, head_cut], preferred_element_type=jnp.float32
            )
            * score_scale
        )
        grad_v_parts.append(
            jnp.einsum(
                "hqk,qhd->khd",
                probs_full.astype(jnp.bfloat16),
                att_cut,
                preferred_element_type=jnp.float32,
            )
        )
    grad_queries = (
        jnp.concatenate(grad_q_parts, axis=1).reshape(tok_count, model_width).astype(jnp.bfloat16)
    )
    grad_dist = jnp.concatenate(dist_parts, axis=1)
    grad_table = lax.dot_general(
        bucket_hot, grad_dist, (((0,), (0,)), ((), ())), precision=FULL_PRECISION
    ).reshape(-1)
    key_terms = jnp.concatenate(grad_k_parts, axis=1).reshape(length, model_width)
    value_terms = jnp.concatenate(grad_v_parts, axis=1).reshape(length, model_width)
    key_sum, value_sum = (
        lax.psum_scatter(key_terms, "ctx", scatter_dimension=0, tiled=True),
        lax.psum_scatter(value_terms, "ctx", scatter_dimension=0, tiled=True),
    )
    grad_keys = key_sum.astype(jnp.bfloat16)
    grad_values = value_sum.astype(jnp.bfloat16)
    grad_wq = transpose_dot(normed_low, grad_queries)
    grad_wk = transpose_dot(normed_low, grad_keys)
    grad_wv = transpose_dot(normed_low, grad_values)
    grad_normed = (
        dot_back(grad_queries, w_query)
        + dot_back(grad_keys, w_key)
        + dot_back(grad_values, w_value)
    )
    grad_from_norm, grad_gain_attn = norm_pull(grad_normed)
    grad_input = grad_after + grad_from_norm
    shared = (
        lax.psum_scatter(grad_wq, ("ctx", "exp", "dp"), scatter_dimension=0, tiled=True),
        lax.psum_scatter(grad_wk, ("ctx", "exp", "dp"), scatter_dimension=0, tiled=True),
        lax.psum_scatter(grad_wv, ("ctx", "exp", "dp"), scatter_dimension=0, tiled=True),
        lax.psum_scatter(grad_wo, ("ctx", "exp", "dp"), scatter_dimension=0, tiled=True),
        lax.psum_scatter(grad_gain_attn, ("ctx", "exp", "dp"), scatter_dimension=0, tiled=True),
        lax.psum_scatter(grad_gain_ffn, ("ctx", "exp", "dp"), scatter_dimension=0, tiled=True),
        lax.psum_scatter(grad_table, ("ctx", "exp", "dp"), scatter_dimension=0, tiled=True),
    )
    expert_first, expert_second = (
        lax.psum_scatter(grad_first, ("ctx", "dp"), scatter_dimension=0, tiled=True),
        lax.psum_scatter(grad_second, ("ctx", "dp"), scatter_dimension=0, tiled=True),
    )
    factor = clip_level / jnp.maximum(peak_all, clip_level)
    column_scale = jnp.repeat(jnp.sqrt(factor), HDIM)
    clipped_query = w_query.astype(jnp.float32) * column_scale[None, :]
    clipped_key = w_key.astype(jnp.float32) * column_scale[None, :]
    return (
        mixed.astype(jnp.bfloat16)[None],
        grad_input[None],
        shared[4],
        shared[5],
        shared[0],
        shared[1],
        shared[2],
        shared[3],
        shared[6],
        expert_first[None],
        expert_second[None],
        clipped_query,
        clipped_key,
        factor,
    )


def solution(mesh):
    in_specs = (
        P(("exp", "dp"), "ctx", None),
        P(("exp", "dp"), None),
        P(("exp", "dp"), "ctx", None),
        P(("exp", "dp"), "ctx", None),
        P(),
        P(),
        P(),
        P(),
        P(),
        P(),
        P(),
        P(),
        P(),
        P("exp", None, None),
        P("exp", None, None),
        P(("exp", "dp"), "ctx", None),
    )
    out_specs = (
        P(("exp", "dp"), "ctx", None),
        P(("exp", "dp"), "ctx", None),
        P(("ctx", "exp", "dp")),
        P(("ctx", "exp", "dp")),
        P(("ctx", "exp", "dp"), None),
        P(("ctx", "exp", "dp"), None),
        P(("ctx", "exp", "dp"), None),
        P(("ctx", "exp", "dp"), None),
        P(("ctx", "exp", "dp")),
        P("exp", ("ctx", "dp"), None),
        P("exp", ("ctx", "dp"), None),
        P(),
        P(),
        P(),
    )
    return jax.shard_map(local, mesh=mesh, in_specs=in_specs, out_specs=out_specs, check_vma=False)
```

profile of v0, /device:TPU:0, one launch (start us, length us, event | category | flops | bytes accessed | tf_op | source)
XLA Modules:
  0.0 1483.3 jit_solution(15469626891187705497)
XLA Ops:
  11.4 2.2 convolution_convert_fusion.1
  13.6 10.0 all_gather.7
  32.9 8.3 all_gather.6
  43.9 345.2 %gather_fusion = s32[32768]{0:T(1024)} fusion(s32[256]{0:T(256)S(1)} %copy-done.1, s32[32768]{0:T(1024)S(1)} %broadcast_clamp_fusion), kind=kCustom, calls=%fused_computation | custom fusion | bytes 393216 | tf_op jit(solution)/shard_map/gather | solution.py:110
  393.6 2.5 copy.109
  399.2 3.2 fusion.236
  418.2 38.2 %scatter_fusion = bf16[4,96,1024]{2,1,0:T(8,128)(2,1)} fusion(bf16[4,96,1024]{2,1,0:T(8,128)(2,1)} %broadcast.331.clone, s32[256]{0:T(256)S(1)} %bitcast.352, bf16[256,1024]{1,0:T(8,128)(2,1)S(1)} %reshape.506), kind=kCustom, calls=%fused_computation.3 | custom fusion | bytes 1574912 | tf_op jit(solution)/shard_map/scatter | solution.py:156
  456.4 5.1 all-to-all-start
  463.9 2.9 mul.426
  470.7 38.8 %scatter_fusion.1 = bf16[4,96,1024]{2,1,0:T(8,128)(2,1)} fusion(bf16[4,96,1024]{2,1,0:T(8,128)(2,1)} %broadcast.331.clone.1, s32[256]{0:T(256)S(1)} %bitcast.353, bf16[256,1024]{1,0:T(8,128)(2,1)} %multiply_convert_fusion.2), kind=kCustom, calls=%fused_computation.4 | custom fusion | bytes 1574912 | tf_op jit(solution)/shard_map/scatter | solution.py:185
  509.5 4.7 all-to-all-start.2
  514.2 11.1 fusion.2
  525.3 7.0 all-to-all-done.2
  532.3 10.4 fusion.14
  542.8 11.4 fusion.21
  554.1 3.5 all-to-all-start.3
  559.1 6.6 fusion.18
  565.7 11.1 all-to-all-done.3
  576.8 4.2 all-to-all-start.1
  581.5 3.6 gather_fusion.2
  585.1 2.7 reshape.483
  587.8 2.5 reduce_sum.328
  592.9 7.8 all-to-all-done.1
  600.7 4.2 gather_fusion.1
  604.8 2.7 reshape.481
  607.5 2.7 multiply_reduce_fusion
  649.7 2.9 fusion.97
  652.7 2.7 fusion.147
  655.5 3.8 fusion.137
  659.4 13.2 reduce-scatter.11.cloned.1.call-done
  672.6 3.8 fusion.134
  676.5 9.2 fusion.253
  685.8 13.3 fusion.16
  699.9 40.1 %pmax.7 = f32[16]{0:T(128)S(1)} all-reduce(f32[16]{0:T(128)S(1)} %concatenate.132), channel_id=1, replica_groups=mesh['ctx'=2,'exp'=4,'dp'=4] {'ctx','exp','dp'}, use_global_device_ids=true, to_apply=%region_64.65 | all-reduce | flops 16 | bytes 128 | tf_op jit(solution)/shard_map/pmax | solution.py:139
  740.7 6.9 convert_multiply_fusion
  753.0 2.3 reshape.466
  759.9 2.3 reshape.468
  770.0 2.3 reshape.472
  776.9 2.3 reshape.474
  786.3 2.3 reshape.478
  795.6 2.6 fusion.252
  798.2 2.5 convolution_add_fusion.1
  801.7 41.7 %all-reduce.27 = (f32[1024]{0:T(1024)S(1)}, f32[1024]{0:T(1024)S(1)}, f32[512]{0:T(512)S(1)}) all-reduce(f32[1024]{0:T(1024)S(1)} %get-tuple-element.16, f32[1024]{0:T(1024)S(1)} %copy-done.58, f32[512]{0:T(512)S(1)} %reshape.479), channel_id=4, replica_groups=mesh['ctx'=2,'exp'=4,'dp'=4] {'ctx','exp','dp'}, use_global_device_ids=true, to_apply=%region_38.39.clone | all-reduce | flops 2560 | bytes 20480
  846.2 111.0 %reduce-scatter.19.cloned.1.call-done = f32[32,1024]{1,0:T(8,128)} async-done(((f32[1024,1024]{1,0:T(8,128)}), f32[32,1024]{1,0:T(8,128)}) %reduce-scatter.19.cloned.1.call-update) | async-done | bytes 131088 | tf_op jit(solution)/shard_map/reduce_scatter | solution.py:278
  957.2 140.8 %reduce-scatter.15.cloned.1.call-done = f32[32,1024]{1,0:T(8,128)} async-done(((f32[1024,1024]{1,0:T(8,128)}), f32[32,1024]{1,0:T(8,128)}) %reduce-scatter.15.cloned.1.call-update) | async-done | bytes 131088 | tf_op jit(solution)/shard_map/reduce_scatter | solution.py:276
  1097.9 140.5 %reduce-scatter.17.cloned.1.call-done = f32[32,1024]{1,0:T(8,128)} async-done(((f32[1024,1024]{1,0:T(8,128)}), f32[32,1024]{1,0:T(8,128)}) %reduce-scatter.17.cloned.1.call-update) | async-done | bytes 131088 | tf_op jit(solution)/shard_map/reduce_scatter | solution.py:277
  1238.4 87.5 %reduce-scatter.23.cloned.1.call-done = f32[352,1024]{1,0:T(8,128)} async-done(((f32[2816,1024]{1,0:T(8,128)}), f32[352,1024]{1,0:T(8,128)}) %reduce-scatter.23.cloned.1.call-update) | async-done | bytes 1441808 | tf_op jit(solution)/shard_map/reduce_scatter | solution.py:285
  1325.9 150.1 %reduce-scatter.21.cloned.1.call-done = f32[128,5632]{1,0:T(8,128)} async-done(((f32[1024,5632]{1,0:T(8,128)}), f32[128,5632]{1,0:T(8,128)}) %reduce-scatter.21.cloned.1.call-update) | async-done | bytes 2883600 | tf_op jit(solution)/shard_map/reduce_scatter | solution.py:284
  (380 shorter events, 130.8 us)
Async XLA Ops:
  7.2 25.2 %copy-start = (bf16[1024,1024]{1,0:T(8,128)(2,1)S(1)}, bf16[1024,1024]{1,0:T(8,128)(2,1)}, u32[]{:S(2)}) copy-start(bf16[1024,1024]{1,0:T(8,128)(2,1)} %param.25) | copy-start | bytes 6291460
  11.1 19.6 %copy-start.77 = (s32[1,128,2]{1,2,0:T(2,128)S(1)}, s32[1,128,2]{1,2,0:T(2,128)}, u32[]{:S(2)}) copy-start(s32[1,128,2]{1,2,0:T(2,128)} %param.18) | copy-start | bytes 3076
  11.2 21.2 %copy-start.2 = (bf16[1,128,1024]{2,1,0:T(8,128)(2,1)S(1)}, bf16[1,128,1024]{2,1,0:T(8,128)(2,1)}, u32[]{:S(2)}) copy-start(bf16[1,128,1024]{2,1,0:T(8,128)(2,1)} %param.16) | copy-start | bytes 786436
  11.2 21.2 %copy-start.56 = (f32[1024]{0:T(1024)S(1)}, f32[1024]{0:T(1024)}, u32[]{:S(2)}) copy-start(f32[1024]{0:T(1024)} %param.21) | copy-start | bytes 12292
  24.8 374.3 %copy-start.3 = (bf16[256,1024]{0,1:T(8,128)(2,1)}, bf16[256,1024]{0,1:T(8,128)(2,1)S(1)}, u32[]{:S(2)}) copy-start(bf16[256,1024]{0,1:T(8,128)(2,1)S(1)} %copy.82) | copy-start | bytes 1572868
  24.9 19.1 %copy-start.1 = (s32[256]{0:T(256)S(1)}, s32[256]{0:T(256)}, u32[]{:S(2)}) copy-start(s32[256]{0:T(256)} %param.20) | copy-start | bytes 3076
  402.3 8.3 copy-start.27
  402.4 8.5 copy-start.14
  402.4 9.9 copy-start.11
  405.3 8.6 copy-start.60
  414.0 42.4 %copy-start.81 = (f32[128]{0:T(128)}, f32[128]{0:T(128)S(1)}, u32[]{:S(2)}) copy-start(f32[128]{0:T(128)S(1)} %get-tuple-element.78) | copy-start | bytes 1540
  456.4 10.4 copy-start.59
  456.4 53.1 %all-to-all-start = ((bf16[4,96,1024]{2,1,0:T(8,128)(2,1)}), bf16[4,96,1024]{2,1,0:T(8,128)(2,1)S(1)}, u32[]{:S(2)}, u32[]{:S(2)}) async-start(bf16[4,96,1024]{2,1,0:T(8,128)(2,1)} %scatter_fusion), calls=%async_computation | async-start | bytes 1572864 | tf_op jit(solution)/shard_map/all_to_all | solution.py:158
  470.7 43.5 %copy-start.65 = (f32[2,128]{1,0:T(2,128)S(1)}, f32[2,128]{1,0:T(2,128)}, u32[]{:S(2)}) copy-start(f32[2,128]{1,0:T(2,128)} %copy-done.64) | copy-start | bytes 3076
  509.5 15.8 %copy-start.45 = (bf16[4,96,1024]{2,1,0:T(8,128)(2,1)}, bf16[4,96,1024]{2,1,0:T(8,128)(2,1)S(1)}, u32[]{:S(2)}) copy-start(bf16[4,96,1024]{2,1,0:T(8,128)(2,1)S(1)} %all-to-all-done) | copy-start | bytes 2359300
  509.5 22.8 %all-to-all-start.2 = ((bf16[4,96,1024]{2,1,0:T(8,128)(2,1)}), bf16[4,96,1024]{2,1,0:T(8,128)(2,1)}, u32[]{:S(2)}, u32[]{:S(2)}) async-start(bf16[4,96,1024]{2,1,0:T(8,128)(2,1)} %scatter_fusion.1), calls=%async_computation.2 | async-start | bytes 1572864 | tf_op jit(solution)/shard_map/all_to_all | solution.py:187
  542.7 11.4 copy-start.46
  542.7 11.4 copy-start.47
  542.7 14.9 %copy-start.62 = (f32[2,128]{1,0:T(2,128)S(1)}, f32[2,128]{1,0:T(2,128)}, u32[]{:S(2)}) copy-start(f32[2,128]{1,0:T(2,128)} %copy-done.61) | copy-start | bytes 3076
  554.1 22.7 %all-to-all-start.3 = ((bf16[4,96,1024]{2,1,0:T(8,128)(2,1)}), bf16[4,96,1024]{2,1,0:T(8,128)(2,1)S(1)}, u32[]{:S(2)}, u32[]{:S(2)}) async-start(bf16[4,96,1024]{2,1,0:T(8,128)(2,1)} %bitcast.438), calls=%async_computation.3 | async-start | bytes 1572864 | tf_op jit(solution)/shard_map/all_to_all | solution.py:200
  576.8 23.9 %all-to-all-start.1 = ((bf16[4,96,1024]{2,1,0:T(8,128)(2,1)}), bf16[4,96,1024]{2,1,0:T(8,128)(2,1)}, u32[]{:S(2)}, u32[]{:S(2)}) async-start(bf16[4,96,1024]{2,1,0:T(8,128)(2,1)} %bitcast.437), calls=%async_computation.1 | async-start | bytes 1572864 | tf_op jit(solution)/shard_map/all_to_all | solution.py:171
  581.0 74.5 %reduce-scatter.9.cloned.1.call-start = ((), (), s32[]{:S(2)}) async-start(), calls=%async_computation.12 | async-start | bytes 1572864 | tf_op jit(solution)/shard_map/reduce_scatter | solution.py:259
  581.5 11.4 copy-start.82
  592.9 17.4 %copy-start.10 = (f32[128,1024]{1,0:T(8,128)S(1)}, f32[128,1024]{1,0:T(8,128)}, u32[]{:S(2)}) copy-start(f32[128,1024]{1,0:T(8,128)} %copy-done.9) | copy-start | bytes 1572868
  592.9 17.4 %copy-start.53 = (bf16[1,128,1024]{2,1,0:T(8,128)(2,1)S(1)}, bf16[1,128,1024]{2,1,0:T(8,128)(2,1)}, u32[]{:S(2)}) copy-start(bf16[1,128,1024]{2,1,0:T(8,128)(2,1)} %param.31) | copy-start | bytes 786436
  612.3 11.5 copy-start.12
  612.3 12.6 copy-start.15
  615.8 10.4 copy-start.26
  615.8 10.4 copy-start.28
  615.8 11.0 copy-start.22
  615.8 11.0 copy-start.24
  627.9 13.0 copy-start.4
  630.1 18.8 %copy-start.31 = (f32[2,128,256]{2,1,0:T(8,128)S(1)}, f32[2,128,256]{2,1,0:T(8,128)}, u32[]{:S(2)}) copy-start(f32[2,128,256]{2,1,0:T(8,128)} %copy-done.30) | copy-start | bytes 786436
  630.1 42.6 %reduce-scatter.11.cloned.1.call-start = ((), (), s32[]{:S(2)}) async-start(), calls=%async_computation.13 | async-start | bytes 1572864 | tf_op jit(solution)/shard_map/reduce_scatter | solution.py:260
  640.8 205.4 %reduce-scatter.13.cloned.1.call-start = ((), (), s32[]{:S(2)}) async-start(), calls=%async_computation.14 | async-start | bytes 4325376 | tf_op jit(solution)/shard_map/reduce_scatter | solution.py:275
  652.6 304.5 %reduce-scatter.19.cloned.1.call-start = ((), (), s32[]{:S(2)}) async-start(), calls=%async_computation.17 | async-start | bytes 4325376 | tf_op jit(solution)/shard_map/reduce_scatter | solution.py:278
  655.5 442.5 %reduce-scatter.15.cloned.1.call-start = ((), (), s32[]{:S(2)}) async-start(), calls=%async_computation.15 | async-start | bytes 4325376 | tf_op jit(solution)/shard_map/reduce_scatter | solution.py:276
  659.4 579.0 %reduce-scatter.17.cloned.1.call-start = ((), (), s32[]{:S(2)}) async-start(), calls=%async_computation.16 | async-start | bytes 4325376 | tf_op jit(solution)/shard_map/reduce_scatter | solution.py:277
  676.5 649.4 %reduce-scatter.23.cloned.1.call-start = ((), (), s32[]{:S(2)}) async-start(), calls=%async_computation.19 | async-start | bytes 12976128 | tf_op jit(solution)/shard_map/reduce_scatter | solution.py:285
  685.7 790.3 %reduce-scatter.21.cloned.1.call-start = ((), (), s32[]{:S(2)}) async-start(), calls=%async_computation.18 | async-start | bytes 25952256 | tf_op jit(solution)/shard_map/reduce_scatter | solution.py:284
  699.2 40.8 %copy-start.80 = (f32[16]{0:T(128)S(1)}, f32[16]{0:T(128)}, u32[]{:S(2)}) copy-start(f32[16]{0:T(128)} %param.28) | copy-start | bytes 196
  740.7 11.1 copy-start.42
  749.4 15.1 %copy-start.39 = (f32[2,128,256]{2,1,0:T(8,128)S(1)}, f32[2,128,256]{2,1,0:T(8,128)}, u32[]{:S(2)}) copy-start(f32[2,128,256]{2,1,0:T(8,128)} %copy-done.38) | copy-start | bytes 786436
  755.4 13.4 copy-start.37
  766.4 15.1 %copy-start.34 = (f32[2,128,256]{2,1,0:T(8,128)S(1)}, f32[2,128,256]{2,1,0:T(8,128)}, u32[]{:S(2)}) copy-start(f32[2,128,256]{2,1,0:T(8,128)} %copy-done.33) | copy-start | bytes 786436
  772.3 12.8 copy-start.32
  785.1 13.1 copy-start.48
  798.2 47.0 %copy-start.79 = (f32[128]{0:T(128)S(1)}, f32[128]{0:T(128)}, u32[]{:S(2)}) copy-start(f32[128]{0:T(128)} %copy-done.78) | copy-start | bytes 1540
  (47 other events, 153.5 us)
Sparse Core Ops, SparseCore 0:
  630.2 19.7 reduce-scatter.8
  652.3 20.3 reduce-scatter.10
  675.5 141.4 reduce-scatter.12
  819.7 137.4 reduce-scatter.18
  959.9 138.0 reduce-scatter.14
  1100.6 137.7 reduce-scatter.16
  1242.5 83.3 reduce-scatter.22
  1330.1 145.8 reduce-scatter.20
where the time goes:
time: 1500 us; the launch traced here: 1480 us
  waiting for transfers between devices  669 us (45%)
  local copies, waits for them, and re-layouts  505 us (34%)
  matrix products  138 us (9%)
  blocking collectives  100 us (7%)
  other arithmetic  37 us (2%)
  starting transfers between devices  18.2 us (1%)
  between operations  15.9 us (1%)
    gather x2, local copies, waits for them, and re-layouts, local(): bias_fwd = bias_block(buckets[distance], bias_table)  346 us
    reduce_scatter x1, waiting for transfers between devices, local(): lax.psum_scatter(grad_first, ('ctx', 'dp'), scatter_dimension=0, tiled=True)  150 us
    reduce_scatter x1, waiting for transfers between devices, local(): lax.psum_scatter(grad_wk, ('ctx', 'exp', 'dp'), scatter_dimension=0, tile...  141 us
    reduce_scatter x1, waiting for transfers between devices, local(): lax.psum_scatter(grad_wv, ('ctx', 'exp', 'dp'), scatter_dimension=0, tile...  140 us
    reduce_scatter x1, waiting for transfers between devices, local(): lax.psum_scatter(grad_wo, ('ctx', 'exp', 'dp'), scatter_dimension=0, tile...  111 us
    reduce_scatter x1, waiting for transfers between devices, local(): lax.psum_scatter(grad_second, ('ctx', 'dp'), scatter_dimension=0, tiled=T...  87.5 us
    unnamed x1, blocking collectives  41.7 us
    pmax x1, blocking collectives, local(): peak_all = lax.pmax(jnp.concatenate(peak_parts), ('ctx', 'exp', 'dp'))  40.1 us
  transfers between devices with their start and end apart: 12, of which 9 were waited for; matrix products, arithmetic and copies ran while one was open for 13% of the time, Pallas kernels for 0%

commit v1 on v0

v1 whole, which is shorter than its diff:
```python
import functools

import jax
import jax.numpy as jnp
from jax import lax
from jax.experimental import pallas as pl
from jax.experimental.pallas import tpu as pltpu
from jax.sharding import PartitionSpec as P

HDIM = 64
NB = 32
GROUP = 4
LANES = 128
EPSILON = 1e-06
FULL_PRECISION = lax.Precision.HIGHEST
LOW = jnp.bfloat16
FULL = jnp.float32
OUTSIDE = -1e30
GELU_SCALE = 0.7978845608028654
GELU_CUBE = 0.044715


def rms_norm(rows, gain):
    return rows * lax.rsqrt(jnp.mean(rows * rows, axis=-1, keepdims=True) + EPSILON) * gain


def dot_rows(left, right):
    return lax.dot_general(left, right, (((1,), (0,)), ((), ())), preferred_element_type=FULL)


def dot_back(left, right):
    return lax.dot_general(left, right, (((1,), (1,)), ((), ())), preferred_element_type=FULL)


def transpose_dot(left, right):
    return lax.dot_general(left, right, (((0,), (0,)), ((), ())), preferred_element_type=FULL)


def swapped(array, axis, bit):
    size = lax.axis_size(axis)
    return lax.ppermute(array, axis, [(i, i ^ bit) for i in range(size)])


def over_experts(blocks):
    return lax.all_to_all(blocks, "exp", split_axis=0, concat_axis=0, tiled=True)


MICROSECOND = 1.15e9


def call(
    body, name, inputs, outputs, us, grid=(1,), token=None, prefetch=(), scratch=(), vmem=12,
    near_in=(), near_out=(),
):
    n_pre, n_in, n_out = len(prefetch), len(inputs), len(outputs)
    held = [] if token is None else [token]

    def kernel(*refs):
        split = n_pre + n_in
        outs = split + len(held)
        refs[outs + n_out][...] = jnp.zeros((8, LANES), FULL)
        body(*refs[:split], *refs[outs : outs + n_out], *refs[outs + n_out + 1 :])

    where = lambda at, near: pltpu.VMEM if at in near else pltpu.HBM
    arrays = [
        pltpu.with_memory_space_constraint(array, where(at, near_in))
        for at, (array, _) in enumerate(inputs)
    ]
    held = [pltpu.with_memory_space_constraint(array, pltpu.HBM) for array in held]
    results = pl.pallas_call(
        kernel,
        grid_spec=pltpu.PrefetchScalarGridSpec(
            num_scalar_prefetch=n_pre,
            grid=grid,
            in_specs=[spec for _, spec in inputs]
            + [pl.BlockSpec(memory_space=pl.ANY)] * len(held),
            out_specs=[spec for _, _, spec in outputs]
            + [pl.BlockSpec((8, LANES), lambda *_: (0, 0))],
            scratch_shapes=list(scratch),
        ),
        out_shape=[
            where(at, near_out)(shape, dtype) for at, (shape, dtype, _) in enumerate(outputs)
        ]
        + [pltpu.HBM((8, LANES), FULL)],
        cost_estimate=pl.CostEstimate(
            flops=int(us * MICROSECOND), bytes_accessed=1, transcendentals=0
        ),
        compiler_params=pltpu.CompilerParams(vmem_limit_bytes=vmem * 2**20),
        name=name,
    )(*prefetch, *arrays, *held)
    return list(results[:-1]), results[-1]


def whole(array):
    return array, pl.BlockSpec(array.shape, lambda *_: (0,) * array.ndim)


def whole_out(shape, dtype):
    return shape, dtype, pl.BlockSpec(shape, lambda *_: (0,) * len(shape))


def hold(token, *arrays):
    anywhere = pl.BlockSpec(memory_space=pl.ANY)
    return pl.pallas_call(
        lambda *refs: None,
        in_specs=[anywhere] * (len(arrays) + 1),
        out_specs=[anywhere] * len(arrays),
        out_shape=[jax.ShapeDtypeStruct(array.shape, array.dtype) for array in arrays],
        input_output_aliases={at + 1: at for at in range(len(arrays))},
        cost_estimate=pl.CostEstimate(flops=1, bytes_accessed=1, transcendentals=0),
        name="hold",
    )(token, *arrays)


def eye(size):
    rows = lax.broadcasted_iota(jnp.int32, (size, size), 0)
    return rows == lax.broadcasted_iota(jnp.int32, (size, size), 1)


def to_column(row):
    size = row.shape[1]
    return jnp.sum(jnp.where(eye(size), row, jnp.zeros_like(row)), 1, keepdims=True)


def front_kernel(
    at_ref, routes_ref, gates_ref, grad_ref, seg_ref, spread_ref, pick_ref, out_ref, mask_ref
):
    top, tokens = routes_ref.shape
    experts, capacity, _ = out_ref.shape
    routes = [routes_ref[r : r + 1, :] for r in range(top)]
    gates = [gates_ref[r : r + 1, :] for r in range(top)]
    before = lax.broadcasted_iota(jnp.int32, (tokens, tokens), 0)
    before = before < lax.broadcasted_iota(jnp.int32, (tokens, tokens), 1)
    slots = lax.broadcasted_iota(jnp.int32, (capacity, tokens), 0).astype(FULL)
    for e in range(experts):
        part = pl.ds(e * capacity, capacity)
        hits = [jnp.where(route == e, 1.0, 0.0) for route in routes]
        named = functools.reduce(jnp.add, hits)
        slot = jnp.sum(jnp.where(before, to_column(named), 0.0), 0, keepdims=True)
        place = (slots == slot).astype(FULL)
        spread = place * named
        gate = functools.reduce(jnp.add, [hit * g for hit, g in zip(hits, gates)])
        spread_low = spread.astype(LOW)
        spread_ref[part, :] = spread_low
        for r in range(top):
            pick_ref[part, pl.ds(r * tokens, tokens)] = (place * hits[r]).astype(LOW)
        slot_gate = jnp.sum(spread * gate, 1, keepdims=True)
        out_ref[e] = (slot_gate * dot_rows(spread_low, grad_ref[...])).astype(LOW)
    length = mask_ref.shape[1]
    ctx = at_ref[0]
    seg = jnp.broadcast_to(seg_ref[...].astype(FULL), (8, length))
    keys = pltpu.roll(seg, length - (ctx + 1) * tokens, 1)[:1, :]
    at_row = lax.broadcasted_iota(jnp.int32, (tokens, length), 0) + (length - tokens)
    at_key = lax.broadcasted_iota(jnp.int32, (tokens, length), 1)
    own = jnp.sum(jnp.where(at_row == at_key, keys, 0.0), 1, keepdims=True)
    allowed = (at_key <= at_row) & (own == keys) & (at_key >= length - (ctx + 1) * tokens)
    mask_ref[...] = jnp.where(allowed, 0.0, OUTSIDE)


def front(at, routes, gates, grad, seg, experts, capacity):
    top, tokens = routes.shape
    slots = experts * capacity
    return call(
        front_kernel,
        "front",
        [whole(routes), whole(gates), whole(grad), whole(seg)],
        [
            whole_out((slots, tokens), LOW),
            whole_out((slots, top * tokens), LOW),
            whole_out((experts, capacity, grad.shape[1]), LOW),
            whole_out((tokens, seg.shape[1]), FULL),
        ],
        prefetch=(at,),
        us=1.5,
    near_out=(0, 3),
        )


def bias_kernel(buckets_ref, table_ref, hot_ref, bias_ref, by_lane):
    group, rows, keys = bias_ref.shape
    width = hot_ref.shape[1]
    step = pl.program_id(0)

    @pl.when(step == 0)
    def _():
        buckets = buckets_ref[...].astype(FULL)
        column = jnp.sum(jnp.where(eye(keys), buckets, 0.0), 1, keepdims=True)
        distance = lax.broadcasted_iota(jnp.int32, (keys, width), 0)
        lane = lax.broadcasted_iota(jnp.int32, (keys, width), 1)
        turned = jnp.sum(jnp.where(distance + lane == keys - 1, column, 0.0), 0, keepdims=True)
        bucket = lax.broadcasted_iota(jnp.int32, (NB, width), 0).astype(FULL)
        hot = jnp.where(bucket == turned, 1.0, 0.0)
        hot_ref[...] = hot
        lines = lax.dot_general(
            table_ref[...], hot, (((0,), (0,)), ((), ())), precision=FULL_PRECISION,
            preferred_element_type=FULL,
        )
        by_lane[...] = lines

    for at in range(group):
        line = jnp.broadcast_to(by_lane[pl.ds(step * group + at, 1), :], (8, width))
        line = pltpu.roll(line, keys + 1, 1, stride=1, stride_axis=0)
        for start in range(0, rows, 8):
            moved = line if start == 0 else pltpu.roll(line, start, 1)
            bias_ref[at, pl.ds(start, 8), :] = moved[:, :keys]


def bias_tiles(buckets, table, rows):
    heads, keys = table.shape[1], buckets.shape[1]
    width = keys + rows
    return call(
        bias_kernel,
        "bias_tiles",
        [whole(buckets), whole(table)],
        [
            whole_out((NB, width), FULL),
            ((heads, rows, keys), FULL, pl.BlockSpec((GROUP, rows, keys), lambda g: (g, 0, 0))),
        ],
        grid=(heads // GROUP,),
        scratch=[pltpu.VMEM((heads, width), FULL)],
        us=2.5,
        near_out=(1,),
    )


def half_lanes(half, shape):
    lane = lax.broadcasted_iota(jnp.int32, shape, 1)
    return lane < HDIM if half == 0 else lane >= HDIM


def attention_kernel(q_ref, k_ref, v_ref, bias_ref, mask_ref, out_ref, probs_ref, peak_ref):
    mask = mask_ref[...]
    for pair in range(GROUP // 2):
        lanes = pl.ds(pair * LANES, LANES)
        queries, keys, values = q_ref[:, lanes], k_ref[:, lanes], v_ref[:, lanes]
        parts = []
        for half in range(2):
            at = 2 * pair + half
            own = half_lanes(half, queries.shape)
            raw = dot_back(jnp.where(own, queries, jnp.zeros_like(queries)), keys)
            raw = raw * HDIM**-0.5 + mask
            top = jnp.max(raw, axis=0, keepdims=True)
            best = top[:, :LANES]
            for start in range(LANES, top.shape[1], LANES):
                best = jnp.maximum(best, top[:, start : start + LANES])
            peak_ref[0, at : at + 1, :] = best
            scores = raw + bias_ref[at]
            raised = jnp.exp(scores - jnp.max(scores, axis=1, keepdims=True))
            probs = raised * (1.0 / jnp.sum(raised, axis=1, keepdims=True))
            probs_ref[at] = probs
            parts.append(dot_rows(probs.astype(LOW), values))
        first = half_lanes(0, parts[0].shape)
        out_ref[:, lanes] = jnp.where(first, parts[0], parts[1]).astype(LOW)


def column_spec(size):
    return pl.BlockSpec((size, GROUP * HDIM), lambda g: (0, g))


def attention(queries, keys, values, bias, mask):
    rows, width = queries.shape
    length = keys.shape[0]
    heads = width // HDIM
    groups = heads // GROUP
    tile = pl.BlockSpec((GROUP, rows, length), lambda g: (g, 0, 0))
    (out, probs, peak), _ = call(
        attention_kernel,
        "attention",
        [
            (queries, column_spec(rows)),
            (keys, column_spec(length)),
            (values, column_spec(length)),
            (bias, tile),
            whole(mask),
        ],
        [
            ((rows, width), LOW, column_spec(rows)),
            ((heads, rows, length), FULL, tile),
            ((groups, 8, LANES), FULL, pl.BlockSpec((1, 8, LANES), lambda g: (g, 0, 0))),
        ],
        grid=(groups,),
        near_in=(0, 1, 2, 3, 4),
        near_out=(0, 1),
        us=4.5,
    )
    return out, probs, peak


def attention_back_kernel(q_ref, k_ref, v_ref, probs_ref, grad_ref, dq_ref, dk_ref, dv_ref, lines_ref):
    rows, length = probs_ref.shape[1:]
    scale = HDIM**-0.5
    for pair in range(GROUP // 2):
        lanes = pl.ds(pair * LANES, LANES)
        queries, keys, values, grad = (ref[:, lanes] for ref in (q_ref, k_ref, v_ref, grad_ref))
        dq, dk, dv = [], [], []
        for half in range(2):
            at = 2 * pair + half
            own = half_lanes(half, grad.shape)
            dp = dot_back(jnp.where(own, grad, jnp.zeros_like(grad)), values)
            probs = probs_ref[at]
            ds = probs * (dp - jnp.sum(probs * dp, axis=1, keepdims=True))
            ds_low = ds.astype(LOW)
            dq.append(dot_rows(ds_low, keys))
            dk.append(transpose_dot(ds_low, queries))
            dv.append(transpose_dot(probs.astype(LOW), grad))
            wide = jnp.concatenate([ds, jnp.zeros((rows, rows), FULL)], axis=1)
            total = wide[rows - 8 :, :]
            for start in range(0, rows - 8, 8):
                total = total + pltpu.roll(wide[start : start + 8, :], rows - 8 - start, 1)
            line = lax.broadcasted_iota(jnp.int32, total.shape, 0)
            for bit in (1, 2, 4):
                total = jnp.where(((7 - line) & bit) != 0, pltpu.roll(total, bit, 1), total)
            lines_ref[0, at : at + 1, :] = jnp.sum(total, axis=0, keepdims=True)
        first = half_lanes(0, dq[0].shape)
        dq_ref[:, lanes] = (jnp.where(first, dq[0], dq[1]) * scale).astype(LOW)
        first = half_lanes(0, dk[0].shape)
        dk_ref[:, lanes] = (jnp.where(first, dk[0], dk[1]) * scale).astype(LOW)
        dv_ref[:, lanes] = jnp.where(first, dv[0], dv[1]).astype(LOW)


def packed_back_kernel(
    q_ref, k_ref, v_ref, probs_ref, grad_ref, branch_ref, hot_ref, gain_ref, out_ref, lines_ref, small
):
    rows, length = probs_ref.shape[1:]
    ends = [0, rows, rows + length, rows + 2 * length, 2 * rows + 2 * length]
    parts = [out_ref.at[pl.ds(a, b - a), :] for a, b in zip(ends, ends[1:])]
    attention_back_kernel(q_ref, k_ref, v_ref, probs_ref, grad_ref, *parts[:3], lines_ref)
    parts[3][...] = branch_ref[...]
    step = pl.program_id(0)
    devices, width = small.shape[0], gain_ref.shape[1]
    own = width // devices

    @pl.when(step == 0)
    def _():
        device = lax.broadcasted_iota(jnp.int32, (devices, width), 0)
        feature = lax.broadcasted_iota(jnp.int32, (devices, width), 1)
        spread = jnp.where(feature // own == device, gain_ref[...], 0.0)
        feature = lax.broadcasted_iota(jnp.int32, (width, LANES), 0)
        lane = lax.broadcasted_iota(jnp.int32, (width, LANES), 1)
        small[...] = jnp.dot(
            spread, jnp.where(feature % own == lane, 1.0, 0.0), precision=FULL_PRECISION,
            preferred_element_type=FULL,
        )

    head = lax.broadcasted_iota(jnp.int32, (8, LANES), 0)
    lane = lax.broadcasted_iota(jnp.int32, (8, LANES), 1)
    lines = jnp.where(lax.broadcasted_iota(jnp.int32, lines_ref.shape[1:], 0) < GROUP, lines_ref[0], 0.0)
    table = lax.dot_general(
        hot_ref[...], lines, (((1,), (1,)), ((), ())), precision=FULL_PRECISION,
        preferred_element_type=FULL,
    )
    to_lane = jnp.where(lane == TABLE_LANE + step * GROUP + head, 1.0, 0.0)
    small[...] += jnp.dot(table, to_lane, precision=FULL_PRECISION, preferred_element_type=FULL)
    out_ref[pl.ds(ends[4], devices), :] = jnp.zeros((devices, out_ref.shape[1]), LOW)
    out_ref[pl.ds(ends[4], devices), :LANES] = small[...].astype(LOW)


def attention_back(queries, keys, values, probs, grad, token, packed=None):
    rows, width = queries.shape
    length = keys.shape[0]
    heads = width // HDIM
    groups = heads // GROUP
    lines = (
        (groups, 8, length + rows), FULL, pl.BlockSpec((1, 8, length + rows), lambda g: (g, 0, 0))
    )
    inputs = [
        (queries, column_spec(rows)),
        (keys, column_spec(length)),
        (values, column_spec(length)),
        (probs, pl.BlockSpec((GROUP, rows, length), lambda g: (g, 0, 0))),
        (grad, column_spec(rows)),
    ]
    if packed is None:
        outs, token = call(
            attention_back_kernel,
            "attention_back",
            inputs,
            [((size, width), LOW, column_spec(size)) for size in (rows, length, length)] + [lines],
            grid=(groups,),
            token=token,
            us=6.6,
        )
        return *outs, token
    branch, hot, gain, devices = packed
    total = 2 * rows + 2 * length + devices
    (out, _), token = call(
        packed_back_kernel,
        "attention_back",
        inputs + [(branch, column_spec(rows)), whole(hot), whole(gain)],
        [((total, width), LOW, column_spec(total)), lines],
        grid=(groups,),
        token=token,
        scratch=[pltpu.VMEM((devices, LANES), FULL)],
        near_in=(0, 1, 2, 3, 4, 5),
        near_out=(0,),
        us=7,
    )
    return out, token


def expert_part(rows, grad, gate_w, up_w, down_w):
    gate = dot_rows(rows, gate_w)
    up = dot_rows(rows, up_w)
    dhid = dot_back(grad, down_w)
    square = gate * gate
    curve = jnp.tanh(GELU_SCALE * gate * (1.0 + GELU_CUBE * square))
    upper = 0.5 * (1.0 + curve)
    gelu = gate * upper
    slope = upper + 0.5 * gate * (1.0 - curve * curve) * (
        GELU_SCALE * (1.0 + 3.0 * GELU_CUBE * square)
    )
    hid = (gelu * up).astype(LOW)
    dgate = (dhid * up * slope).astype(LOW)
    dup = (dhid * gelu).astype(LOW)
    return hid, dgate, dup, dot_rows(hid, down_w), dot_back(dgate, gate_w) + dot_back(dup, up_w)


def expert_kernel(
    rows_ref, grad_ref, gate_w_ref, up_w_ref, down_w_ref,
    out_ref, back_ref, dgate_ref, dup_ref, hid_ref, turned_ref, out_sum, back_sum,
):
    step = pl.program_id(0)

    @pl.when(step == 0)
    def _():
        out_sum[...] = jnp.zeros_like(out_sum)
        back_sum[...] = jnp.zeros_like(back_sum)

    hid, dgate, dup, out_more, back_more = expert_part(
        rows_ref[...], grad_ref[...], gate_w_ref[0], up_w_ref[0], down_w_ref[0]
    )
    dgate_ref[...] = dgate
    dup_ref[...] = dup
    hid_ref[...] = hid.T
    out_sum[...] += out_more
    back_sum[...] += back_more

    @pl.when(step == pl.num_programs(0) - 1)
    def _():
        out_ref[...] = out_sum[...].astype(LOW)
        back_ref[...] = back_sum[...].astype(LOW)
        turned_ref[...] = rows_ref[...].T


def expert(rows, grad, w_in, w_down, token):
    count, width = rows.shape
    hidden = w_down.shape[1]
    part = 256
    steps = hidden // part
    return call(
        expert_kernel,
        "expert",
        [
            whole(rows),
            whole(grad),
            (w_in, pl.BlockSpec((1, width, part), lambda i: (0, 0, i))),
            (w_in, pl.BlockSpec((1, width, part), lambda i: (0, 0, i + steps))),
            (w_down, pl.BlockSpec((1, part, width), lambda i: (0, i, 0))),
        ],
        [
            whole_out((count, width), LOW),
            whole_out((count, width), LOW),
            ((count, hidden), LOW, pl.BlockSpec((count, part), lambda i: (0, i))),
            ((count, hidden), LOW, pl.BlockSpec((count, part), lambda i: (0, i))),
            ((hidden, count), LOW, pl.BlockSpec((part, count), lambda i: (i, 0))),
            whole_out((width, count), LOW),
        ],
        grid=(steps,),
        token=token,
        scratch=[pltpu.VMEM((count, width), FULL), pltpu.VMEM((count, width), FULL)],
        vmem=24,
        us=20,
    )


PART = 256


def halves_kernel(*refs):
    x_refs, g_refs, w_refs = refs[1:3], refs[3:5], refs[5:11]
    out_keep, out_send, back_keep, back_send, dgate_ref, dup_ref, a_ref, b_ref, turned_ref = refs[11:20]
    out_sum, back_sum = refs[20:]
    step, last = pl.program_id(0), pl.num_programs(0) - 1
    count = x_refs[0].shape[0]

    @pl.when(step == 0)
    def _():
        out_sum[...] = jnp.zeros_like(out_sum)
        back_sum[...] = jnp.zeros_like(back_sum)

    def part(units):
        blocks = units // LANES
        gate_w = jnp.concatenate([ref[0] for ref in w_refs[0:blocks]], axis=1)
        up_w = jnp.concatenate([ref[0] for ref in w_refs[2 : 2 + blocks]], axis=1)
        down_w = jnp.concatenate([ref[0] for ref in w_refs[4 : 4 + blocks]], axis=0)
        down_g = None
        for half in range(2):
            rows = pl.ds(half * count, count)
            hid, dgate, dup, out_more, back_more = expert_part(
                x_refs[half][...], g_refs[half][...], gate_w, up_w, down_w
            )
            dgate_ref[rows, pl.ds(0, units)] = dgate
            dup_ref[rows, pl.ds(0, units)] = dup
            more = transpose_dot(hid, g_refs[half][...])
            down_g = more if half == 0 else down_g + more
            out_sum[rows, :] += out_more
            back_sum[rows, :] += back_more
        width = down_g.shape[1] // 2
        a_ref[pl.ds(0, units), :] = down_g[:, :width].astype(LOW)
        b_ref[pl.ds(0, units), :] = down_g[:, width:].astype(LOW)

    @pl.when(step < last)
    def _():
        part(PART)

    @pl.when(step == last)
    def _():
        part(PART // 2)
        own, other = pl.ds(0, count), pl.ds(count, count)
        back_keep[...] = back_sum[own, :]
        back_send[...] = back_sum[other, :].astype(LOW)
        out_keep[...] = out_sum[own, :]
        out_send[...] = out_sum[other, :].astype(LOW)
        for half in range(2):
            turned_ref[:, pl.ds(half * count, count)] = x_refs[half][...].T


def expert_halves(at, rows, grads, w_in, w_down, token):
    count, width = rows[0].shape
    hidden = w_down.shape[1]
    units = hidden // (2 * LANES)
    steps = (units + 1) // 2

    def block(step, at, second):
        return at[2] * units + jnp.minimum(2 * step + second, units - 1)

    column = lambda first, second: pl.BlockSpec(
        (1, width, LANES), lambda i, at: (0, 0, first + block(i, at, second))
    )
    row = lambda second: pl.BlockSpec((1, LANES, width), lambda i, at: (0, block(i, at, second), 0))
    shape = (count, width)
    return call(
        halves_kernel,
        "expert_halves",
        [whole(array) for array in (*rows, *grads)]
        + [(w_in, column(first, second)) for first in (0, 2 * units) for second in range(2)]
        + [(w_down, row(second)) for second in range(2)],
        [
            whole_out(shape, FULL),
            whole_out(shape, LOW),
            whole_out(shape, FULL),
            whole_out(shape, LOW),
            ((2 * count, steps * PART), LOW, pl.BlockSpec((2 * count, PART), lambda i, at: (0, i))),
            ((2 * count, steps * PART), LOW, pl.BlockSpec((2 * count, PART), lambda i, at: (0, i))),
            ((hidden // 2, width // 2), LOW, pl.BlockSpec((PART, width // 2), lambda i, at: (i, 0))),
            ((hidden // 2, width // 2), LOW, pl.BlockSpec((PART, width // 2), lambda i, at: (i, 0))),
            whole_out((width, 2 * count), LOW),
        ],
        grid=(steps,),
        token=token,
        prefetch=(at,),
        scratch=[pltpu.VMEM((2 * count, width), FULL)] * 2,
        vmem=40,
        near_in=(0, 1, 2, 3),
        near_out=(2, 3, 4, 5, 6, 7, 8),
        us=24,
    )


def join_kernel(kept_ref, got_ref, out_ref):
    out_ref[...] = (kept_ref[...] + got_ref[...].astype(FULL)).astype(LOW).reshape(out_ref.shape)


def join(kept, got, shape, token):
    (out,), token = call(
        join_kernel,
        "join",
        [whole(kept), whole(got)],
        [whole_out(shape, LOW)],
        token=token,
        near_in=(0, 1),
        near_out=(0,),
        us=1,
    )
    return out, token


def join_peak_kernel(kept_ref, got_ref, peak_ref, out_ref):
    blocks, size, width = out_ref.shape
    rows = kept_ref.shape[0] // blocks
    best = jnp.concatenate([peak_ref[g, :GROUP, :] for g in range(peak_ref.shape[0])], axis=0)
    best = jnp.broadcast_to(jnp.max(best, axis=1, keepdims=True), (size - rows, LANES))
    upper = best.astype(LOW)
    lower = (best - upper.astype(FULL)).astype(LOW)
    for block in range(blocks):
        part = pl.ds(block * rows, rows)
        total = kept_ref[part, :] + got_ref[part, :].astype(FULL)
        out_ref[block, :rows, :] = total.astype(LOW)
        out_ref[block, rows:, :] = jnp.zeros((size - rows, width), LOW)
        out_ref[block, rows:, :LANES] = upper
        out_ref[block, rows:, LANES : 2 * LANES] = lower


def join_peak(kept, got, peak, blocks, token):
    rows, width = kept.shape
    heads = peak.shape[0] * GROUP
    (out,), token = call(
        join_peak_kernel,
        "join_peak",
        [whole(kept), whole(got), whole(peak)],
        [whole_out((blocks, rows // blocks + heads, width), LOW)],
        token=token,
        us=1.5,
    )
    return out, token


def larger_kernel(one_ref, two_ref, out_ref):
    out_ref[...] = jnp.maximum(one_ref[...], two_ref[...])


def larger(one, two, token):
    (out,), token = call(
        larger_kernel,
        "larger",
        [whole(one), whole(two)],
        [whole_out(one.shape, FULL)],
        token=token,
        near_in=(0, 1),
        near_out=(0,),
        us=0.5,
    )
    return out, token


def place():
    dp = lax.axis_index("dp")
    return lax.axis_index("ctx"), lax.axis_index("exp"), dp // 2, dp % 2


def pick_block(blocks, index):
    return lax.dynamic_index_in_dim(blocks, index, 0, keepdims=False)


def to_down_plane(array):
    pairs = [
        ((1 - core) * 4 + x * 2 + core, core * 4 + x * 2 + core)
        for core in range(2)
        for x in range(2)
    ]
    return lax.ppermute(array, ("ctx", "dp"), pairs)


def in_down_plane(array):
    pairs = [
        (core * 4 + x * 2 + core, core * 4 + (1 - x) * 2 + core)
        for core in range(2)
        for x in range(2)
    ]
    return lax.ppermute(array, ("ctx", "dp"), pairs)


def in_kernel(
    at_ref, rows_ref, gate_ref, up_ref, a_send_ref, a_keep_ref, b_send_ref, b_keep_ref
):
    size = a_send_ref.shape[1]
    right = jnp.concatenate([gate_ref[...], up_ref[...]], axis=1)
    for block in range(4):
        ry, rx = block // 2, block % 2
        chip = (at_ref[0] ^ ry) * 2 + (at_ref[1] ^ rx)
        both = dot_rows(rows_ref[pl.ds(chip * size, size), :], right)
        a, b = both[:, :LANES], both[:, LANES:]
        (a_send_ref if rx else a_keep_ref)[ry] = a.astype(LOW)
        (b_send_ref if ry else b_keep_ref)[rx] = b.astype(LOW)


def in_terms(at, rows, gate, up, hidden, token):
    width, count = rows.shape
    size = width // 4
    right = pl.BlockSpec((count, LANES), lambda i, at: (0, i))
    spec = pl.BlockSpec((2, size, LANES), lambda i, at: (0, 0, i))
    shape = (2, size, hidden // 2)
    return call(
        in_kernel,
        "in_terms",
        [whole(rows), (gate, right), (up, right)],
        [(shape, LOW, spec)] * 4,
        grid=(hidden // (2 * LANES),),
        token=token,
        prefetch=(at,),
        near_in=(0, 1, 2),
        near_out=(0, 2),
        us=6,
    )


def plane_first(parts):
    a_send, a_keep, b_send, b_keep = parts
    return swapped(a_send, "dp", 2), a_keep, swapped(b_send, "ctx", 1), b_keep


def second_kernel(a_ref, a_keep_ref, b_ref, b_keep_ref, a_send_ref, b_send_ref):
    a_send_ref[...] = (a_keep_ref[...].astype(FULL) + a_ref[...].astype(FULL)).astype(LOW)
    b_send_ref[...] = (b_keep_ref[...].astype(FULL) + b_ref[...].astype(FULL)).astype(LOW)


def second_terms(parts, token, cuts, us):
    inputs = []
    for part, axis in zip(parts, cuts):
        if axis is None:
            inputs.append(whole(part))
        else:
            shape = part.shape[:axis] + (None,) + part.shape[axis + 1 :]
            index = tuple(int(at == axis) for at in range(part.ndim))
            inputs.append((part, pl.BlockSpec(shape, lambda *_, index=index: index)))
    shapes = [
        tuple(size for size in spec.block_shape if size is not None)
        for _, spec in (inputs[0], inputs[2])
    ]
    return call(
        second_kernel,
        "second_terms",
        inputs,
        [whole_out(shape, LOW) for shape in shapes],
        token=token,
        us=us,
    )


def plane_second(parts, token, axis=0, us=1.5):
    (a_send, b_send), token = second_terms(parts, token, (axis,) * 4, us)
    return (parts, swapped(a_send, "ctx", 1), swapped(b_send, "dp", 2)), token


def plane_last(parts, axis=0):
    (a, a_keep, b, b_keep), a2, b2 = parts
    cut = lambda array: lax.index_in_dim(array, 0, axis, keepdims=False).astype(FULL)
    return cut(a_keep) + cut(a) + a2.astype(FULL), cut(b_keep) + cut(b) + b2.astype(FULL)


def down_last_kernel(
    at_ref, a_ref, a_keep_ref, b_ref, b_keep_ref, a2_ref, b2_ref, keep_ref, send_ref
):
    half = a_ref.shape[1]
    a, b = (
        sum(ref[...].astype(FULL) for ref in refs)
        for refs in ((a_keep_ref, a_ref, a2_ref), (b_keep_ref, b_ref, b2_ref))
    )

    @pl.when(pl.program_id(0) == 0)
    def _():
        send_ref[:, :half] = a.astype(LOW)
        send_ref[:, half:] = b.astype(LOW)

    @pl.when(pl.program_id(0) == 1)
    def _():
        keep_ref[:, :half] = a
        keep_ref[:, half:] = b


def down_last(at, parts, a2, b2, token):
    _, size, half = a2.shape
    core = lambda i, at: at[2] ^ (1 - i)
    three = pl.BlockSpec((None, size, half), lambda i, at: (core(i, at), 0, 0))
    four = pl.BlockSpec((None, None, size, half), lambda i, at: (0, core(i, at), 0, 0))
    shape = (size, 2 * half)
    (keep, send), token = call(
        down_last_kernel,
        "down_last",
        [(parts[0], three), (parts[1], three), (parts[2], four), (parts[3], four)]
        + [(a2, three), (b2, three)],
        [whole_out(shape, FULL), whole_out(shape, LOW)],
        grid=(2,),
        token=token,
        prefetch=(at,),
        us=3,
    )
    return keep, send, token


def choose_kernel(at_ref, keep_ref, got_ref, out_ref):
    mine = at_ref[0] == at_ref[2]
    out_ref[0] = jnp.where(mine, keep_ref[...], got_ref[...].astype(FULL))


def choose(at, keep, got, token):
    size, width = keep.shape
    rows = pl.BlockSpec((size // 2, width), lambda i, at: (i, 0))
    (out,), token = call(
        choose_kernel,
        "choose",
        [(keep, rows), (got, rows)],
        [((1, size, width), FULL, pl.BlockSpec((1, size // 2, width), lambda i, at: (0, i, 0)))],
        grid=(2,),
        token=token,
        prefetch=(at,),
        us=2,
    )
    return out, token


def in_last_kernel(
    at_ref, a_ref, a_keep_ref, b_ref, b_keep_ref, a2_ref, b2_ref, keep_ref, send_ref
):
    a, b = (
        sum(ref[...].astype(FULL) for ref in refs)
        for refs in ((a_keep_ref, a_ref, a2_ref), (b_keep_ref, b_ref, b2_ref))
    )

    @pl.when(pl.program_id(0) == 0)
    def _():
        send_ref[0] = a.astype(LOW)
        send_ref[1] = b.astype(LOW)

    @pl.when(pl.program_id(0) == 1)
    def _():
        keep_ref[0] = a
        keep_ref[1] = b


def in_last(at, parts, token):
    firsts, a2, b2 = parts
    rows, half = a2.shape
    size = rows // 2
    core = lambda i, at: at[2] ^ (1 - i)
    first = pl.BlockSpec((None, size, half), lambda i, at: (0, core(i, at), 0))
    second = pl.BlockSpec((size, half), lambda i, at: (core(i, at), 0))
    shape = (2, size, half)
    (keep, send), token = call(
        in_last_kernel,
        "in_last",
        [(part, first) for part in firsts] + [(a2, second), (b2, second)],
        [whole_out(shape, FULL), whole_out(shape, LOW)],
        grid=(2,),
        token=token,
        prefetch=(at,),
        us=4,
        vmem=16,
    )
    return keep, send, token


def in_end_kernel(at_ref, keep_ref, got_ref, out_ref):
    half = keep_ref.shape[2]
    for part in range(2):
        for first, value in (
            (at_ref[2], keep_ref[part]),
            (1 - at_ref[2], got_ref[part].astype(FULL)),
        ):
            start = pl.multiple_of((part * 2 + first) * half, LANES)
            out_ref[0, :, pl.ds(start, half)] = value


def in_end(at, keep, got, token):
    _, rows, half = keep.shape
    size = rows // 4
    spec = pl.BlockSpec((2, size, half), lambda i, at: (0, i, 0))
    (out,), token = call(
        in_end_kernel,
        "in_end",
        [(keep, spec), (got, spec)],
        [((1, rows, 4 * half), FULL, pl.BlockSpec((1, size, 4 * half), lambda i, at: (0, i, 0)))],
        grid=(4,),
        token=token,
        prefetch=(at,),
        us=2.5,
    )
    return out, token


EXTRA = 16
TABLE_LANE = 32


def turn_kernel(at_ref, own_ref, other_ref, out_ref, turned):
    count = own_ref.shape[0]
    turned[:, :count] = own_ref[...].T
    turned[:, count:] = other_ref[...].T
    size = out_ref.shape[0] // 16
    for to in range(16):
        device = device_at(to % 4, to // 4, at_ref)
        out_ref[pl.ds(to * size, size), :] = turned[pl.ds(device * size, size), :]


def device_at(block, z, at_ref):
    return (
        (at_ref[0] ^ (block // 2)) * 16 + z * 4 + (at_ref[1] ^ (block % 2)) * 2 + at_ref[2]
    )


def line_at(step, at):
    return at[3] ^ (step // 2) ^ (2 * (step % 2))


def turn(at, own, other, token):
    count, width = own.shape
    (out,), token = call(
        turn_kernel,
        "turn",
        [whole(own), whole(other)],
        [whole_out((width // 2, 2 * count), LOW)],
        token=token,
        prefetch=(at,),
        scratch=[pltpu.VMEM((width, 2 * count), LOW)],
        us=2,
        near_in=(0, 1),
        near_out=(0,),
    )
    return out, token


def shared_kernel(
    at_ref, left_ref, own_ref, other_ref,
    a_send_ref, a_keep_ref, b_send_ref, b_keep_ref, line_send_ref, line_keep_ref,
):
    step = pl.program_id(0)
    rows, count = left_ref.shape[0], left_ref.shape[1] // 2
    width = own_ref.shape[1]
    tokens = count // 3
    left = left_ref[...]

    def product(columns, start, length):
        return dot_rows(left[:, columns : columns + length], own_ref[start : start + length, :]) + (
            dot_rows(
                left[:, count + columns : count + columns + length],
                other_ref[start : start + length, :],
            )
        )

    total = [
        product(2 * tokens, 5 * tokens, tokens),
        product(tokens, 0, tokens),
        product(0, tokens, 2 * tokens),
        product(0, 3 * tokens, 2 * tokens),
    ]
    size = rows // 4
    first_lane = width - GROUP * HDIM
    small = own_ref[6 * tokens :, first_lane : first_lane + LANES].astype(FULL)
    small = small + other_ref[6 * tokens :, first_lane : first_lane + LANES].astype(FULL)
    place = lax.broadcasted_iota(jnp.int32, small.shape, 0)
    extras = []
    for block in range(4):
        device = device_at(block, line_at(step, at_ref), at_ref)
        row = jnp.sum(jnp.where(place == device, small, 0.0), 0, keepdims=True)
        extras.append(jnp.broadcast_to(row, (EXTRA, LANES)))
    for r in range(2):
        a_keep_ref[0, r] = total[0][(2 * r) * size : (2 * r + 1) * size]
        a_send_ref[0, r] = total[0][(2 * r + 1) * size : (2 * r + 2) * size].astype(LOW)
        b_keep_ref[0, r, :size, :] = total[1][r * size : (r + 1) * size]
        b_send_ref[0, r, :size, :] = total[1][(2 + r) * size : (3 + r) * size].astype(LOW)
        b_keep_ref[0, r, size:, :] = jnp.zeros((EXTRA, width), FULL)
        b_send_ref[0, r, size:, :] = jnp.zeros((EXTRA, width), LOW)
        b_keep_ref[0, r, size:, :LANES] = extras[r]
        b_send_ref[0, r, size:, :LANES] = extras[2 + r].astype(LOW)

    @pl.when(step < 2)
    def _():
        line_keep_ref[0, 0] = total[2]
        line_keep_ref[0, 1] = total[3]

    @pl.when(step >= 2)
    def _():
        line_send_ref[0, 0] = total[2].astype(LOW)
        line_send_ref[0, 1] = total[3].astype(LOW)


def shared_terms(at, left, own, other, experts, token):
    rows, count = left.shape
    width = own.shape[1]
    size = rows // experts
    a_shape, b_shape = ((experts, 2, size // 4 + extra, width) for extra in (0, EXTRA))
    cut = lambda shape: pl.BlockSpec((1, *shape[1:]), lambda i, at: (line_at(i, at), 0, 0, 0))
    line_shape = (2, 2, size, width)
    line = lambda index: pl.BlockSpec((1, *line_shape[1:]), lambda i, at: (index(i), 0, 0, 0))
    outs, token = call(
        shared_kernel,
        "shared_terms",
        [
            (left, pl.BlockSpec((size, count), lambda i, at: (line_at(i, at), 0))),
            whole(own),
            whole(other),
        ],
        [
            (a_shape, LOW, cut(a_shape)),
            (a_shape, FULL, cut(a_shape)),
            (b_shape, LOW, cut(b_shape)),
            (b_shape, FULL, cut(b_shape)),
            (line_shape, LOW, line(lambda i: i // 3)),
            (line_shape, FULL, line(lambda i: (i + 1) // 2 - i // 3)),
        ],
        grid=(experts,),
        token=token,
        prefetch=(at,),
        vmem=24,
        near_in=(0, 1, 2),
        near_out=(0, 2, 4),
        us=4,
    )
    return outs[:4], outs[4:], token


def line_second_kernel(got_ref, keep_ref, out_ref):
    out_ref[...] = (keep_ref[...] + got_ref[...].astype(FULL)).astype(LOW)


def line_second(got, keep, token):
    spec = pl.BlockSpec((None, *got.shape[1:]), lambda *_: (1, 0, 0, 0))
    (out,), token = call(
        line_second_kernel,
        "line_second",
        [(got, spec), (keep, spec)],
        [whole_out(got.shape[1:], LOW)],
        token=token,
        us=1,
    )
    return out, token


def line_last_kernel(
    got_ref, keep_ref, second_ref, a_send_ref, a_keep_ref, b_send_ref, b_keep_ref
):
    size = a_send_ref.shape[1]
    total = keep_ref[...] + got_ref[...].astype(FULL) + second_ref[...].astype(FULL)
    for r in range(2):
        a_keep_ref[r] = total[0, (2 * r) * size : (2 * r + 1) * size]
        a_send_ref[r] = total[0, (2 * r + 1) * size : (2 * r + 2) * size].astype(LOW)
        b_keep_ref[r] = total[1, r * size : (r + 1) * size]
        b_send_ref[r] = total[1, (2 + r) * size : (3 + r) * size].astype(LOW)


def line_last(got, keep, second, token):
    _, rows, width = second.shape
    shape = (2, rows // 4, width)
    spec = pl.BlockSpec((None, *got.shape[1:]), lambda *_: (0, 0, 0, 0))
    return call(
        line_last_kernel,
        "line_last",
        [(got, spec), (keep, spec), whole(second)],
        [whole_out(shape, dtype) for dtype in (LOW, FULL, LOW, FULL)],
        token=token,
        us=1,
    )


def back_kernel(
    spread_ref, rows_ref, after_ref, gain_ref, grad_ref, weights_ref,
    total_ref, branch_ref, attended_ref, gain_grad_ref,
):
    rows = after_ref[...]
    inverse = lax.rsqrt(jnp.mean(rows * rows, axis=1, keepdims=True) + EPSILON)
    scaled = rows * inverse
    grad = transpose_dot(spread_ref[...], rows_ref[...])
    gain_grad_ref[...] = jnp.sum(scaled * grad, axis=0, keepdims=True)
    grad = grad * gain_ref[...]
    along = jnp.mean(scaled * grad, axis=1, keepdims=True)
    total = grad_ref[...].astype(FULL) + inverse * (grad - scaled * along)
    total_ref[...] = total
    branch = total.astype(LOW)
    branch_ref[...] = branch
    attended_ref[...] = dot_back(branch, weights_ref[...]).astype(LOW)


def back_to_attention(spread, rows, after, gain, grad, weights, token):
    shape = after.shape
    inputs = (spread, rows, after, gain, grad, weights)
    return call(
        back_kernel,
        "back",
        [whole(array) for array in inputs],
        [
            whole_out(shape, FULL),
            whole_out(shape, LOW),
            whole_out(shape, LOW),
            whole_out((1, shape[1]), FULL),
        ],
        token=token,
        vmem=16,
        us=3,
        near_in=(0, 1, 2, 5),
        near_out=(1, 2),
    )


def mix_kernel(pick_ref, rows_ref, gates_ref, after_ref, out_ref, peak_ref):
    top, tokens = gates_ref.shape
    blocks = rows_ref.shape[0]
    size = pick_ref.shape[0] // blocks
    total = after_ref[...]
    gates = [to_column(gates_ref[r : r + 1, :]) for r in range(top)]
    for block in range(blocks):
        rows = rows_ref[block, :size, :]
        for r in range(top):
            pick = pick_ref[pl.ds(block * size, size), pl.ds(r * tokens, tokens)]
            total = total + gates[r] * transpose_dot(pick, rows)
    out_ref[0] = total.astype(LOW)
    if rows_ref.shape[1] > size:
        peaks = [
            rows_ref[block, size:, :LANES].astype(FULL)
            + rows_ref[block, size:, LANES : 2 * LANES].astype(FULL)
            for block in range(blocks)
        ]
        peak_ref[...] = functools.reduce(jnp.maximum, peaks)


def mix(pick, rows, gates, after, token):
    (out, peak), token = call(
        mix_kernel,
        "mix",
        [whole(pick), whole(rows), whole(gates), whole(after)],
        [whole_out((1, *after.shape), LOW), whole_out((16, LANES), FULL)],
        token=token,
        near_in=(1,),
        us=2.5,
    )
    return out, peak, token


def local(
    block_in,
    seg_ids,
    routes,
    gates,
    buckets,
    norm_attn,
    norm_ffn,
    w_query,
    w_key,
    w_value,
    w_out_attn,
    rel_bias,
    clip_level,
    w_in,
    w_down,
    cotangent,
):
    tokens, width = block_in.shape[1:]
    heads = width // HDIM
    n_ctx, experts, n_dp = (lax.axis_size(axis) for axis in ("ctx", "exp", "dp"))
    fast = (n_ctx, experts, n_dp) == (2, 4, 4)
    devices = n_ctx * experts * n_dp
    length = n_ctx * tokens
    hidden = w_down.shape[1]
    y, z, x, core = place()
    place_all = (y * experts + z) * n_dp + lax.axis_index("dp")
    top_count = routes.shape[-1]
    capacity = tokens * top_count * 3 // (2 * experts)
    at = jnp.stack([y, x, core, z])

    backs = list(range(n_ctx - 1, 0, -1))
    earlier = [
        lax.ppermute(block_in[0], "ctx", [(i, (i + back) % n_ctx) for i in range(n_ctx)])
        for back in backs
    ]

    (spread, pick, grad_out, mask), _ = front(
        at, routes[0].T, gates[0].T, cotangent[0], seg_ids, experts, capacity
    )
    expert_grad = over_experts(grad_out).reshape(-1, width)
    (bucket_hot, bias), _ = bias_tiles(
        buckets.reshape(1, length), rel_bias.reshape(NB, heads), tokens
    )

    own_rows = block_in[0].astype(FULL)
    normed_own = rms_norm(own_rows, norm_attn).astype(LOW)
    normed_all = jnp.concatenate(
        [rms_norm(rows.astype(FULL), norm_attn).astype(LOW) for rows in earlier] + [normed_own],
        axis=0,
    )
    queries = dot_rows(normed_own, w_query).astype(LOW)
    keys = dot_rows(normed_all, w_key).astype(LOW)
    values = dot_rows(normed_all, w_value).astype(LOW)
    attended, probs, peak_lanes = attention(queries, keys, values, bias, mask)
    after = own_rows + dot_rows(attended, w_out_attn)

    sent = rms_norm(after, norm_ffn).astype(LOW)
    sent_rows = dot_rows(spread, sent).astype(LOW).reshape(experts, capacity, width)
    expert_rows = over_experts(sent_rows).reshape(-1, width)
    own_gain, own_table = width // devices, NB * heads // devices
    token = None
    if fast:
        beside = jnp.concatenate([normed_all, attended], axis=0)
        left, token = turn(at, beside, swapped(beside, "dp", 1), token)
        peak, token = larger(peak_lanes, swapped(peak_lanes, "dp", 1), token)
        peak, token = larger(peak, swapped(peak, "dp", 2), token)
        peak, token = larger(peak, swapped(peak, "ctx", 1), token)
        both_rows = expert_rows, swapped(expert_rows, "dp", 1)
        both_grads = expert_grad, swapped(expert_grad, "dp", 1)
        outs, token = expert_halves(at, both_rows, both_grads, w_in, w_down, token)
        out_keep, out_send, back_keep, back_send, dgate, dup, down_a, down_b, rows_turned = outs
        back_got = swapped(back_send, "dp", 1)
        down_a = down_a.reshape(2, 2, hidden // 8, width // 2)
        down_b = down_b.reshape(2, 2, hidden // 8, width // 2)
        down_by_x = jnp.stack([pick_block(down_b, x), pick_block(down_b, 1 - x)])
        down = (
            swapped(pick_block(down_a, 1 - x), "dp", 2),
            pick_block(down_a, x),
            to_down_plane(down_by_x),
            down_by_x,
        )
        back_rows, token = join(back_keep, back_got, (experts, capacity, width), token)
    else:
        (out_rows, back_rows, dgate, dup, hid_turned, rows_turned), token = expert(
            expert_rows, expert_grad, w_in, w_down, token
        )
        back_rows = back_rows.reshape(experts, capacity, width)
        expert_first, expert_second = (
            lax.psum_scatter(grads, ("ctx", "dp"), scatter_dimension=0, tiled=True)[None]
            for grads in (
                dot_rows(rows_turned, jnp.concatenate([dgate, dup], axis=1)),
                dot_rows(hid_turned, expert_grad),
            )
        )
    back_home = over_experts(back_rows).reshape(-1, width)
    if fast:
        first, token = in_terms(at, rows_turned, dgate, dup, hidden, token)
        first = plane_first(first)

    (grad_after, grad_branch, grad_attended, grad_gain_ffn), token = back_to_attention(
        spread, back_home, after, norm_ffn.reshape(1, width), cotangent[0], w_out_attn, token
    )
    if fast:
        packed, token = attention_back(
            queries, keys, values, probs, grad_attended, token,
            (grad_branch, bucket_hot, grad_gain_ffn, devices),
        )
        packed_got = swapped(packed, "dp", 1)
        (a_send, b_send), token = second_terms(down, token, (None, None, 0, 0), 20)
        down_more = to_down_plane(a_send), in_down_plane(b_send)
        out_got = swapped(out_send, "dp", 1)
        plane_2, line, token = shared_terms(at, left, packed, packed_got, experts, token)
        line_send, line_keep = line
        line_got = swapped(line_send, "exp", 1)
        plane_2 = plane_first(plane_2)
        out_rows, token = join_peak(out_keep, out_got, peak, experts, token)
        out_home = over_experts(out_rows)
        first, token = plane_second(first, token, us=3)
        keep, send, token = down_last(at, down, *down_more, token)
        down_got = swapped(send, "dp", 1)
        line_send, token = line_second(line_got, line_keep, token)
        line_more = swapped(line_send, "exp", 2)
        expert_second, token = choose(at, keep, down_got, token)
        mixed, peak, token = mix(pick, out_home, gates[0].T, after, token)
        peak = peak[:, 0]
        packed, = hold(token, packed)
        dq = packed[:tokens]
        dk = packed[tokens : tokens + length]
        dv = packed[tokens + length : tokens + 2 * length]
    else:
        dq, dk, dv, lines, token = attention_back(
            queries, keys, values, probs, grad_attended, token
        )
        lines = lines[:, :GROUP, :].reshape(heads, length + tokens)
        grad_table = lax.dot_general(
            bucket_hot, lines, (((1,), (1,)), ((), ())), precision=FULL_PRECISION
        ).reshape(-1)
        out_home = over_experts(out_rows.reshape(experts, capacity, width))
        mixed, _, _ = mix(pick, out_home, gates[0].T, after, token)
        peak = jnp.max(peak_lanes[:, :GROUP, :], axis=-1).reshape(heads)
        peak = lax.pmax(peak, ("ctx", "exp", "dp"))

    grad_normed = dot_back(dk, w_key) + dot_back(dv, w_value)
    grad_normed_own = grad_normed[length - tokens :] + dot_back(dq, w_query)
    for block, back in enumerate(backs):
        term = grad_normed[block * tokens : (block + 1) * tokens].astype(LOW)
        returned = lax.ppermute(term, "ctx", [((i + back) % n_ctx, i) for i in range(n_ctx)])
        grad_normed_own = grad_normed_own + returned.astype(FULL)
    _, norm_pull = jax.vjp(lambda rows: rms_norm(rows, norm_attn), own_rows)
    grad_input = grad_after + norm_pull(grad_normed_own)[0]

    factor = clip_level / jnp.maximum(peak, clip_level)
    column_scale = jnp.repeat(jnp.sqrt(factor), HDIM)
    clipped_query = w_query.astype(FULL) * column_scale[None, :]
    clipped_key = w_key.astype(FULL) * column_scale[None, :]

    if fast:
        plane_2, token = plane_second(plane_2, token, axis=1)
        line, token = line_last(line_got, line_keep, line_more, token)
        line = plane_first(line)
        keep, send, token = in_last(at, first, token)
        in_got = swapped(send, "dp", 1)
        plane_o, plane_q = plane_last(plane_2, axis=1)
        total = jnp.concatenate([plane_o, plane_q], axis=1).astype(LOW)
        total = over_experts(total).astype(FULL).sum(axis=0)
        shared_o, shared_q = total[:own_gain], total[own_gain : 2 * own_gain]
        small = total[2 * own_gain]
        small_ffn, small_table = small[:own_gain], small[TABLE_LANE : TABLE_LANE + own_table]
        line, token = plane_second(line, token)
        expert_first, token = in_end(at, keep, in_got, token)
        shared_k, shared_v = plane_last(line)
    else:
        shared_q, shared_k, shared_v, shared_o = (
            lax.psum_scatter(grads, ("ctx", "exp", "dp"), scatter_dimension=0, tiled=True)
            for grads in (
                transpose_dot(normed_own, dq),
                transpose_dot(normed_all, dk),
                transpose_dot(normed_all, dv),
                transpose_dot(attended, grad_branch),
            )
        )
        small_ffn, small_table = (
            lax.dynamic_slice_in_dim(lax.psum(array, ("ctx", "exp", "dp")), place_all * own, own)
            for array, own in ((grad_gain_ffn[0], own_gain), (grad_table, own_table))
        )
    pairs = ((shared_q, w_query), (shared_k, w_key), (shared_v, w_value))
    row_sums = sum(
        jnp.sum(
            grads * lax.dynamic_slice_in_dim(weights, place_all * own_gain, own_gain).astype(FULL),
            axis=1,
        )
        for grads, weights in pairs
    )
    small_attn = row_sums / lax.dynamic_slice_in_dim(norm_attn, place_all * own_gain, own_gain)

    return (
        mixed,
        grad_input[None],
        small_attn,
        small_ffn,
        shared_q,
        shared_k,
        shared_v,
        shared_o,
        small_table,
        expert_first,
        expert_second,
        clipped_query,
        clipped_key,
        factor,
    )


def solution(mesh):
    tokens = P(("exp", "dp"), "ctx", None)
    everywhere = P(("ctx", "exp", "dp"))
    by_rows = P(("ctx", "exp", "dp"), None)
    by_expert = P("exp", None, None)
    expert_rows = P("exp", ("ctx", "dp"), None)
    in_specs = (tokens, P(("exp", "dp"), None), tokens, tokens) + (P(),) * 9
    in_specs = in_specs + (by_expert, by_expert, tokens)
    out_specs = (tokens, tokens, everywhere, everywhere) + (by_rows,) * 4
    out_specs = out_specs + (everywhere, expert_rows, expert_rows, P(), P(), P())
    return jax.shard_map(local, mesh=mesh, in_specs=in_specs, out_specs=out_specs, check_vma=False)
```

time: 1500 us -> 273 us (0.18); the launches traced: 1480 us -> 271 us
  waiting for transfers between devices: 669 us -> 60.1 us
  local copies, waits for them, and re-layouts: 505 us -> 17.4 us
  matrix products: 138 us -> 11 us
  Pallas kernels: 0 us -> 108 us
  blocking collectives: 100 us -> 0 us
  starting transfers between devices: 18.2 us -> 54.6 us
  other arithmetic: 37 us -> 19.3 us
    reduce_scatter x8 -> x0, waiting for transfers between devices: 643 us -> none  [the longest x1 150 us: local(): lax.psum_scatter(grad_first, ('ctx', 'dp'), scatter_dimension=0, tiled=True)]
    gather x4 -> x0, local copies, waits for them, and re-layouts: 354 us -> none  [the longest x2 346 us: local(): bias_fwd = bias_block(buckets[distance], bias_table)]
    dot_general x68 -> x8, matrix products: 138 us -> 11 us  [the longest x3 7.26 us: dot_back(): lax.dot_general(left, right, (((1,), (1,)), ((), ())), preferred_element_...]
    pallas_call x0 -> x26, Pallas kernels: none -> 108 us  [the longest x25 108 us: call(): pl.pallas_call(kernel, grid_spec=pltpu.PrefetchScalarGridSpec(num_scalar_...]
    scatter x2 -> x0, local copies, waits for them, and re-layouts: 77 us -> none  [the longest x1 38.8 us: local(): grad_outgoing = jnp.zeros((experts, capacity, model_width), jnp.bfloat16)...]
    unnamed x1 -> x0, blocking collectives: 41.7 us -> none
    pmax x1 -> x0, blocking collectives: 40.1 us -> none  [local(): peak_all = lax.pmax(jnp.concatenate(peak_parts), ('ctx', 'exp', 'dp'))]
    ppermute x0 -> x31, starting transfers between devices: none -> 33.7 us  [the longest x26 23.1 us: swapped(): return lax.ppermute(array, axis, [(i, i ^ bit) for i in range(size)])]
  transfers between devices with their start and end apart: 12 -> 36, of which waited for: 9 -> 12; matrix products, arithmetic and copies ran while one was open for 13% -> 13% of each run, Pallas kernels for 0% -> 30%
where the time goes in v1:
time: 273 us; the launch traced here: 271 us
  Pallas kernels  108 us (40%)
  waiting for transfers between devices  60.1 us (22%)
  starting transfers between devices  54.6 us (20%)
  other arithmetic  19.3 us (7%)
  local copies, waits for them, and re-layouts  17.4 us (6%)
  matrix products  11 us (4%)
    pallas_call x25, Pallas kernels, call(): pl.pallas_call(kernel, grid_spec=pltpu.PrefetchScalarGridSpec(num_scalar_...  108 us
    ppermute x26, waiting for transfers between devices, swapped(): return lax.ppermute(array, axis, [(i, i ^ bit) for i in range(size)])  27.8 us
    all_to_all x5, waiting for transfers between devices, over_experts(): lax.all_to_all(blocks, 'exp', split_axis=0, concat_axis=0, tiled=True)  27.6 us
    ppermute x26, starting transfers between devices, swapped(): return lax.ppermute(array, axis, [(i, i ^ bit) for i in range(size)])  23.1 us
    all_to_all x5, starting transfers between devices, over_experts(): lax.all_to_all(blocks, 'exp', split_axis=0, concat_axis=0, tiled=True)  20.9 us
    unnamed x120, local copies, waits for them, and re-layouts  11 us
    dot_general x3, matrix products, dot_back(): lax.dot_general(left, right, (((1,), (1,)), ((), ())), preferred_element_...  7.26 us
    mul x1, other arithmetic, local(): clipped_key = w_key.astype(FULL) * column_scale[None, :]  6.22 us
  transfers between devices with their start and end apart: 36, of which 12 were waited for; matrix products, arithmetic and copies ran while one was open for 13% of the time, Pallas kernels for 30%

profile of v1, /device:TPU:0, one launch (start us, length us, event | category | flops | bytes accessed | tf_op | source)
XLA Modules:
  0.0 271.5 jit_solution(8461606217920252345)
XLA Ops:
  0.6 3.0 %collective-permute-start = (bf16[128,1024]{1,0:T(8,128)(2,1)}, bf16[128,1024]{1,0:T(8,128)(2,1)S(1)}, u32[]{:S(2)}, u32[]{:S(2)}) collective-permute-start(bf16[128,1024]{1,0:T(8,128)(2,1)} %bitcast.64), channel_id=1, source_target_pairs={{0,16},{16,0},{1,17},{17,1},{2,18},{18,2},{3,19},{19,3},{4,20},{20... | collective-permute-start | bytes 786440 | tf_op jit(solution)/shard_map/ppermute | solution.py:1151
  3.8 2.9 %front.1 = (bf16[384,128]{1,0:T(8,128)(2,1)S(1)}, bf16[384,256]{1,0:T(8,128)(2,1)}, bf16[4,96,1024]{2,1,0:T(8,128)(2,1)}, f32[128,256]{1,0:T(8,128)S(1)}, f32[8,128]{1,0:T(8,128)}) custom-call(s32[4]{0:T(128)S(1)} %pad_add_fusion.refs_0_, s32[2,128]{1,0:T(2,128)} %bitcast.69, f32[2,128]{1,0:T(2,128)} %bitcast.71, bf16[128,1024]{1,0:T(8,128)(2,1)} %bitcast.67, ...), custom_call_target="tpu_custom_call" | custom-call | flops 1724999936 | bytes 1 | tf_op jit(solution)/shard_map/front/pallas_call | solution.py:70
  6.6 4.9 %all-to-all-start.1 = ((bf16[4,96,1024]{2,1,0:T(8,128)(2,1)}), bf16[4,96,1024]{2,1,0:T(8,128)(2,1)}, u32[]{:S(2)}, u32[]{:S(2)}) async-start(bf16[4,96,1024]{2,1,0:T(8,128)(2,1)} %get-tuple-element.100), calls=%async_computation.1 | async-start | bytes 1572864 | tf_op jit(solution)/shard_map/all_to_all | solution.py:45
  12.3 3.5 %bias_tiles.1 = (f32[32,384]{1,0:T(8,128)}, f32[16,128,256]{2,1,0:T(8,128)S(1)}, f32[8,128]{1,0:T(8,128)}) custom-call(s32[1,256]{1,0:T(1,128)} %bitcast.70, f32[32,16]{1,0:T(8,128)} %reshape.99.refs_1_), custom_call_target="tpu_custom_call" | custom-call | flops 2875000064 | bytes 1 | tf_op jit(solution)/shard_map/bias_tiles/pallas_call | solution.py:70
  19.3 4.5 %attention.1 = (bf16[128,1024]{1,0:T(8,128)(2,1)S(1)}, f32[16,128,256]{2,1,0:T(8,128)S(1)}, f32[4,8,128]{2,1,0:T(8,128)}, f32[8,128]{1,0:T(8,128)}) custom-call(bf16[128,1024]{1,0:T(8,128)(2,1)S(1)} %convolution_convert_fusion.3.refs_0_, bf16[256,1024]{1,0:T(8,128)(2,1)S(1)} %convolution_convert_fusion.2.refs_1_, ...), custom_call_target="tpu_custom_call" | custom-call | flops 5175000064 | bytes 1 | tf_op jit(solution)/shard_map/attention/pallas_call | solution.py:70
  27.1 4.3 %all-to-all-done.1 = bf16[4,96,1024]{2,1,0:T(8,128)(2,1)} async-done(((bf16[4,96,1024]{2,1,0:T(8,128)(2,1)}), bf16[4,96,1024]{2,1,0:T(8,128)(2,1)}, u32[]{:S(2)}, u32[]{:S(2)}) %all-to-all-start.1) | async-done | bytes 786464 | tf_op jit(solution)/shard_map/all_to_all | solution.py:45
  31.4 4.4 %all-to-all-start = ((bf16[4,96,1024]{2,1,0:T(8,128)(2,1)}), bf16[4,96,1024]{2,1,0:T(8,128)(2,1)}, u32[]{:S(2)}, u32[]{:S(2)}) async-start(bf16[4,96,1024]{2,1,0:T(8,128)(2,1)} %bitcast.65), calls=%async_computation | async-start | bytes 1572864 | tf_op jit(solution)/shard_map/all_to_all | solution.py:45
  37.3 18.0 %all-to-all-done = bf16[4,96,1024]{2,1,0:T(8,128)(2,1)} async-done(((bf16[4,96,1024]{2,1,0:T(8,128)(2,1)}), bf16[4,96,1024]{2,1,0:T(8,128)(2,1)}, u32[]{:S(2)}, u32[]{:S(2)}) %all-to-all-start) | async-done | bytes 786464 | tf_op jit(solution)/shard_map/all_to_all | solution.py:45
  55.8 2.9 %turn.1 = (bf16[512,768]{1,0:T(8,128)(2,1)S(1)}, f32[8,128]{1,0:T(8,128)}) custom-call(s32[4]{0:T(128)S(1)} %pad_add_fusion.refs_0_, bf16[384,1024]{1,0:T(8,128)(2,1)} %pad_maximum_fusion.1.refs_1_, bf16[384,1024]{1,0:T(8,128)(2,1)} %collective-permute-done.4.refs_2_), custom_call_target="tpu_custom_call" | custom-call | flops 2300000000 | bytes 1 | tf_op jit(solution)/shard_map/turn/pallas_call | solution.py:70
  61.7 2.2 collective-permute-done.5.refs_1_
  65.1 3.2 %collective-permute-done.6.refs_1_ = f32[4,8,128]{2,1,0:T(8,128)S(1)} collective-permute-done((f32[4,8,128]{2,1,0:T(8,128)S(1)}, f32[4,8,128]{2,1,0:T(8,128)S(1)}, u32[]{:S(2)}, u32[]{:S(2)}) %collective-permute-start.6) | collective-permute-done | bytes 16416 | tf_op jit(solution)/shard_map/ppermute | solution.py:41
  68.9 26.3 %expert_halves.1 = (f32[384,1024]{1,0:T(8,128)}, bf16[384,1024]{1,0:T(8,128)(2,1)}, f32[384,1024]{1,0:T(8,128)S(1)}, bf16[384,1024]{1,0:T(8,128)(2,1)S(1)}, bf16...) custom-call(s32[4]{0:T(128)} %copy-done.9, ...), custom_call_target="tpu_custom_call" | custom-call | flops 27599998976 | bytes 1 | tf_op jit(solution)/shard_map/expert_halves/pallas_call | solution.py:70
  99.2 2.3 collective-permute-done.8.refs_1_
  103.1 3.5 %all-to-all-start.2 = ((bf16[4,96,1024]{2,1,0:T(8,128)(2,1)}), bf16[4,96,1024]{2,1,0:T(8,128)(2,1)S(1)}, u32[]{:S(2)}, u32[]{:S(2)}) async-start(bf16[4,96,1024]{2,1,0:T(8,128)(2,1)} %copy-done.6), calls=%async_computation.2 | async-start | bytes 1572864 | tf_op jit(solution)/shard_map/all_to_all | solution.py:45
  106.8 2.7 dynamic-slice_bitcast_fusion
  113.9 8.9 %in_terms.1 = (bf16[2,256,1408]{2,1,0:T(8,128)(2,1)}, bf16[2,256,1408]{2,1,0:T(8,128)(2,1)}, bf16[2,256,1408]{2,1,0:T(8,128)(2,1)}, bf16[2,256,1408]{2,1,0:T(8,128)(2,1)}, f32[8,128]{1,0:T(8,128)}) custom-call(s32[4]{0:T(128)S(1)} %copy-done.10, bf16[1024,768]{1,0:T(8,128)(2,1)S(1)} %copy-done.28, bf16[768,1536]{1,0:T(8,128)(2,1)S(1)} %copy-done.24, ...), custom_call_target="tpu_custom_call" | custom-call | flops 6899999744 | bytes 1 | tf_op jit(solution)/shard_map/in_terms/pallas_call | solution.py:70
  123.4 3.7 %collective-permute-start.15 = (bf16[2,256,1408]{2,1,0:T(8,128)(2,1)}, bf16[2,256,1408]{2,1,0:T(8,128)(2,1)}, u32[]{:S(2)}, u32[]{:S(2)}) collective-permute-start(bf16[2,256,1408]{2,1,0:T(8,128)(2,1)} %get-tuple-element.138), channel_id=1, source_target_pairs={{0,16},{16,0},{1,17},{17,1},{2,18},{18,2},{3,19},{19,3},{4,20},{20... | collective-permute-start | bytes 4325384 | tf_op jit(solution)/shard_map/ppermute | solution.py:41
  127.2 2.8 %back.1 = (f32[128,1024]{1,0:T(8,128)}, bf16[128,1024]{1,0:T(8,128)(2,1)S(1)}, bf16[128,1024]{1,0:T(8,128)(2,1)S(1)}, f32[1,1024]{1,0:T(1,128)}, f32[8,128]{1,0:T(8,128)}) custom-call(bf16[384,128]{1,0:T(8,128)(2,1)S(1)} %get-tuple-element.96.refs_0_, bf16[384,1024]{1,0:T(8,128)(2,1)S(1)} %bitcast.63, f32[128,1024]{1,0:T(8,128)S(1)} %get-tuple-element.194.refs_2_.refs_3_, ...), custom_call_target="tpu_custom_call" | custom-call | flops 3449999872 | bytes 1 | tf_op jit(solution)/shard_map/back/pallas_call | solution.py:70
  130.1 9.7 %attention_back.1 = (bf16[800,1024]{1,0:T(8,128)(2,1)S(1)}, f32[4,8,384]{2,1,0:T(8,128)}, f32[8,128]{1,0:T(8,128)}) custom-call(bf16[128,1024]{1,0:T(8,128)(2,1)S(1)} %copy-done.8, bf16[256,1024]{1,0:T(8,128)(2,1)S(1)} %copy-done.16, bf16[256,1024]{1,0:T(8,128)(2,1)S(1)} %copy-done.18, f32[16,128,256]{2,1,0:T(8,128)S(1)} %copy-done.22, ...), custom_call_target="tpu_custom_call" | custom-call | flops 8049999872 | bytes 1 | tf_op jit(solution)/shard_map/attention_back/pallas_call | solution.py:70
  139.9 3.6 %second_terms.4 = (bf16[2,352,512]{2,1,0:T(8,128)(2,1)}, bf16[2,352,512]{2,1,0:T(8,128)(2,1)}, f32[8,128]{1,0:T(8,128)}) custom-call(bf16[2,352,512]{2,1,0:T(8,128)(2,1)} %collective-permute-done.10.refs_0_.refs_1_, bf16[2,352,512]{2,1,0:T(8,128)(2,1)} %get-tuple-element.186.refs_1_.refs_2_, ...), custom_call_target="tpu_custom_call" | custom-call | flops 23000000512 | bytes 1 | tf_op jit(solution)/shard_map/second_terms/pallas_call | solution.py:70
  145.0 3.4 %collective-permute-start.13 = (bf16[2,352,512]{2,1,0:T(8,128)(2,1)}, bf16[2,352,512]{2,1,0:T(8,128)(2,1)}, u32[]{:S(2)}, u32[]{:S(2)}) collective-permute-start(bf16[2,352,512]{2,1,0:T(8,128)(2,1)} %get-tuple-element.135), channel_id=1, source_target_pairs={{0,2},{2,0},{17,19},{19,17},{4,6},{6,4},{21,23},{23,21},{8,10},{10... | collective-permute-start | bytes 2162696 | tf_op jit(solution)/shard_map/ppermute | solution.py:660
  148.4 5.4 %shared_terms.1 = (bf16[4,2,32,1024]{3,2,1,0:T(8,128)(2,1)S(1)}, f32[4,2,32,1024]{3,2,1,0:T(8,128)}, bf16[4,2,48,1024]{3,2,1,0:T(8,128)(2,1)S(1)}, f32[4,2,48,10...) custom-call(s32[4]{0:T(128)S(1)} %copy-done.10, ...), custom_call_target="tpu_custom_call" | custom-call | flops 4600000000 | bytes 1 | tf_op jit(solution)/shard_map/shared_terms/pallas_call | solution.py:70
  153.8 3.4 %join_peak.1 = (bf16[4,112,1024]{2,1,0:T(8,128)(2,1)}, f32[8,128]{1,0:T(8,128)}) custom-call(f32[384,1024]{1,0:T(8,128)} %get-tuple-element.108.refs_0_, bf16[384,1024]{1,0:T(8,128)(2,1)} %collective-permute-done.7.refs_1_, f32[4,8,128]{2,1,0:T(8,128)} %copy-done.29, f32[8,128]{1,0:T(8,128)} %get-tuple-element.132.refs_3_), custom_call_target="tpu_custom_call" | custom-call | flops 1724999936 | bytes 1 | tf_op jit(solution)/shard_map/join_peak/pallas_call | solution.py:70
  157.3 4.7 %all-to-all-start.3 = ((bf16[4,112,1024]{2,1,0:T(8,128)(2,1)}), bf16[4,112,1024]{2,1,0:T(8,128)(2,1)S(1)}, u32[]{:S(2)}, u32[]{:S(2)}) async-start(bf16[4,112,1024]{2,1,0:T(8,128)(2,1)} %get-tuple-element.133), calls=%async_computation.3 | async-start | bytes 1835008 | tf_op jit(solution)/shard_map/all_to_all | solution.py:45
  162.0 2.0 collective-permute-start.17
  164.6 3.0 %second_terms.5 = (bf16[256,1408]{1,0:T(8,128)(2,1)}, bf16[256,1408]{1,0:T(8,128)(2,1)}, f32[8,128]{1,0:T(8,128)}) custom-call(bf16[2,256,1408]{2,1,0:T(8,128)(2,1)} %collective-permute-done.14.refs_0_.refs_1_, bf16[2,256,1408]{2,1,0:T(8,128)(2,1)} %get-tuple-element.137.refs_1_.refs_2_, bf16[2,256,1408]{2,1,0:T(8,128)(2,1)} %collective-permute-done.15.refs_2_.refs_3_, ...), custom_call_target="tpu_custom_call" | custom-call | flops 3449999872 | bytes 1 | tf_op jit(solution)/shard_map/second_terms/pallas_call | solution.py:70
  167.6 4.6 %collective-permute-done.12.refs_5_ = bf16[2,352,512]{2,1,0:T(8,128)(2,1)S(1)} collective-permute-done((bf16[2,352,512]{2,1,0:T(8,128)(2,1)}, bf16[2,352,512]{2,1,0:T(8,128)(2,1)S(1)}, u32[]{:S(2)}, u32[]{:S(2)}) %collective-permute-start.12) | collective-permute-done | bytes 720928 | tf_op jit(solution)/shard_map/ppermute | solution.py:651
  173.1 4.6 %down_last.1 = (f32[352,1024]{1,0:T(8,128)}, bf16[352,1024]{1,0:T(8,128)(2,1)}, f32[8,128]{1,0:T(8,128)}) custom-call(s32[4]{0:T(128)S(1)} %copy-done.10, bf16[2,352,512]{2,1,0:T(8,128)(2,1)} %collective-permute-done.10.refs_0_.refs_1_, bf16[2,352,512]{2,1,0:T(8,128)(2,1)} %get-tuple-element.186.refs_1_.refs_2_, ...), custom_call_target="tpu_custom_call" | custom-call | flops 3449999872 | bytes 1 | tf_op jit(solution)/shard_map/down_last/pallas_call | solution.py:70
  178.3 2.0 collective-permute-start.26
  180.4 11.8 %collective-permute-done.19 = bf16[4,2,32,1024]{3,2,0,1:T(8,128)(2,1)S(1)} collective-permute-done((bf16[4,2,32,1024]{3,2,0,1:T(8,128)(2,1)S(1)}, bf16[4,2,32,1024]{3,2,0,1:T(8,128)(2,1)S(1)}, u32[]{:S(2)}, u32[]{:S(2)}) %collective-permute-start.19) | collective-permute-done | bytes 524320 | tf_op jit(solution)/shard_map/ppermute | solution.py:41
  193.5 6.8 %collective-permute-done.17.refs_0_ = bf16[2,2,128,1024]{3,2,1,0:T(8,128)(2,1)} collective-permute-done((bf16[2,2,128,1024]{3,2,1,0:T(8,128)(2,1)}, bf16[2,2,128,1024]{3,2,1,0:T(8,128)(2,1)}, u32[]{:S(2)}, u32[]{:S(2)}) %collective-permute-start.17) | collective-permute-done | bytes 1048608 | tf_op jit(solution)/shard_map/ppermute | solution.py:41
  200.3 2.3 line_second.1
  202.6 2.4 collective-permute-start.23
  205.9 3.0 %choose.1 = (f32[1,352,1024]{2,1,0:T(8,128)}, f32[8,128]{1,0:T(8,128)}) custom-call(s32[4]{0:T(128)S(1)} %copy-done.10, f32[352,1024]{1,0:T(8,128)} %get-tuple-element.142.refs_1_, bf16[352,1024]{1,0:T(8,128)(2,1)} %copy-done.57, f32[8,128]{1,0:T(8,128)} %get-tuple-element.147.refs_3_), custom_call_target="tpu_custom_call" | custom-call | flops 2300000000 | bytes 1 | tf_op jit(solution)/shard_map/choose/pallas_call | solution.py:70
  208.9 2.6 mix.1
  211.5 2.6 fusion.14
  214.2 1.8 convolution_add_fusion
  218.0 2.6 second_terms.6
  221.9 6.2 %convert_multiply_fusion = (f32[1024,1024]{1,0:T(8,128)}, f32[1024,1024]{1,0:T(8,128)}) fusion(bf16[1024,1024]{1,0:T(8,128)(2,1)} %param.24, f32[1024]{0:T(1024)S(1)} %mul.154, bf16[1024,1024]{1,0:T(8,128)(2,1)S(1)} %copy-done.31), kind=kLoop, calls=%fused_computation | loop fusion | flops 4194304 | bytes 12587008 | tf_op jit(solution)/shard_map/mul | solution.py:1273
  228.1 1.7 collective-permute-start.21
  229.9 2.4 line_last.1
  234.1 4.6 %in_last.1 = (f32[2,128,1408]{2,1,0:T(8,128)}, bf16[2,128,1408]{2,1,0:T(8,128)(2,1)}, f32[8,128]{1,0:T(8,128)}) custom-call(s32[4]{0:T(128)S(1)} %copy-done.10, bf16[2,256,1408]{2,1,0:T(8,128)(2,1)} %collective-permute-done.14.refs_0_.refs_1_, bf16[2,256,1408]{2,1,0:T(8,128)(2,1)} %get-tuple-element.137.refs_1_.refs_2_, ...), custom_call_target="tpu_custom_call" | custom-call | flops 4600000000 | bytes 1 | tf_op jit(solution)/shard_map/in_last/pallas_call | solution.py:70
  238.8 2.8 %fusion.9 = (f32[128]{0:T(128)S(1)}, f32[128,1024]{1,0:T(8,128)}) fusion(bf16[128,1024]{1,0:T(8,128)(2,1)} %collective-permute-done.18, f32[1024]{0:T(1024)S(1)} %copy-done.46, bf16[1,128,1024]{2,1,0:T(8,128)(2,1)S(1)} %copy-done.34, bf16[1024,1024]{1,0:T(8,128)(2,1)S(1)} %copy-done.31, bf16[800,1024]{1,0:T(8,128)(2,1)} %hold.1, ...), kind=kOutput, calls=%fused_computation.32 | convolution fusion | flops 269352832 | bytes 3936768 | tf_op jit(solution)/shard_map/dot_general | solution.py:32
  242.9 1.8 second_terms.7
  247.6 3.5 %all-to-all-start.4 = ((bf16[4,80,1024]{2,1,0:T(8,128)(2,1)}), bf16[4,80,1024]{2,1,0:T(8,128)(2,1)S(1)}, u32[]{:S(2)}, u32[]{:S(2)}) async-start(bf16[4,80,1024]{2,1,0:T(8,128)(2,1)} %pad_maximum_fusion.2), calls=%async_computation.4 | async-start | bytes 1310720 | tf_op jit(solution)/shard_map/all_to_all | solution.py:45
  251.1 2.2 fusion.5
  259.2 4.5 %in_end.1 = (f32[1,128,5632]{2,1,0:T(8,128)}, f32[8,128]{1,0:T(8,128)}) custom-call(s32[4]{0:T(128)S(1)} %copy-done.10, f32[2,128,1408]{2,1,0:T(8,128)} %get-tuple-element.170.refs_1_, bf16[2,128,1408]{2,1,0:T(8,128)(2,1)} %collective-permute-done.30.refs_2_, f32[8,128]{1,0:T(8,128)} %get-tuple-element.172.refs_3_), custom_call_target="tpu_custom_call" | custom-call | flops 2875000064 | bytes 1 | tf_op jit(solution)/shard_map/in_end/pallas_call | solution.py:70
  263.7 5.2 %all-to-all-done.4 = bf16[4,80,1024]{2,1,0:T(8,128)(2,1)S(1)} async-done(((bf16[4,80,1024]{2,1,0:T(8,128)(2,1)}), bf16[4,80,1024]{2,1,0:T(8,128)(2,1)S(1)}, u32[]{:S(2)}, u32[]{:S(2)}) %all-to-all-start.4) | async-done | bytes 655392 | tf_op jit(solution)/shard_map/all_to_all | solution.py:45
  (210 shorter events, 48.9 us)
Async XLA Ops:
  0.6 15.2 %collective-permute-start = (bf16[128,1024]{1,0:T(8,128)(2,1)}, bf16[128,1024]{1,0:T(8,128)(2,1)S(1)}, u32[]{:S(2)}, u32[]{:S(2)}) collective-permute-start(bf16[128,1024]{1,0:T(8,128)(2,1)} %bitcast.64), channel_id=1, source_target_pairs={{0,16},{16,0},{1,17},{17,1},{2,18},{18,2},{3,19},{19,3},{4,20},{20... | collective-permute-start | bytes 786440 | tf_op jit(solution)/shard_map/ppermute | solution.py:1151
  3.8 52.0 %copy-start.9 = (s32[4]{0:T(128)}, s32[4]{0:T(128)S(1)}, u32[]{:S(2)}) copy-start(s32[4]{0:T(128)S(1)} %pad_add_fusion.refs_0_) | copy-start | bytes 52
  3.8 7.7 %copy-start.33 = (bf16[1,128,1024]{2,1,0:T(8,128)(2,1)S(1)}, bf16[1,128,1024]{2,1,0:T(8,128)(2,1)}, u32[]{:S(2)}) copy-start(bf16[1,128,1024]{2,1,0:T(8,128)(2,1)} %param.16) | copy-start | bytes 786436
  3.8 7.9 %copy-start.53 = (f32[512]{0:T(512)S(1)}, f32[512]{0:T(512)}, u32[]{:S(2)}) copy-start(f32[512]{0:T(512)} %param.27) | copy-start | bytes 6148
  6.6 24.8 %all-to-all-start.1 = ((bf16[4,96,1024]{2,1,0:T(8,128)(2,1)}), bf16[4,96,1024]{2,1,0:T(8,128)(2,1)}, u32[]{:S(2)}, u32[]{:S(2)}) async-start(bf16[4,96,1024]{2,1,0:T(8,128)(2,1)} %get-tuple-element.100), calls=%async_computation.1 | async-start | bytes 1572864 | tf_op jit(solution)/shard_map/all_to_all | solution.py:45
  25.7 101.5 %copy-start.2 = (f32[128,1024]{1,0:T(8,128)}, f32[128,1024]{1,0:T(8,128)S(1)}, u32[]{:S(2)}) copy-start(f32[128,1024]{1,0:T(8,128)S(1)} %get-tuple-element.194.refs_2_.refs_3_) | copy-start | bytes 1572868
  25.7 10.1 %copy-start.41 = (bf16[128,1024]{1,0:T(8,128)(2,1)S(1)}, bf16[128,1024]{1,0:T(8,128)(2,1)}, u32[]{:S(2)}) copy-start(bf16[128,1024]{1,0:T(8,128)(2,1)} %copy-done.40) | copy-start | bytes 786436
  25.8 29.5 %copy-start.14 = (f32[4,8,128]{2,1,0:T(8,128)S(1)}, f32[4,8,128]{2,1,0:T(8,128)}, u32[]{:S(2)}) copy-start(f32[4,8,128]{2,1,0:T(8,128)} %get-tuple-element.101.refs_0_) | copy-start | bytes 49156
  31.4 23.9 %all-to-all-start = ((bf16[4,96,1024]{2,1,0:T(8,128)(2,1)}), bf16[4,96,1024]{2,1,0:T(8,128)(2,1)}, u32[]{:S(2)}, u32[]{:S(2)}) async-start(bf16[4,96,1024]{2,1,0:T(8,128)(2,1)} %bitcast.65), calls=%async_computation | async-start | bytes 1572864 | tf_op jit(solution)/shard_map/all_to_all | solution.py:45
  36.7 19.1 %collective-permute-start.4 = (bf16[384,1024]{1,0:T(8,128)(2,1)}, bf16[384,1024]{1,0:T(8,128)(2,1)}, u32[]{:S(2)}, u32[]{:S(2)}) collective-permute-start(bf16[384,1024]{1,0:T(8,128)(2,1)} %pad_maximum_fusion.1.refs_1_), channel_id=1, source_target_pairs={{0,1},{1,0},{2,3},{3,2},{4,5},{5,4},{6,7},{7,6},{8,9},{9,8},{10,11... | collective-permute-start | bytes 2359304 | tf_op jit(solution)/shard_map/ppermute | solution.py:41
  36.7 32.2 %collective-permute-start.2 = (bf16[384,1024]{1,0:T(8,128)(2,1)}, bf16[384,1024]{1,0:T(8,128)(2,1)S(1)}, u32[]{:S(2)}, u32[]{:S(2)}) collective-permute-start(bf16[384,1024]{1,0:T(8,128)(2,1)} %bitcast.13.refs_3_), channel_id=1, source_target_pairs={{0,1},{1,0},{2,3},{3,2},{4,5},{5,4},{6,7},{7,6},{8,9},{9,8},{10,11... | collective-permute-start | bytes 2359304 | tf_op jit(solution)/shard_map/ppermute | solution.py:41
  55.3 13.6 %collective-permute-start.1 = (bf16[384,1024]{1,0:T(8,128)(2,1)}, bf16[384,1024]{1,0:T(8,128)(2,1)S(1)}, u32[]{:S(2)}, u32[]{:S(2)}) collective-permute-start(bf16[384,1024]{1,0:T(8,128)(2,1)} %bitcast.12.refs_1_), channel_id=1, source_target_pairs={{0,1},{1,0},{2,3},{3,2},{4,5},{5,4},{6,7},{7,6},{8,9},{9,8},{10,11... | collective-permute-start | bytes 2359304 | tf_op jit(solution)/shard_map/ppermute | solution.py:41
  55.3 4.3 %collective-permute-start.3 = (f32[4,8,128]{2,1,0:T(8,128)S(1)}, f32[4,8,128]{2,1,0:T(8,128)S(1)}, u32[]{:S(2)}, u32[]{:S(2)}) collective-permute-start(f32[4,8,128]{2,1,0:T(8,128)S(1)} %copy-done.14), channel_id=1, source_target_pairs={{0,1},{1,0},{2,3},{3,2},{4,5},{5,4},{6,7},{7,6},{8,9},{9,8},{10,11... | collective-permute-start | bytes 49160 | tf_op jit(solution)/shard_map/ppermute | solution.py:41
  60.2 3.7 %collective-permute-start.5 = (f32[4,8,128]{2,1,0:T(8,128)S(1)}, f32[4,8,128]{2,1,0:T(8,128)S(1)}, u32[]{:S(2)}, u32[]{:S(2)}) collective-permute-start(f32[4,8,128]{2,1,0:T(8,128)S(1)} %get-tuple-element.103.refs_0_), channel_id=1, source_target_pairs={{0,2},{1,3},{2,0},{3,1},{4,6},{5,7},{6,4},{7,5},{8,10},{9,11},{10,... | collective-permute-start | bytes 49160 | tf_op jit(solution)/shard_map/ppermute | solution.py:41
  64.6 3.7 %collective-permute-start.6 = (f32[4,8,128]{2,1,0:T(8,128)S(1)}, f32[4,8,128]{2,1,0:T(8,128)S(1)}, u32[]{:S(2)}, u32[]{:S(2)}) collective-permute-start(f32[4,8,128]{2,1,0:T(8,128)S(1)} %get-tuple-element.105.refs_0_), channel_id=1, source_target_pairs={{0,16},{16,0},{1,17},{17,1},{2,18},{18,2},{3,19},{19,3},{4,20},{20... | collective-permute-start | bytes 49160 | tf_op jit(solution)/shard_map/ppermute | solution.py:41
  68.9 26.3 %copy-start.29 = (f32[4,8,128]{2,1,0:T(8,128)}, f32[4,8,128]{2,1,0:T(8,128)S(1)}, u32[]{:S(2)}) copy-start(f32[4,8,128]{2,1,0:T(8,128)S(1)} %get-tuple-element.110.refs_2_) | copy-start | bytes 49156
  99.2 2.3 collective-permute-start.8
  103.1 24.2 %all-to-all-start.2 = ((bf16[4,96,1024]{2,1,0:T(8,128)(2,1)}), bf16[4,96,1024]{2,1,0:T(8,128)(2,1)S(1)}, u32[]{:S(2)}, u32[]{:S(2)}) async-start(bf16[4,96,1024]{2,1,0:T(8,128)(2,1)} %copy-done.6), calls=%async_computation.2 | async-start | bytes 1572864 | tf_op jit(solution)/shard_map/all_to_all | solution.py:45
  106.6 47.2 %collective-permute-start.7 = (bf16[384,1024]{1,0:T(8,128)(2,1)}, bf16[384,1024]{1,0:T(8,128)(2,1)}, u32[]{:S(2)}, u32[]{:S(2)}) collective-permute-start(bf16[384,1024]{1,0:T(8,128)(2,1)} %get-tuple-element.109), channel_id=1, source_target_pairs={{0,1},{1,0},{2,3},{3,2},{4,5},{5,4},{6,7},{7,6},{8,9},{9,8},{10,11... | collective-permute-start | bytes 2359304 | tf_op jit(solution)/shard_map/ppermute | solution.py:41
  106.8 7.0 %copy-start.28 = (bf16[1024,768]{1,0:T(8,128)(2,1)S(1)}, bf16[1024,768]{1,0:T(8,128)(2,1)}, u32[]{:S(2)}) copy-start(bf16[1024,768]{1,0:T(8,128)(2,1)} %copy-done.27) | copy-start | bytes 4718596
  109.4 30.4 %collective-permute-start.10 = (bf16[2,352,512]{2,1,0:T(8,128)(2,1)}, bf16[2,352,512]{2,1,0:T(8,128)(2,1)}, u32[]{:S(2)}, u32[]{:S(2)}) collective-permute-start(bf16[2,352,512]{2,1,0:T(8,128)(2,1)} %get-tuple-element.187), channel_id=1, source_target_pairs={{0,2},{1,3},{2,0},{3,1},{4,6},{5,7},{6,4},{7,5},{8,10},{9,11},{10,... | collective-permute-start | bytes 2162696 | tf_op jit(solution)/shard_map/ppermute | solution.py:41
  112.4 27.5 %collective-permute-start.11 = (bf16[2,2,352,512]{3,2,1,0:T(8,128)(2,1)}, bf16[2,2,352,512]{3,2,1,0:T(8,128)(2,1)}, u32[]{:S(2)}, u32[]{:S(2)}) collective-permute-start(bf16[2,2,352,512]{3,2,1,0:T(8,128)(2,1)} %pad_maximum_fusion.refs_3_.refs_4_), channel_id=1, source_target_pairs={{16,0},{18,2},{1,17},{3,19},{20,4},{22,6},{5,21},{7,23},{24,8},{26... | collective-permute-start | bytes 4325384 | tf_op jit(solution)/shard_map/ppermute | solution.py:651
  122.8 41.2 %collective-permute-start.14 = (bf16[2,256,1408]{2,1,0:T(8,128)(2,1)}, bf16[2,256,1408]{2,1,0:T(8,128)(2,1)}, u32[]{:S(2)}, u32[]{:S(2)}) collective-permute-start(bf16[2,256,1408]{2,1,0:T(8,128)(2,1)} %get-tuple-element.136), channel_id=1, source_target_pairs={{0,2},{1,3},{2,0},{3,1},{4,6},{5,7},{6,4},{7,5},{8,10},{9,11},{10,... | collective-permute-start | bytes 4325384 | tf_op jit(solution)/shard_map/ppermute | solution.py:41
  123.4 41.2 %collective-permute-start.15 = (bf16[2,256,1408]{2,1,0:T(8,128)(2,1)}, bf16[2,256,1408]{2,1,0:T(8,128)(2,1)}, u32[]{:S(2)}, u32[]{:S(2)}) collective-permute-start(bf16[2,256,1408]{2,1,0:T(8,128)(2,1)} %get-tuple-element.138), channel_id=1, source_target_pairs={{0,16},{16,0},{1,17},{17,1},{2,18},{18,2},{3,19},{19,3},{4,20},{20... | collective-permute-start | bytes 4325384 | tf_op jit(solution)/shard_map/ppermute | solution.py:41
  139.8 8.6 %copy-start = (bf16[800,1024]{1,0:T(8,128)(2,1)}, bf16[800,1024]{1,0:T(8,128)(2,1)S(1)}, u32[]{:S(2)}) copy-start(bf16[800,1024]{1,0:T(8,128)(2,1)S(1)} %get-tuple-element.127.refs_2_.refs_1_) | copy-start | bytes 4915204
  139.8 5.2 %collective-permute-start.9 = (bf16[800,1024]{1,0:T(8,128)(2,1)S(1)}, bf16[800,1024]{1,0:T(8,128)(2,1)S(1)}, u32[]{:S(2)}, u32[]{:S(2)}) collective-permute-start(bf16[800,1024]{1,0:T(8,128)(2,1)S(1)} %get-tuple-element.127.refs_2_.refs_1_), channel_id=1, source_target_pairs={{0,1},{1,0},{2,3},{3,2},{4,5},{5,4},{6,7},{7,6},{8,9},{9,8},{10,11... | collective-permute-start | bytes 4915208 | tf_op jit(solution)/shard_map/ppermute | solution.py:41
  139.9 8.5 %copy-start.20 = (bf16[512,768]{1,0:T(8,128)(2,1)S(1)}, bf16[512,768]{1,0:T(8,128)(2,1)}, u32[]{:S(2)}) copy-start(bf16[512,768]{1,0:T(8,128)(2,1)} %copy-done.19) | copy-start | bytes 2359300
  143.5 28.7 %collective-permute-start.12 = (bf16[2,352,512]{2,1,0:T(8,128)(2,1)}, bf16[2,352,512]{2,1,0:T(8,128)(2,1)S(1)}, u32[]{:S(2)}, u32[]{:S(2)}) collective-permute-start(bf16[2,352,512]{2,1,0:T(8,128)(2,1)} %get-tuple-element.134), channel_id=1, source_target_pairs={{16,0},{18,2},{1,17},{3,19},{20,4},{22,6},{5,21},{7,23},{24,8},{26... | collective-permute-start | bytes 2162696 | tf_op jit(solution)/shard_map/ppermute | solution.py:651
  145.0 27.2 %collective-permute-start.13 = (bf16[2,352,512]{2,1,0:T(8,128)(2,1)}, bf16[2,352,512]{2,1,0:T(8,128)(2,1)}, u32[]{:S(2)}, u32[]{:S(2)}) collective-permute-start(bf16[2,352,512]{2,1,0:T(8,128)(2,1)} %get-tuple-element.135), channel_id=1, source_target_pairs={{0,2},{2,0},{17,19},{19,17},{4,6},{6,4},{21,23},{23,21},{8,10},{10... | collective-permute-start | bytes 2162696 | tf_op jit(solution)/shard_map/ppermute | solution.py:660
  157.3 51.6 %all-to-all-start.3 = ((bf16[4,112,1024]{2,1,0:T(8,128)(2,1)}), bf16[4,112,1024]{2,1,0:T(8,128)(2,1)S(1)}, u32[]{:S(2)}, u32[]{:S(2)}) async-start(bf16[4,112,1024]{2,1,0:T(8,128)(2,1)} %get-tuple-element.133), calls=%async_computation.3 | async-start | bytes 1835008 | tf_op jit(solution)/shard_map/all_to_all | solution.py:45
  162.0 38.4 %collective-permute-start.17 = (bf16[2,2,128,1024]{3,2,1,0:T(8,128)(2,1)}, bf16[2,2,128,1024]{3,2,1,0:T(8,128)(2,1)}, u32[]{:S(2)}, u32[]{:S(2)}) collective-permute-start(bf16[2,2,128,1024]{3,2,1,0:T(8,128)(2,1)} %copy-done.11), channel_id=1, source_target_pairs={{0,4},{4,0},{8,12},{12,8},{1,5},{5,1},{9,13},{13,9},{2,6},{6,2},{1... | collective-permute-start | bytes 3145736 | tf_op jit(solution)/shard_map/ppermute | solution.py:41
  177.7 27.3 %collective-permute-start.16 = (bf16[352,1024]{1,0:T(8,128)(2,1)}, bf16[352,1024]{1,0:T(8,128)(2,1)S(1)}, u32[]{:S(2)}, u32[]{:S(2)}) collective-permute-start(bf16[352,1024]{1,0:T(8,128)(2,1)} %get-tuple-element.143), channel_id=1, source_target_pairs={{0,1},{1,0},{2,3},{3,2},{4,5},{5,4},{6,7},{7,6},{8,9},{9,8},{10,11... | collective-permute-start | bytes 2162696 | tf_op jit(solution)/shard_map/ppermute | solution.py:41
  177.7 14.4 %collective-permute-start.19 = (bf16[4,2,32,1024]{3,2,0,1:T(8,128)(2,1)S(1)}, bf16[4,2,32,1024]{3,2,0,1:T(8,128)(2,1)S(1)}, u32[]{:S(2)}, u32[]{:S(2)}) collective-permute-start(bf16[4,2,32,1024]{3,2,0,1:T(8,128)(2,1)S(1)} %copy.35), channel_id=1, source_target_pairs={{0,2},{1,3},{2,0},{3,1},{4,6},{5,7},{6,4},{7,5},{8,10},{9,11},{10,... | collective-permute-start | bytes 1572872 | tf_op jit(solution)/shard_map/ppermute | solution.py:41
  178.3 39.6 %collective-permute-start.20 = (bf16[4,2,48,1024]{3,2,1,0:T(8,128)(2,1)S(1)}, bf16[4,2,48,1024]{3,2,1,0:T(8,128)(2,1)}, u32[]{:S(2)}, u32[]{:S(2)}) collective-permute-start(bf16[4,2,48,1024]{3,2,1,0:T(8,128)(2,1)S(1)} %copy-done.13), channel_id=1, source_target_pairs={{0,16},{16,0},{1,17},{17,1},{2,18},{18,2},{3,19},{19,3},{4,20},{20... | collective-permute-start | bytes 2359304 | tf_op jit(solution)/shard_map/ppermute | solution.py:41
  178.3 54.0 %collective-permute-start.26 = (bf16[256,1408]{1,0:T(8,128)(2,1)}, bf16[256,1408]{1,0:T(8,128)(2,1)}, u32[]{:S(2)}, u32[]{:S(2)}) collective-permute-start(bf16[256,1408]{1,0:T(8,128)(2,1)} %get-tuple-element.164), channel_id=1, source_target_pairs={{0,16},{16,0},{1,17},{17,1},{2,18},{18,2},{3,19},{19,3},{4,20},{20... | collective-permute-start | bytes 2162696 | tf_op jit(solution)/shard_map/ppermute | solution.py:41
  192.1 10.5 %copy-start.38 = (bf16[4,2,32,1024]{3,2,0,1:T(8,128)(2,1)}, bf16[4,2,32,1024]{3,2,0,1:T(8,128)(2,1)S(1)}, u32[]{:S(2)}) copy-start(bf16[4,2,32,1024]{3,2,0,1:T(8,128)(2,1)S(1)} %collective-permute-done.19) | copy-start | bytes 1572868
  192.1 40.7 %collective-permute-start.27 = (bf16[256,1408]{1,0:T(8,128)(2,1)}, bf16[256,1408]{1,0:T(8,128)(2,1)}, u32[]{:S(2)}, u32[]{:S(2)}) collective-permute-start(bf16[256,1408]{1,0:T(8,128)(2,1)} %get-tuple-element.165), channel_id=1, source_target_pairs={{0,2},{1,3},{2,0},{3,1},{4,6},{5,7},{6,4},{7,5},{8,10},{9,11},{10,... | collective-permute-start | bytes 2162696 | tf_op jit(solution)/shard_map/ppermute | solution.py:41
  202.6 25.5 %collective-permute-start.23 = (bf16[2,128,1024]{2,1,0:T(8,128)(2,1)}, bf16[2,128,1024]{2,1,0:T(8,128)(2,1)}, u32[]{:S(2)}, u32[]{:S(2)}) collective-permute-start(bf16[2,128,1024]{2,1,0:T(8,128)(2,1)} %get-tuple-element.158), channel_id=1, source_target_pairs={{0,8},{4,12},{8,0},{12,4},{1,9},{5,13},{9,1},{13,5},{2,10},{6,14},... | collective-permute-start | bytes 1572872 | tf_op jit(solution)/shard_map/ppermute | solution.py:41
  216.7 22.0 %collective-permute-start.18 = (bf16[128,1024]{1,0:T(8,128)(2,1)}, bf16[128,1024]{1,0:T(8,128)(2,1)}, u32[]{:S(2)}, u32[]{:S(2)}) collective-permute-start(bf16[128,1024]{1,0:T(8,128)(2,1)} %slice.123), channel_id=1, source_target_pairs={{16,0},{0,16},{17,1},{1,17},{18,2},{2,18},{19,3},{3,19},{20,4},{4,... | collective-permute-start | bytes 786440 | tf_op jit(solution)/shard_map/ppermute | solution.py:1265
  220.5 24.8 %collective-permute-start.22 = (bf16[4,48,1024]{2,1,0:T(8,128)(2,1)}, bf16[4,48,1024]{2,1,0:T(8,128)(2,1)}, u32[]{:S(2)}, u32[]{:S(2)}) collective-permute-start(bf16[4,48,1024]{2,1,0:T(8,128)(2,1)} %get-tuple-element.157), channel_id=1, source_target_pairs={{0,2},{1,3},{2,0},{3,1},{4,6},{5,7},{6,4},{7,5},{8,10},{9,11},{10,... | collective-permute-start | bytes 1179656 | tf_op jit(solution)/shard_map/ppermute | solution.py:41
  228.1 13.5 %collective-permute-start.21 = (bf16[4,32,1024]{2,1,0:T(8,128)(2,1)S(1)}, bf16[4,32,1024]{2,1,0:T(8,128)(2,1)S(1)}, u32[]{:S(2)}, u32[]{:S(2)}) collective-permute-start(bf16[4,32,1024]{2,1,0:T(8,128)(2,1)S(1)} %copy-done.58), channel_id=1, source_target_pairs={{0,16},{16,0},{1,17},{17,1},{2,18},{18,2},{3,19},{19,3},{4,20},{20... | collective-permute-start | bytes 786440 | tf_op jit(solution)/shard_map/ppermute | solution.py:41
  232.3 9.9 %collective-permute-start.24 = (bf16[2,32,1024]{2,1,0:T(8,128)(2,1)}, bf16[2,32,1024]{2,1,0:T(8,128)(2,1)S(1)}, u32[]{:S(2)}, u32[]{:S(2)}) collective-permute-start(bf16[2,32,1024]{2,1,0:T(8,128)(2,1)} %get-tuple-element.161), channel_id=1, source_target_pairs={{0,2},{1,3},{2,0},{3,1},{4,6},{5,7},{6,4},{7,5},{8,10},{9,11},{10,... | collective-permute-start | bytes 393224 | tf_op jit(solution)/shard_map/ppermute | solution.py:41
  232.8 9.4 %collective-permute-start.25 = (bf16[2,32,1024]{2,1,0:T(8,128)(2,1)}, bf16[2,32,1024]{2,1,0:T(8,128)(2,1)S(1)}, u32[]{:S(2)}, u32[]{:S(2)}) collective-permute-start(bf16[2,32,1024]{2,1,0:T(8,128)(2,1)} %get-tuple-element.162), channel_id=1, source_target_pairs={{0,16},{16,0},{1,17},{17,1},{2,18},{18,2},{3,19},{19,3},{4,20},{20... | collective-permute-start | bytes 393224 | tf_op jit(solution)/shard_map/ppermute | solution.py:41
  238.7 20.5 %collective-permute-start.30 = (bf16[2,128,1408]{2,1,0:T(8,128)(2,1)}, bf16[2,128,1408]{2,1,0:T(8,128)(2,1)}, u32[]{:S(2)}, u32[]{:S(2)}) collective-permute-start(bf16[2,128,1408]{2,1,0:T(8,128)(2,1)} %get-tuple-element.171), channel_id=1, source_target_pairs={{0,1},{1,0},{2,3},{3,2},{4,5},{5,4},{6,7},{7,6},{8,9},{9,8},{10,11... | collective-permute-start | bytes 2162696 | tf_op jit(solution)/shard_map/ppermute | solution.py:41
  244.8 10.3 %collective-permute-start.29 = (bf16[32,1024]{1,0:T(8,128)(2,1)}, bf16[32,1024]{1,0:T(8,128)(2,1)}, u32[]{:S(2)}, u32[]{:S(2)}) collective-permute-start(bf16[32,1024]{1,0:T(8,128)(2,1)} %get-tuple-element.169), channel_id=1, source_target_pairs={{0,2},{1,3},{2,0},{3,1},{4,6},{5,7},{6,4},{7,5},{8,10},{9,11},{10,... | collective-permute-start | bytes 196616 | tf_op jit(solution)/shard_map/ppermute | solution.py:41
  247.6 21.3 %all-to-all-start.4 = ((bf16[4,80,1024]{2,1,0:T(8,128)(2,1)}), bf16[4,80,1024]{2,1,0:T(8,128)(2,1)S(1)}, u32[]{:S(2)}, u32[]{:S(2)}) async-start(bf16[4,80,1024]{2,1,0:T(8,128)(2,1)} %pad_maximum_fusion.2), calls=%async_computation.4 | async-start | bytes 1310720 | tf_op jit(solution)/shard_map/all_to_all | solution.py:45
  251.1 6.5 %copy-start.44 = (f32[2,32,1024]{2,1,0:T(8,128)S(1)}, f32[2,32,1024]{2,1,0:T(8,128)}, u32[]{:S(2)}) copy-start(f32[2,32,1024]{2,1,0:T(8,128)} %get-tuple-element.160.refs_1_) | copy-start | bytes 786436
  253.3 4.3 %collective-permute-start.28 = (bf16[32,1024]{1,0:T(8,128)(2,1)S(1)}, bf16[32,1024]{1,0:T(8,128)(2,1)S(1)}, u32[]{:S(2)}, u32[]{:S(2)}) collective-permute-start(bf16[32,1024]{1,0:T(8,128)(2,1)S(1)} %copy-done.59), channel_id=1, source_target_pairs={{0,16},{16,0},{1,17},{17,1},{2,18},{18,2},{3,19},{19,3},{4,20},{20... | collective-permute-start | bytes 196616 | tf_op jit(solution)/shard_map/ppermute | solution.py:41
  (48 other events, 146.2 us)

commit v2 on v1

v2 whole, which is shorter than its diff:
```python
import functools

import jax
import jax.numpy as jnp
from jax import lax
from jax.experimental import pallas as pl
from jax.experimental.pallas import tpu as pltpu
from jax.sharding import PartitionSpec as P

HDIM = 64
NB = 32
GROUP = 4
LANES = 128
EPSILON = 1e-06
FULL_PRECISION = lax.Precision.HIGHEST
LOW = jnp.bfloat16
FULL = jnp.float32
OUTSIDE = -1e30
GELU_SCALE = 0.7978845608028654
GELU_CUBE = 0.044715


def rms_norm(rows, gain):
    return rows * lax.rsqrt(jnp.mean(rows * rows, axis=-1, keepdims=True) + EPSILON) * gain


def dot_rows(left, right):
    return lax.dot_general(left, right, (((1,), (0,)), ((), ())), preferred_element_type=FULL)


def dot_back(left, right):
    return lax.dot_general(left, right, (((1,), (1,)), ((), ())), preferred_element_type=FULL)


def transpose_dot(left, right):
    return lax.dot_general(left, right, (((0,), (0,)), ((), ())), preferred_element_type=FULL)


def swapped(array, axis, bit):
    size = lax.axis_size(axis)
    return lax.ppermute(array, axis, [(i, i ^ bit) for i in range(size)])


def shifted(array, axis, shift):
    size = lax.axis_size(axis)
    return lax.ppermute(array, axis, [(i, (i + shift) % size) for i in range(size)])


def to_experts(blocks):
    return [blocks[0]] + [shifted(blocks[k], "exp", k) for k in range(1, len(blocks))]


def from_experts(blocks):
    return [blocks[0]] + [shifted(blocks[k], "exp", len(blocks) - k) for k in range(1, len(blocks))]


def over_experts(blocks):
    return lax.all_to_all(blocks, "exp", split_axis=0, concat_axis=0, tiled=True)


MICROSECOND = 1.15e9


def call(
    body, name, inputs, outputs, us, grid=None, token=None, prefetch=(), scratch=(), vmem=6,
    near_in=(), near_out=(), far_in=(), far_out=(), fetch=(),
    part_in=None,
):
    part_in = dict(part_in or {})
    far_in = tuple(far_in) + tuple(part_in)
    inputs = list(inputs) + [(array, None) for array in fetch]
    outputs = list(outputs) + [whole_out(array.shape, array.dtype) for array in fetch]
    n_pre, n_in, n_out = len(prefetch), len(inputs), len(outputs)
    held = [] if token is None else [token]
    n_far, n_scratch = len(far_in) + len(far_out), len(scratch)

    def kernel(*refs):
        split = n_pre + n_in
        outs = split + len(held)
        rest = refs[outs + n_out + 1 :]
        ins_here, outs_here = list(refs[:split]), list(refs[outs : outs + n_out])
        copies = []
        for number, at in enumerate(far_in):
            here = rest[n_scratch + number]
            source = refs[n_pre + at].at[part_in[at]] if at in part_in else refs[n_pre + at]
            copies.append(pltpu.make_async_copy(source, here, rest[-1].at[number]))
            ins_here[n_pre + at] = here
        for copy in copies:
            copy.start()
        fetches = [
            pltpu.make_async_copy(ins_here.pop(), outs_here.pop(), rest[-1].at[n_far + number])
            for number in range(len(fetch))
        ]
        for copy in fetches:
            copy.start()
        for copy in copies:
            copy.wait()
        copies = []
        for number, at in enumerate(far_out, len(far_in)):
            here = rest[n_scratch + number]
            copies.append(pltpu.make_async_copy(here, refs[outs + at], rest[-1].at[number]))
            outs_here[at] = here
        body(*ins_here, *outs_here, *rest[:n_scratch])
        for copy in fetches:
            copy.wait()
        for copy in copies:
            copy.start()
        for copy in copies:
            copy.wait()

    where = lambda at, near: pltpu.VMEM if at in near else pltpu.HBM
    arrays = [array for array, _ in inputs]
    shapes = [(shape, dtype) for shape, dtype, _ in outputs]
    anywhere = pl.BlockSpec(memory_space=pl.ANY)
    if grid is None:
        near = pl.BlockSpec(memory_space=pltpu.VMEM)
        far = [at in far_in or spec is None for at, (_, spec) in enumerate(inputs)]
        far_results = [at in far_out or spec is None for at, (_, _, spec) in enumerate(outputs)]
        left = lambda at: tuple(
            size if axis >= len(part_in.get(at, ())) else len(range(size)[part_in[at][axis]])
            for axis, size in enumerate(arrays[at].shape)
            if axis >= len(part_in.get(at, ())) or isinstance(part_in[at][axis], slice)
        )
        buffers = [pltpu.VMEM(left(at), arrays[at].dtype) for at in far_in]
        buffers += [pltpu.VMEM(*shapes[at]) for at in far_out]
        n_sems = n_far + len(fetch)
        buffers += [pltpu.SemaphoreType.DMA((n_sems,))] if n_sems else []
        form = dict(
            in_specs=[pl.BlockSpec(memory_space=pltpu.SMEM)] * n_pre
            + [anywhere if away else near for away in far]
            + [anywhere] * len(held),
            out_specs=[anywhere if away else near for away in far_results] + [anywhere],
            scratch_shapes=list(scratch) + buffers,
        )
        arrays = [
            pltpu.with_memory_space_constraint(array, pltpu.HBM) if away else array
            for array, away in zip(arrays, far)
        ]
        shapes = [
            pltpu.HBM(*one) if away else jax.ShapeDtypeStruct(*one)
            for away, one in zip(far_results, shapes)
        ]
    else:
        form = dict(
            grid_spec=pltpu.PrefetchScalarGridSpec(
                num_scalar_prefetch=n_pre,
                grid=grid,
                in_specs=[spec for _, spec in inputs] + [anywhere] * len(held),
                out_specs=[spec for _, _, spec in outputs] + [anywhere],
                scratch_shapes=list(scratch),
            )
        )
        arrays = [
            pltpu.with_memory_space_constraint(array, where(at, near_in))
            for at, array in enumerate(arrays)
        ]
        shapes = [where(at, near_out)(*one) for at, one in enumerate(shapes)]
    held = [pltpu.with_memory_space_constraint(array, pltpu.HBM) for array in held]
    results = pl.pallas_call(
        kernel,
        out_shape=shapes + [pltpu.HBM((8, LANES), FULL)],
        cost_estimate=pl.CostEstimate(
            flops=int(us * MICROSECOND), bytes_accessed=1, transcendentals=0
        ),
        compiler_params=pltpu.CompilerParams(vmem_limit_bytes=vmem * 2**20),
        name=name,
        **form,
    )(*prefetch, *arrays, *held)
    return list(results[:-1]), results[-1]


def whole(array):
    return array, pl.BlockSpec(array.shape, lambda *_: (0,) * array.ndim)


def whole_out(shape, dtype):
    return shape, dtype, pl.BlockSpec(shape, lambda *_: (0,) * len(shape))


def hold(token, *arrays):
    anywhere = pl.BlockSpec(memory_space=pl.ANY)
    return pl.pallas_call(
        lambda *refs: None,
        in_specs=[anywhere] * (len(arrays) + 1),
        out_specs=[anywhere] * len(arrays),
        out_shape=[jax.ShapeDtypeStruct(array.shape, array.dtype) for array in arrays],
        input_output_aliases={at + 1: at for at in range(len(arrays))},
        cost_estimate=pl.CostEstimate(flops=1, bytes_accessed=1, transcendentals=0),
        name="hold",
    )(token, *arrays)


def pass_kernel(*refs):
    half = len(refs) // 2
    for ref, out_ref in zip(refs[:half], refs[half:]):
        out_ref[...] = ref[...]


def pass_on(token, *arrays):
    return call(
        pass_kernel,
        "pass_on",
        [whole(array) for array in arrays],
        [whole_out(array.shape, array.dtype) for array in arrays],
        token=token,
        us=1,
    )


def eye(size):
    rows = lax.broadcasted_iota(jnp.int32, (size, size), 0)
    return rows == lax.broadcasted_iota(jnp.int32, (size, size), 1)


def to_column(row):
    size = row.shape[1]
    return jnp.sum(jnp.where(eye(size), row, jnp.zeros_like(row)), 1, keepdims=True)


def front_kernel(
    at_ref, routes_ref, gates_ref, grad_ref, seg_ref, rows_ref,
    spread_ref, pick_ref, mask_ref, copy_ref, *out_refs,
):
    top, tokens = routes_ref.shape
    experts, capacity = len(out_refs), out_refs[0].shape[0]
    routes = [routes_ref[r : r + 1, :] for r in range(top)]
    gates = [gates_ref[r : r + 1, :] for r in range(top)]
    before = lax.broadcasted_iota(jnp.int32, (tokens, tokens), 0)
    before = before < lax.broadcasted_iota(jnp.int32, (tokens, tokens), 1)
    slots = lax.broadcasted_iota(jnp.int32, (capacity, tokens), 0).astype(FULL)
    for e in range(experts):
        part = pl.ds(e * capacity, capacity)
        name = lax.rem(at_ref[3] + e, experts)
        hits = [jnp.where(route == name, 1.0, 0.0) for route in routes]
        named = functools.reduce(jnp.add, hits)
        slot = jnp.sum(jnp.where(before, to_column(named), 0.0), 0, keepdims=True)
        place = (slots == slot).astype(FULL)
        spread = place * named
        gate = functools.reduce(jnp.add, [hit * g for hit, g in zip(hits, gates)])
        spread_low = spread.astype(LOW)
        spread_ref[part, :] = spread_low
        for r in range(top):
            pick_ref[part, pl.ds(r * tokens, tokens)] = (place * hits[r]).astype(LOW)
        slot_gate = jnp.sum(spread * gate, 1, keepdims=True)
        out_refs[e][...] = (slot_gate * dot_rows(spread_low, grad_ref[...])).astype(LOW)
    length = mask_ref.shape[1]
    ctx = at_ref[0]
    seg = jnp.broadcast_to(seg_ref[...].astype(FULL), (8, length))
    keys = pltpu.roll(seg, length - (ctx + 1) * tokens, 1)[:1, :]
    at_row = lax.broadcasted_iota(jnp.int32, (tokens, length), 0) + (length - tokens)
    at_key = lax.broadcasted_iota(jnp.int32, (tokens, length), 1)
    own = jnp.sum(jnp.where(at_row == at_key, keys, 0.0), 1, keepdims=True)
    allowed = (at_key <= at_row) & (own == keys) & (at_key >= length - (ctx + 1) * tokens)
    mask_ref[...] = jnp.where(allowed, 0.0, OUTSIDE)
    copy_ref[...] = rows_ref[...]


def front(at, routes, gates, grad, seg, rows, experts, capacity):
    top, tokens = routes.shape
    slots = experts * capacity
    return call(
        front_kernel,
        "front",
        [whole(array) for array in (routes, gates, grad, seg, rows)],
        [
            whole_out((slots, tokens), LOW),
            whole_out((slots, top * tokens), LOW),
            whole_out((tokens, seg.shape[1]), FULL),
            whole_out(rows.shape, LOW),
        ]
        + [whole_out((capacity, grad.shape[1]), LOW)] * experts,
        prefetch=(at,),
        far_in=(0, 1, 2, 3, 4),
        far_out=(1,),
        us=1.5,
    )


def bias_kernel(buckets_ref, table_ref, hot_ref, bias_ref):
    heads, rows, keys = bias_ref.shape
    width = hot_ref.shape[1]
    buckets = buckets_ref[...].astype(FULL)
    column = jnp.sum(jnp.where(eye(keys), buckets, 0.0), 1, keepdims=True)
    distance = lax.broadcasted_iota(jnp.int32, (keys, width), 0)
    lane = lax.broadcasted_iota(jnp.int32, (keys, width), 1)
    turned = jnp.sum(jnp.where(distance + lane == keys - 1, column, 0.0), 0, keepdims=True)
    bucket = lax.broadcasted_iota(jnp.int32, (NB, width), 0).astype(FULL)
    hot = jnp.where(bucket == turned, 1.0, 0.0)
    hot_ref[...] = hot
    by_lane = lax.dot_general(
        table_ref[...], hot, (((0,), (0,)), ((), ())), precision=FULL_PRECISION,
        preferred_element_type=FULL,
    )
    for head in range(heads):
        line = jnp.broadcast_to(by_lane[head : head + 1, :], (8, width))
        line = pltpu.roll(line, keys + 1, 1, stride=1, stride_axis=0)
        for start in range(0, rows, 8):
            moved = line if start == 0 else pltpu.roll(line, start, 1)
            bias_ref[head, pl.ds(start, 8), :] = moved[:, :keys]


def bias_tiles(buckets, table, rows, fetch):
    heads, keys = table.shape[1], buckets.shape[1]
    return call(
        bias_kernel,
        "bias_tiles",
        [whole(buckets), whole(table)],
        [whole_out((NB, keys + rows), FULL), whole_out((heads, rows, keys), FULL)],
        us=2.5,
        vmem=16,
        fetch=fetch,
    )


def half_lanes(half, shape):
    lane = lax.broadcasted_iota(jnp.int32, shape, 1)
    return lane < HDIM if half == 0 else lane >= HDIM


def attention_kernel(q_ref, k_ref, v_ref, bias_ref, mask_ref, out_ref, probs_ref, peak_ref):
    groups = peak_ref.shape[0]

    def group(step, _):
        mask = mask_ref[...]
        for pair in range(GROUP // 2):
            lanes = pair_lanes(step, pair)
            queries, keys, values = q_ref[:, lanes], k_ref[:, lanes], v_ref[:, lanes]
            parts = []
            for half in range(2):
                at = 2 * pair + half
                own = half_lanes(half, queries.shape)
                raw = dot_back(jnp.where(own, queries, jnp.zeros_like(queries)), keys)
                raw = raw * HDIM**-0.5 + mask
                top = jnp.max(raw, axis=0, keepdims=True)
                best = top[:, :LANES]
                for start in range(LANES, top.shape[1], LANES):
                    best = jnp.maximum(best, top[:, start : start + LANES])
                peak_ref[step, at : at + 1, :] = best
                scores = raw + bias_ref[step * GROUP + at]
                raised = jnp.exp(scores - jnp.max(scores, axis=1, keepdims=True))
                probs = raised * (1.0 / jnp.sum(raised, axis=1, keepdims=True))
                probs_low = probs.astype(LOW)
                probs_ref[step * GROUP + at] = probs_low
                parts.append(dot_rows(probs_low, values))
            first = half_lanes(0, parts[0].shape)
            out_ref[:, lanes] = jnp.where(first, parts[0], parts[1]).astype(LOW)
        return 0

    lax.fori_loop(0, groups, group, 0)


def pair_lanes(step, pair):
    return pl.ds(pl.multiple_of(step * GROUP * HDIM + pair * LANES, LANES), LANES)


def attention(queries, keys, values, bias, mask, fetch):
    rows, width = queries.shape
    length = keys.shape[0]
    heads = width // HDIM
    (out, probs, peak, *fetched), _ = call(
        attention_kernel,
        "attention",
        [whole(array) for array in (queries, keys, values, bias, mask)],
        [
            whole_out((rows, width), LOW),
            whole_out((heads, rows, length), LOW),
            whole_out((heads // GROUP, 8, LANES), FULL),
        ],
        us=4.5,
        vmem=10,
        far_out=(1,),
        fetch=fetch,
    )
    return out, probs, peak, *fetched


def attention_back_kernel(
    q_ref, k_ref, v_ref, probs_ref, grad_ref, dq_ref, dk_ref, dv_ref, lines_ref
):
    groups = lines_ref.shape[0]
    rows, length = probs_ref.shape[1:]
    scale = HDIM**-0.5

    def group(step, _):
        for pair in range(GROUP // 2):
            lanes = pair_lanes(step, pair)
            queries, keys, values, grad = (
                ref[:, lanes] for ref in (q_ref, k_ref, v_ref, grad_ref)
            )
            dq, dk, dv = [], [], []
            for half in range(2):
                at = 2 * pair + half
                own = half_lanes(half, grad.shape)
                dp = dot_back(jnp.where(own, grad, jnp.zeros_like(grad)), values)
                probs_low = probs_ref[step * GROUP + at]
                probs = probs_low.astype(FULL)
                ds = probs * (dp - jnp.sum(probs * dp, axis=1, keepdims=True))
                ds_low = ds.astype(LOW)
                dq.append(dot_rows(ds_low, keys))
                dk.append(transpose_dot(ds_low, queries))
                dv.append(transpose_dot(probs_low, grad))
                wide = jnp.concatenate([ds, jnp.zeros((rows, rows), FULL)], axis=1)
                total = wide[rows - 8 :, :]
                for start in range(0, rows - 8, 8):
                    total = total + pltpu.roll(wide[start : start + 8, :], rows - 8 - start, 1)
                line = lax.broadcasted_iota(jnp.int32, total.shape, 0)
                for bit in (1, 2, 4):
                    total = jnp.where(((7 - line) & bit) != 0, pltpu.roll(total, bit, 1), total)
                lines_ref[step, at : at + 1, :] = jnp.sum(total, axis=0, keepdims=True)
            first = half_lanes(0, dq[0].shape)
            dq_ref[:, lanes] = (jnp.where(first, dq[0], dq[1]) * scale).astype(LOW)
            first = half_lanes(0, dk[0].shape)
            dk_ref[:, lanes] = (jnp.where(first, dk[0], dk[1]) * scale).astype(LOW)
            dv_ref[:, lanes] = jnp.where(first, dv[0], dv[1]).astype(LOW)
        return 0

    lax.fori_loop(0, groups, group, 0)


def packed_back_kernel(
    q_ref, k_ref, v_ref, probs_ref, grad_ref, branch_ref, hot_ref, gain_ref, out_ref, lines_ref
):
    rows, length = probs_ref.shape[1:]
    ends = [0, rows, rows + length, rows + 2 * length, 2 * rows + 2 * length]
    parts = [out_ref.at[pl.ds(a, b - a), :] for a, b in zip(ends, ends[1:])]
    attention_back_kernel(q_ref, k_ref, v_ref, probs_ref, grad_ref, *parts[:3], lines_ref)
    parts[3][...] = branch_ref[...]
    groups = lines_ref.shape[0]
    width = gain_ref.shape[1]
    devices = out_ref.shape[0] - ends[4]
    own, turns = width // devices, LANES * devices // width
    device = lax.broadcasted_iota(jnp.int32, (devices, width), 0)
    feature = lax.broadcasted_iota(jnp.int32, (devices, width), 1)
    spread = jnp.where(feature // own == device, gain_ref[...], 0.0)
    folded = functools.reduce(
        jnp.add, [spread[:, start : start + LANES] for start in range(0, width, LANES)]
    )
    device = lax.broadcasted_iota(jnp.int32, folded.shape, 0)
    small = folded
    for turn_by in range(1, turns):
        moved = pltpu.roll(folded, LANES - turn_by * own, 1)
        small = jnp.where(device % turns == turn_by, moved, small)
    lines = jnp.concatenate([lines_ref[g, :GROUP, :] for g in range(groups)], axis=0)
    blank = jnp.zeros((LANES - TABLE_LANE - lines.shape[0], lines.shape[1]), FULL)
    lines = jnp.concatenate([jnp.zeros((TABLE_LANE, lines.shape[1]), FULL), lines, blank], axis=0)
    upper = lines.astype(LOW)
    lower = (lines - upper.astype(FULL)).astype(LOW)
    hot = hot_ref[...].astype(LOW)
    small = small + dot_back(hot, upper) + dot_back(hot, lower)
    out_ref[pl.ds(ends[4], devices), :LANES] = small.astype(LOW)


def attention_back(queries, keys, values, probs, grad, token, packed=None):
    rows, width = queries.shape
    length = keys.shape[0]
    heads = width // HDIM
    lines = whole_out((heads // GROUP, 8, length + rows), FULL)
    inputs = [whole(array) for array in (queries, keys, values, probs, grad)]
    if packed is None:
        outs, token = call(
            attention_back_kernel,
            "attention_back",
            inputs,
            [whole_out((size, width), LOW) for size in (rows, length, length)] + [lines],
            token=token,
            us=6.6,
            vmem=16,
        )
        return *outs, token
    branch, hot, gain, devices = packed
    (out, _), token = call(
        packed_back_kernel,
        "attention_back",
        inputs + [whole(branch), whole(hot), whole(gain)],
        [whole_out((2 * rows + 2 * length + devices, width), LOW), lines],
        token=token,
        us=7,
        vmem=16,
        far_in=(0, 1, 2, 3, 6),
    )
    return out, token


def post_kernel(attended_ref, weights_ref, rows_ref, gain_ref, spread_ref, after_ref, *out_refs):
    after = rows_ref[...].astype(FULL) + dot_rows(attended_ref[...], weights_ref[...])
    after_ref[...] = after
    sent = rms_norm(after, gain_ref[...]).astype(LOW)
    size = out_refs[0].shape[0]
    for at, out_ref in enumerate(out_refs):
        out_ref[...] = dot_rows(spread_ref[pl.ds(at * size, size), :], sent).astype(LOW)


def after_attention(attended, weights, rows, gain, spread, experts):
    tokens, width = rows.shape
    (after, *sent), _ = call(
        post_kernel,
        "post",
        [whole(array) for array in (attended, weights, rows, gain, spread)],
        [whole_out((tokens, width), FULL)]
        + [whole_out((spread.shape[0] // experts, width), LOW)] * experts,
        far_out=(0,),
        us=2,
    )
    return after, sent


def gather_kernel(*refs):
    size = refs[0].shape[0]
    for at, ref in enumerate(refs[:-1]):
        refs[-1][pl.ds(at * size, size), :] = ref[...]


def side_by_side(blocks, token):
    size, width = blocks[0].shape
    (out,), token = call(
        gather_kernel,
        "gather",
        [whole(block) for block in blocks],
        [whole_out((len(blocks) * size, width), LOW)],
        token=token,
        us=1,
    )
    return out, token


def expert_part(gate, up, dhid):
    square = gate * gate
    curve = jnp.tanh(GELU_SCALE * gate * (1.0 + GELU_CUBE * square))
    upper = 0.5 * (1.0 + curve)
    gelu = gate * upper
    slope = upper + 0.5 * gate * (1.0 - curve * curve) * (
        GELU_SCALE * (1.0 + 3.0 * GELU_CUBE * square)
    )
    hid = (gelu * up).astype(LOW)
    dgate = (dhid * up * slope).astype(LOW)
    dup = (dhid * gelu).astype(LOW)
    return hid, dgate, dup


def expert_kernel(
    rows_ref, grad_ref, gate_w_ref, up_w_ref, down_w_ref,
    out_ref, back_ref, dgate_ref, dup_ref, hid_ref, turned_ref, out_sum, back_sum,
):
    step = pl.program_id(0)

    @pl.when(step == 0)
    def _():
        out_sum[...] = jnp.zeros_like(out_sum)
        back_sum[...] = jnp.zeros_like(back_sum)

    rows, grad = rows_ref[...], grad_ref[...]
    gate_w, up_w, down_w = gate_w_ref[0], up_w_ref[0], down_w_ref[0]
    hid, dgate, dup = expert_part(
        dot_rows(rows, gate_w), dot_rows(rows, up_w), dot_back(grad, down_w)
    )
    dgate_ref[...] = dgate
    dup_ref[...] = dup
    hid_ref[...] = hid.T
    out_sum[...] += dot_rows(hid, down_w)
    back_sum[...] += dot_back(dgate, gate_w) + dot_back(dup, up_w)

    @pl.when(step == pl.num_programs(0) - 1)
    def _():
        out_ref[...] = out_sum[...].astype(LOW)
        back_ref[...] = back_sum[...].astype(LOW)
        turned_ref[...] = rows_ref[...].T


def expert(rows, grad, w_in, w_down, token):
    count, width = rows.shape
    hidden = w_down.shape[1]
    part = 256
    steps = hidden // part
    return call(
        expert_kernel,
        "expert",
        [
            whole(rows),
            whole(grad),
            (w_in, pl.BlockSpec((1, width, part), lambda i: (0, 0, i))),
            (w_in, pl.BlockSpec((1, width, part), lambda i: (0, 0, i + steps))),
            (w_down, pl.BlockSpec((1, part, width), lambda i: (0, i, 0))),
        ],
        [
            whole_out((count, width), LOW),
            whole_out((count, width), LOW),
            ((count, hidden), LOW, pl.BlockSpec((count, part), lambda i: (0, i))),
            ((count, hidden), LOW, pl.BlockSpec((count, part), lambda i: (0, i))),
            ((hidden, count), LOW, pl.BlockSpec((part, count), lambda i: (i, 0))),
            whole_out((width, count), LOW),
        ],
        grid=(steps,),
        token=token,
        scratch=[pltpu.VMEM((count, width), FULL), pltpu.VMEM((count, width), FULL)],
        vmem=24,
        us=20,
    )


CHUNK = 512
EXPERT_VMEM = 40


def halves_kernel(
    at_ref, x0_ref, x1_ref, g0_ref, g1_ref, w_in_ref, w_down_ref,
    back_keep, back_send, dgate_ref, dup_ref, turned_ref, hid_out, down_out, a_send, a_keep, b_ref,
    both_w, du, turned, hid_ref, down_ref, a_sum, sems, out_sems,
):
    count, width = x0_ref.shape
    half = down_ref.shape[0]
    full, rest = half // CHUNK, half % CHUNK
    first = pl.multiple_of(at_ref[2] * half, LANES)

    def copies(i, units):
        start = pl.multiple_of(i * CHUNK, LANES)
        pairs = []
        for piece in range(4):
            rows = pl.ds(piece * (width // 4), width // 4)
            for part in range(2):
                one = pl.ds(pl.multiple_of(first + start + 2 * part * half, LANES), units)
                two = pl.ds(pl.multiple_of(start + part * half, LANES), units)
                pairs.append((w_in_ref.at[0, rows, one], both_w.at[rows, two]))
            size = units // 4
            one = pl.ds(pl.multiple_of(first + start + piece * size, 16), size)
            two = pl.ds(pl.multiple_of(start + piece * size, 16), size)
            pairs.append((w_down_ref.at[0, one, :], down_ref.at[two, :]))
        return [
            pltpu.make_async_copy(one, two, sems.at[i, at]) for at, (one, two) in enumerate(pairs)
        ]

    def results(i, units):
        copies = []
        for part, ref in enumerate((dgate_ref, dup_ref)):
            one = pl.ds(pl.multiple_of(part * half + i * CHUNK, LANES), units)
            two = pl.ds(pl.multiple_of(i * CHUNK, LANES), units)
            copies.append(pltpu.make_async_copy(du.at[:, one], ref.at[:, two], out_sems.at[i, part]))
        return copies

    sizes = [CHUNK] * full + ([rest] if rest else [])
    for i, units in enumerate(sizes):
        for copy in copies(i, units):
            copy.start()

    turned[:, :count] = x0_ref[...].T
    turned[:, count:] = x1_ref[...].T
    turned_copy = pltpu.make_async_copy(turned, turned_ref, out_sems.at[len(sizes), 0])
    turned_copy.start()

    def chunk(i, units):
        for copy in copies(i, units):
            copy.wait()
        start = pl.multiple_of(i * CHUNK, LANES)
        columns = pl.ds(start, units)
        other = pl.ds(pl.multiple_of(start + half, LANES), units)
        gate_w, up_w, down_w = both_w[:, columns], both_w[:, other], down_ref[columns, :]
        for side, (x_ref, g_ref) in enumerate(((x0_ref, g0_ref), (x1_ref, g1_ref))):
            rows = pl.ds(side * count, count)
            x = x_ref[...]
            hid, dgate, dup = expert_part(
                dot_rows(x, gate_w), dot_rows(x, up_w), dot_back(g_ref[...], down_w)
            )
            hid_ref[rows, columns] = hid
            du[rows, columns] = dgate
            du[rows, other] = dup
        for copy in results(i, units):
            copy.start()

    def step(i, _):
        chunk(i, CHUNK)
        return 0

    lax.fori_loop(0, full, step, 0)
    if rest:
        chunk(full, rest)
    kept = [
        pltpu.make_async_copy(ref, out, out_sems.at[len(sizes) + 1, at])
        for at, (ref, out) in enumerate(((hid_ref, hid_out), (down_ref, down_out)))
    ]
    for copy in kept:
        copy.start()
    terms = transpose_dot(hid_ref[:count, :], g0_ref[...])
    terms = terms + transpose_dot(hid_ref[count:, :], g1_ref[...])
    middle, size = width // 2, half // 2
    b_ref[...] = terms[:, middle:].astype(LOW)
    a_sum[...] = terms[:, :middle].astype(LOW)
    a_keep[...] = a_sum[pl.ds(pl.multiple_of(at_ref[1] * size, 16), size), :]
    a_send[...] = a_sum[pl.ds(pl.multiple_of((1 - at_ref[1]) * size, 16), size), :]
    back_send[...] = dot_back(du[count:, :], both_w[...]).astype(LOW)
    back_keep[...] = dot_back(du[:count, :], both_w[...])
    turned_copy.wait()
    for copy in kept:
        copy.wait()
    for i, units in enumerate(sizes):
        for copy in results(i, units):
            copy.wait()


def expert_halves(at, rows, grads, w_in, w_down, token):
    count, width = rows[0].shape
    half = w_down.shape[1] // 2
    chunks = pl.cdiv(half, CHUNK)
    return call(
        halves_kernel,
        "expert_halves",
        [whole(array) for array in (*rows, *grads)] + [(w_in, None), (w_down, None)],
        [
            whole_out((count, width), FULL),
            whole_out((count, width), LOW),
            ((2 * count, half), LOW, None),
            ((2 * count, half), LOW, None),
            ((width, 2 * count), LOW, None),
            ((2 * count, half), LOW, None),
            ((half, width), LOW, None),
            whole_out((half // 2, width // 2), LOW),
            whole_out((half // 2, width // 2), LOW),
            whole_out((half, width // 2), LOW),
        ],
        token=token,
        prefetch=(at,),
        scratch=[
            pltpu.VMEM((width, 2 * half), LOW),
            pltpu.VMEM((2 * count, 2 * half), LOW),
            pltpu.VMEM((width, 2 * count), LOW),
            pltpu.VMEM((2 * count, half), LOW),
            pltpu.VMEM((half, width), LOW),
            pltpu.VMEM((half, width // 2), LOW),
            pltpu.SemaphoreType.DMA((chunks, 12)),
            pltpu.SemaphoreType.DMA((chunks + 2, 2)),
        ],
        vmem=EXPERT_VMEM,
        us=20,
        far_out=(7, 8, 9),
    )


def results_kernel(hid_ref, down_ref, keep_ref, send_ref):
    count = keep_ref.shape[0]
    send_ref[...] = dot_rows(hid_ref[count:, :], down_ref[...]).astype(LOW)
    keep_ref[...] = dot_rows(hid_ref[:count, :], down_ref[...]).astype(LOW)


def expert_results(hid, down_w, token):
    shape = (hid.shape[0] // 2, down_w.shape[1])
    (keep, send), token = call(
        results_kernel,
        "expert_results",
        [whole(hid), whole(down_w)],
        [whole_out(shape, LOW)] * 2,
        token=token,
        far_in=(0, 1),
        far_out=(0, 1),
        vmem=16,
        us=0.01,
    )
    return keep, send, token


def block_of(at_ref, k, blocks):
    return lax.rem(at_ref[3] + (blocks - k), blocks)


def join_kernel(at_ref, kept_ref, got_ref, out_ref):
    blocks, size, _ = out_ref.shape
    for k in range(blocks):
        rows = pl.ds(k * size, size)
        total = kept_ref[rows, :] + got_ref[rows, :].astype(FULL)
        out_ref[block_of(at_ref, k, blocks)] = total.astype(LOW)


def join(at, kept, got, blocks, token):
    rows, width = kept.shape
    (out,), token = call(
        join_kernel,
        "join",
        [whole(kept), whole(got)],
        [whole_out((blocks, rows // blocks, width), LOW)],
        token=token,
        prefetch=(at,),
        far_out=(0,),
        us=1,
    )
    return out, token


def join_peak_kernel(at_ref, kept_ref, got_ref, peak_ref, out_ref):
    blocks, size, width = out_ref.shape
    rows = kept_ref.shape[0] // blocks
    best = jnp.concatenate([peak_ref[g, :GROUP, :] for g in range(peak_ref.shape[0])], axis=0)
    best = jnp.broadcast_to(jnp.max(best, axis=1, keepdims=True), (size - rows, LANES))
    upper = best.astype(LOW)
    lower = (best - upper.astype(FULL)).astype(LOW)
    for k in range(blocks):
        part = pl.ds(k * rows, rows)
        to = block_of(at_ref, k, blocks)
        total = kept_ref[part, :].astype(FULL) + got_ref[part, :].astype(FULL)
        out_ref[to, :rows, :] = total.astype(LOW)
        out_ref[to, rows:, :] = jnp.zeros((size - rows, width), LOW)
        out_ref[to, rows:, :LANES] = upper
        out_ref[to, rows:, LANES : 2 * LANES] = lower


def join_peak(at, kept, got, peak, blocks, token):
    rows, width = kept.shape
    heads = peak.shape[0] * GROUP
    (out,), token = call(
        join_peak_kernel,
        "join_peak",
        [whole(kept), whole(got), whole(peak)],
        [whole_out((blocks, rows // blocks + heads, width), LOW)],
        token=token,
        prefetch=(at,),
        far_out=(0,),
        us=0.01,
        far_in=(0,),
    )
    return out, token


def larger_kernel(one_ref, two_ref, out_ref):
    out_ref[...] = jnp.maximum(one_ref[...], two_ref[...])


def larger(one, two, token):
    (out,), token = call(
        larger_kernel,
        "larger",
        [whole(one), whole(two)],
        [whole_out(one.shape, FULL)],
        token=token,
        us=0.5,
    )
    return out, token


def place():
    dp = lax.axis_index("dp")
    return lax.axis_index("ctx"), lax.axis_index("exp"), dp // 2, dp % 2


def to_down_plane(array):
    pairs = [
        ((1 - core) * 4 + x * 2 + core, core * 4 + x * 2 + core)
        for core in range(2)
        for x in range(2)
    ]
    return lax.ppermute(array, ("ctx", "dp"), pairs)


def in_down_plane(array):
    pairs = [
        (core * 4 + x * 2 + core, core * 4 + (1 - x) * 2 + core)
        for core in range(2)
        for x in range(2)
    ]
    return lax.ppermute(array, ("ctx", "dp"), pairs)


def in_kernel(
    at_ref, turned_ref, gate_ref, up_ref, *refs,
):
    out_refs, turned, near, results, sems, out_sems = refs[:4], *refs[4:]
    half = gate_ref.shape[1]
    starts = list(range(0, half, CHUNK))
    loads = []
    for at, (ref, to) in enumerate(((gate_ref, near.at[0]), (up_ref, near.at[1]))):
        for i, start in enumerate(starts):
            columns = pl.ds(start, min(CHUNK, half - start))
            loads.append(
                pltpu.make_async_copy(ref.at[:, columns], to.at[:, columns], sems.at[at, i])
            )
    whole_load = pltpu.make_async_copy(turned_ref, turned, sems.at[2, 0])
    whole_load.start()
    for i in range(len(starts)):
        loads[i].start()
        loads[len(starts) + i].start()
    whole_load.wait()
    size = turned.shape[0] // 4
    stores = []
    for i, start in enumerate(starts):
        columns = pl.ds(start, min(CHUNK, half - start))
        loads[i].wait()
        loads[len(starts) + i].wait()
        for block in range(4):
            ry, rx = block // 2, block % 2
            chip = (at_ref[0] ^ ry) * 2 + (at_ref[1] ^ rx)
            rows = turned[pl.ds(pl.multiple_of(chip * size, size), size), :]
            a, b = 1 - rx, 2 + 1 - ry
            results[a, ry, :, columns] = dot_rows(rows, near[0, :, columns]).astype(LOW)
            results[b, rx, :, columns] = dot_rows(rows, near[1, :, columns]).astype(LOW)
        for at, ref in enumerate(out_refs):
            copy = pltpu.make_async_copy(
                results.at[at, :, :, columns], ref.at[:, :, columns], out_sems.at[at, i]
            )
            copy.start()
            stores.append(copy)
    for copy in stores:
        copy.wait()


def in_terms(at, turned, gate, up, token):
    width, count = turned.shape
    half = gate.shape[1]
    shape = (2, width // 4, half)
    chunks = pl.cdiv(half, CHUNK)
    return call(
        in_kernel,
        "in_terms",
        [(turned, None), (gate, None), (up, None)],
        [(shape, LOW, None)] * 4,
        token=token,
        prefetch=(at,),
        scratch=[
            pltpu.VMEM((width, count), LOW),
            pltpu.VMEM((2, count, half), LOW),
            pltpu.VMEM((4, *shape), LOW),
            pltpu.SemaphoreType.DMA((3, chunks)),
            pltpu.SemaphoreType.DMA((4, chunks)),
        ],
        vmem=20,
        us=0.01,
    )


def plane_first(parts):
    a_send, a_keep, b_send, b_keep = parts
    return swapped(a_send, "dp", 2), a_keep, swapped(b_send, "ctx", 1), b_keep


def second_kernel(*refs):
    (a_ref, a_keep_ref, b_ref, b_keep_ref), (a_send_ref, b_send_ref) = refs[:4], refs[-2:]
    rows = a_ref.shape[0]
    total = a_keep_ref[...].astype(FULL) + a_ref[...].astype(FULL)
    a_send_ref[pl.ds(0, rows), :] = total.astype(LOW)
    b_send_ref[...] = (b_keep_ref[...].astype(FULL) + b_ref[...].astype(FULL)).astype(LOW)
    for beside in refs[4:-2]:
        more, width = beside.shape
        a_send_ref[pl.ds(rows, more), pl.ds(0, width)] = beside[...]


def plane_second(parts, token, beside=()):
    extra = sum(part.shape[0] for part in beside)
    (_, a_rows, a_width), (_, b_rows, b_width) = parts[0].shape, parts[2].shape
    (a_send, b_send), token = call(
        second_kernel,
        "second_terms",
        [whole(part) for part in (*parts, *beside)],
        [whole_out((a_rows + extra, a_width), LOW), whole_out((b_rows, b_width), LOW)],
        token=token,
        us=15,
        far_in=tuple(range(4, 4 + len(beside))),
        part_in={at: (1,) for at in range(4)},
        far_out=(0, 1),
        vmem=10,
    )
    return a_send, b_send, token


def down_second_kernel(at_ref, a_ref, a_keep_ref, b_ref, b_keep_ref, a_send_ref, b_send_ref):
    size = b_send_ref.shape[0]
    rows = pl.ds(pl.multiple_of((1 - at_ref[1]) * size, 16), size)
    a_send_ref[...] = (a_keep_ref[...].astype(FULL) + a_ref[...].astype(FULL)).astype(LOW)
    b_send_ref[...] = (b_keep_ref[rows, :].astype(FULL) + b_ref[rows, :].astype(FULL)).astype(LOW)


def down_second(at, parts, token, us):
    shape = parts[0].shape
    (a_send, b_send), token = call(
        down_second_kernel,
        "down_second",
        [whole(part) for part in parts],
        [whole_out(shape, LOW)] * 2,
        token=token,
        prefetch=(at,),
        us=us,
        far_out=(0, 1),
    )
    return a_send, b_send, token


def sum_kernel(one_ref, two_ref, three_ref, out_ref):
    out_ref[...] = sum(ref[...].astype(FULL) for ref in (one_ref, two_ref, three_ref)).astype(LOW)


def plane_sum(got, kept, more, token):
    (out,), token = call(
        sum_kernel,
        "plane_sum",
        [whole(got), whole(kept), whole(more)],
        [whole_out(more.shape, LOW)],
        token=token,
        far_in=(2,),
        part_in={0: (0,), 1: (0,)},
        far_out=(0,),
        us=15,
    )
    return out, token


def pair_last_kernel(a_ref, a_keep_ref, a2_ref, b_ref, out_ref):
    blocks = out_ref.shape[0]
    a = sum(ref[...].astype(FULL) for ref in (a_keep_ref, a_ref, a2_ref))
    size = b_ref.shape[0] // blocks
    for z in range(blocks):
        here = slice(z * size, (z + 1) * size)
        out_ref[z, :size, :] = a[here].astype(LOW)
        small = jnp.broadcast_to(a[blocks * size + z : blocks * size + z + 1], (EXTRA, a.shape[1]))
        out_ref[z, size : size + EXTRA, :] = small.astype(LOW)
        out_ref[z, size + EXTRA :, :] = b_ref[here, :]


def pair_last(got, kept, more, b, blocks, token):
    rows, width = b.shape
    own = slice(0, rows + EXTRA)
    (out,), token = call(
        pair_last_kernel,
        "pair_last",
        [whole(got), whole(kept), whole(more), whole(b)],
        [whole_out((blocks, 2 * rows // blocks + EXTRA, width), LOW)],
        token=token,
        far_in=(3,),
        part_in={0: (0,), 1: (0,), 2: (own,)},
        far_out=(0,),
        us=15,
        vmem=12,
    )
    return out, token


def down_last_kernel(
    at_ref, a_ref, a_keep_ref, b_ref, b_keep_ref, a2_ref, b2_ref, keep_ref, send_ref
):
    size, width = keep_ref.shape
    half = width // 2
    for out_ref, core in ((send_ref, 1 - at_ref[2]), (keep_ref, at_ref[2])):
        rows = pl.ds(pl.multiple_of(core * size, 16), size)
        there = pl.ds(pl.multiple_of((at_ref[1] * 2 + core) * size, 16), size)
        for first, refs in (
            (0, ((a_ref, rows), (a_keep_ref, rows), (a2_ref, rows))),
            (half, ((b_ref, there), (b_keep_ref, there), (b2_ref, rows))),
        ):
            total = sum(ref[cut, :].astype(FULL) for ref, cut in refs)
            out_ref[:, first : first + half] = total.astype(out_ref.dtype)


def down_last(at, parts, a2, b2, token):
    rows, half = a2.shape
    shape = (rows // 2, 2 * half)
    (keep, send), token = call(
        down_last_kernel,
        "down_last",
        [whole(array) for array in (*parts, a2, b2)],
        [whole_out(shape, FULL), whole_out(shape, LOW)],
        token=token,
        prefetch=(at,),
        us=15,
        far_out=(0, 1),
    )
    return keep, send, token


def choose_kernel(at_ref, keep_ref, got_ref, out_ref):
    mine = at_ref[0] == at_ref[2]
    out_ref[0] = jnp.where(mine, keep_ref[...], got_ref[...].astype(FULL))


def choose(at, keep, got, token):
    size, width = keep.shape
    rows = pl.BlockSpec((size // 2, width), lambda i, at: (i, 0))
    (out,), token = call(
        choose_kernel,
        "choose",
        [(keep, rows), (got, rows)],
        [((1, size, width), FULL, pl.BlockSpec((1, size // 2, width), lambda i, at: (0, i, 0)))],
        grid=(2,),
        token=token,
        prefetch=(at,),
        us=15,
    )
    return out, token


def in_last_kernel(
    at_ref, a_ref, a_keep_ref, b_ref, b_keep_ref, a2_ref, b2_ref, keep_ref, send_ref
):
    size = keep_ref.shape[1]
    for out_ref, core in ((send_ref, 1 - at_ref[2]), (keep_ref, at_ref[2])):
        rows = pl.ds(pl.multiple_of(core * size, 16), size)
        for part, refs in enumerate(((a_ref, a_keep_ref, a2_ref), (b_ref, b_keep_ref, b2_ref))):
            total = sum(ref[rows, :].astype(FULL) for ref in refs)
            out_ref[part] = total.astype(out_ref.dtype)


def in_last(at, parts, a2, b2, token):
    rows, half = b2.shape
    shape = (2, rows // 2, half)
    (keep, send), token = call(
        in_last_kernel,
        "in_last",
        [whole(array) for array in (*parts, a2, b2)],
        [whole_out(shape, FULL), whole_out(shape, LOW)],
        token=token,
        prefetch=(at,),
        us=15,
        far_in=(4, 5),
        part_in={at: (0,) for at in range(4)},
        far_out=(0, 1),
        vmem=16,
    )
    return keep, send, token


def in_end_kernel(at_ref, keep_ref, got_ref, out_ref):
    half = keep_ref.shape[2]
    for part in range(2):
        for first, value in (
            (at_ref[2], keep_ref[part]),
            (1 - at_ref[2], got_ref[part].astype(FULL)),
        ):
            start = pl.multiple_of((part * 2 + first) * half, LANES)
            out_ref[0, :, pl.ds(start, half)] = value


def in_end(at, keep, got, token):
    _, rows, half = keep.shape
    size = rows // 2
    spec = pl.BlockSpec((2, size, half), lambda i, at: (0, i, 0))
    (out,), token = call(
        in_end_kernel,
        "in_end",
        [(keep, spec), (got, spec)],
        [((1, rows, 4 * half), FULL, pl.BlockSpec((1, size, 4 * half), lambda i, at: (0, i, 0)))],
        grid=(2,),
        token=token,
        prefetch=(at,),
        us=15,
        vmem=12,
    )
    return out, token


EXTRA = 16
TABLE_LANE = 32


def turn_kernel(at_ref, *refs):
    out_ref, turned = refs[-2:]
    start = 0
    for ref in refs[:-2]:
        turned[:, start : start + ref.shape[0]] = ref[...].T
        start += ref.shape[0]
    size = out_ref.shape[0] // 16
    for to in range(16):
        device = device_at(to % 4, to // 4, at_ref)
        out_ref[pl.ds(to * size, size), :] = turned[pl.ds(device * size, size), :]


def device_at(block, z, at_ref):
    return (
        (at_ref[0] ^ (block // 2)) * 16 + z * 4 + (at_ref[1] ^ (block % 2)) * 2 + at_ref[2]
    )


def turn(at, parts, token):
    count, width = sum(part.shape[0] for part in parts), parts[0].shape[1]
    (out,), token = call(
        turn_kernel,
        "turn",
        [whole(part) for part in parts],
        [whole_out((width // 2, count), LOW)],
        token=token,
        prefetch=(at,),
        scratch=[pltpu.VMEM((width, count), LOW)],
        us=2,
        far_out=(0,),
    )
    return out, token


def shared_kernel(
    at_ref, left_ref, own_ref, other_ref, a_send_ref, a_keep_ref, b_send_ref, b_keep_ref, *, experts
):
    rows, count = left_ref.shape[0] // experts, left_ref.shape[1] // 2
    width = own_ref.shape[1]
    tokens = count // 3
    size = rows // 4
    small = own_ref[6 * tokens :, :LANES].astype(FULL) + other_ref[6 * tokens :, :LANES].astype(FULL)
    place = lax.broadcasted_iota(jnp.int32, small.shape, 0)
    for z in range(experts):
        left = left_ref[pl.ds(z * rows, rows), :]

        def product(columns, start, length):
            right = slice(start, start + length)
            one = left[:, columns : columns + length]
            two = left[:, count + columns : count + columns + length]
            total = dot_rows(one, own_ref[right, :]) + dot_rows(two, other_ref[right, :])
            return total.astype(LOW)

        a_terms = product(2 * tokens, 5 * tokens, tokens), product(tokens, 0, tokens)
        b_terms = product(0, tokens, 2 * tokens), product(0, 3 * tokens, 2 * tokens)
        for block in range(4):
            ry, rx = block // 2, block % 2
            a_ref = (a_send_ref if rx else a_keep_ref).at[ry]
            b_ref = (b_send_ref if ry else b_keep_ref).at[rx]
            here = slice(block * size, (block + 1) * size)
            for at in range(2):
                to = pl.ds((2 * z + at) * size, size)
                a_ref[to, :] = a_terms[at][here]
                b_ref[to, :] = b_terms[at][here]
    line = lax.broadcasted_iota(jnp.int32, (EXTRA, LANES), 0)
    for block in range(4):
        ry, rx = block // 2, block % 2
        a_ref = (a_send_ref if rx else a_keep_ref).at[ry]
        rows_here = jnp.zeros((EXTRA, LANES), FULL)
        for z in range(experts):
            row = jnp.where(place == device_at(block, z, at_ref), small, 0.0)
            rows_here = jnp.where(line == z, jnp.sum(row, 0, keepdims=True), rows_here)
        a_ref[2 * size * experts :, :] = jnp.zeros((EXTRA, width), LOW)
        a_ref[2 * size * experts :, :LANES] = rows_here.astype(LOW)


def shared_terms(at, left, own, other, experts, token):
    rows = left.shape[0]
    width = own.shape[1]
    b_shape = (2, rows // 2, width)
    a_shape = (2, rows // 2 + EXTRA, width)
    return call(
        functools.partial(shared_kernel, experts=experts),
        "shared_terms",
        [whole(array) for array in (left, own, other)],
        [whole_out(shape, LOW) for shape in (a_shape, a_shape, b_shape, b_shape)],
        token=token,
        prefetch=(at,),
        us=0.01,
        far_in=(0,),
        far_out=(0, 1, 2, 3),
        vmem=16,
    )


def rows_kernel(
    place_ref, plane_ref, w_query_ref, w_key_ref, w_value_ref, gain_ref,
    query_ref, key_ref, value_ref, out_ref, gain_grad_ref, ffn_ref, table_ref,
    near_query, near_key, near_value, sems,
):
    rows = query_ref.shape[0]
    at = pl.ds(pl.multiple_of(place_ref[0] * rows, rows), rows)
    pairs = ((w_query_ref, near_query), (w_key_ref, near_key), (w_value_ref, near_value))
    copies = [
        pltpu.make_async_copy(ref.at[at, :], near, sems.at[number])
        for number, (ref, near) in enumerate(pairs)
    ]
    for copy in copies:
        copy.start()
    total = sum(plane_ref[block].astype(FULL) for block in range(plane_ref.shape[0]))
    out_ref[...] = total[:rows]
    query = total[rows : 2 * rows]
    key, value = (
        total[start + EXTRA : start + EXTRA + rows] for start in (2 * rows, 3 * rows)
    )
    query_ref[...] = query
    key_ref[...] = key
    value_ref[...] = value
    small = total[2 * rows : 2 * rows + 1, :LANES]
    ffn_ref[...] = small
    table_ref[...] = pltpu.roll(jnp.broadcast_to(small, (8, LANES)), LANES - TABLE_LANE, 1)[:1]
    for copy in copies:
        copy.wait()
    sums = query * near_query[...].astype(FULL) + key * near_key[...].astype(FULL)
    sums = jnp.sum(sums + value * near_value[...].astype(FULL), axis=1, keepdims=True)
    lane = lax.broadcasted_iota(jnp.int32, (rows, LANES), 1)
    line = lax.broadcasted_iota(jnp.int32, (rows, LANES), 0)
    spread = jnp.sum(jnp.where(lane == line, sums, 0.0), 0, keepdims=True)
    device = place_ref[0]
    block = gain_ref[pl.ds(device * rows // LANES, 1), :]
    gain = pltpu.roll(jnp.broadcast_to(block, (8, LANES)), LANES - device * rows % LANES, 1)[:1]
    gain_grad_ref[...] = spread / gain


def last_rows(place_all, plane, rows, weights, gain, token):
    width = plane.shape[2]
    small = whole_out((1, LANES), FULL)
    outs, token = call(
        rows_kernel,
        "last_rows",
        [whole(plane)] + [(array, None) for array in weights] + [whole(gain.reshape(-1, LANES))],
        [whole_out((rows, width), FULL)] * 4 + [small] * 3,
        token=token,
        prefetch=(place_all.reshape(1),),
        scratch=[pltpu.VMEM((rows, width), LOW)] * 3 + [pltpu.SemaphoreType.DMA((3,))],
        us=15,
    )
    return outs, token


def clip_kernel(query_ref, key_ref, peak_ref, level_ref, query_out, key_out, factor_ref):
    heads = peak_ref.shape[0]
    width = query_ref.shape[1]
    level = jnp.sum(jnp.where(eye(heads), level_ref[...], 0.0), 1, keepdims=True)
    factor = level / jnp.maximum(peak_ref[:, :1], level)
    factor_ref[...] = jnp.broadcast_to(factor, (heads, LANES))
    head = lax.broadcasted_iota(jnp.int32, (heads, width), 0)
    lane = lax.broadcasted_iota(jnp.int32, (heads, width), 1)
    scale = jnp.sum(jnp.where(lane // HDIM == head, jnp.sqrt(factor), 0.0), 0, keepdims=True)
    query_out[...] = query_ref[...].astype(FULL) * scale
    key_out[...] = key_ref[...].astype(FULL) * scale


def clip(w_query, w_key, peak, level, token):
    rows, width = w_query.shape
    spec = pl.BlockSpec((rows // 4, width), lambda i: (i, 0))
    outs, token = call(
        clip_kernel,
        "clip",
        [(w_query, spec), (w_key, spec), whole(peak), whole(level.reshape(1, -1))],
        [((rows, width), FULL, spec)] * 2 + [whole_out(peak.shape, FULL)],
        grid=(4,),
        token=token,
        us=0.01,
        vmem=16,
    )
    return outs, token


def normed_kernel(
    packed_ref, w_query_ref, w_key_ref, w_value_ref, own_ref, other_ref, near, sems
):
    copies = [
        pltpu.make_async_copy(ref, near.at[at], sems.at[at])
        for at, ref in enumerate((w_key_ref, w_value_ref, w_query_ref))
    ]
    for copy in copies:
        copy.start()
    tokens = own_ref.shape[0]
    dq, dk, dv = (
        packed_ref[pl.ds(start * tokens, size * tokens), :]
        for start, size in ((0, 1), (1, 2), (3, 2))
    )
    copies[0].wait()
    total = dot_back(dk, near[0])
    copies[1].wait()
    total = total + dot_back(dv, near[1])
    other_ref[...] = total[:tokens].astype(LOW)
    copies[2].wait()
    own_ref[...] = total[tokens:] + dot_back(dq, near[2])


def normed_grads(packed, weights, tokens, token):
    width = packed.shape[1]
    (own, other), token = call(
        normed_kernel,
        "normed_grads",
        [whole(packed)] + [(array, None) for array in weights],
        [whole_out((tokens, width), FULL), whole_out((tokens, width), LOW)],
        token=token,
        scratch=[pltpu.VMEM((3, width, width), LOW), pltpu.SemaphoreType.DMA((3,))],
        far_in=(0,),
        far_out=(0, 1),
        us=0.01,
        vmem=14,
    )
    return own, other, token


def input_kernel(rows_ref, gain_ref, own_ref, got_ref, past_ref, out_ref):
    rows = rows_ref[...].astype(FULL)
    inverse = lax.rsqrt(jnp.mean(rows * rows, axis=1, keepdims=True) + EPSILON)
    scaled = rows * inverse
    grad = (own_ref[...] + got_ref[...].astype(FULL)) * gain_ref[...]
    along = jnp.mean(scaled * grad, axis=1, keepdims=True)
    out_ref[0] = past_ref[...] + inverse * (grad - scaled * along)


def input_grads(rows, gain, own, got, past, token):
    tokens, width = rows.shape
    start = got.shape[0] - tokens
    (out,), token = call(
        input_kernel,
        "input_grads",
        [whole(array) for array in (rows, gain, own, got, past)],
        [whole_out((1, tokens, width), FULL)],
        token=token,
        far_in=(0, 1, 2, 4),
        part_in={3: (slice(start, start + tokens), slice(0, width))},
        far_out=(0,),
        us=0.01,
    )
    return out, token


def back_kernel(
    at_ref, spread_ref, rows_ref, after_ref, gain_ref, grad_ref, weights_ref,
    total_ref, branch_ref, attended_ref, gain_grad_ref,
):
    rows = after_ref[...]
    inverse = lax.rsqrt(jnp.mean(rows * rows, axis=1, keepdims=True) + EPSILON)
    scaled = rows * inverse
    blocks, size, _ = rows_ref.shape
    grad = sum(
        transpose_dot(spread_ref[pl.ds(k * size, size), :], rows_ref[lax.rem(at_ref[3] + k, blocks)])
        for k in range(blocks)
    )
    gain_grad_ref[...] = jnp.sum(scaled * grad, axis=0, keepdims=True)
    grad = grad * gain_ref[...]
    along = jnp.mean(scaled * grad, axis=1, keepdims=True)
    total = grad_ref[...].astype(FULL) + inverse * (grad - scaled * along)
    total_ref[...] = total
    branch = total.astype(LOW)
    branch_ref[...] = branch
    attended_ref[...] = dot_back(branch, weights_ref[...]).astype(LOW)


def back_to_attention(at, spread, rows, after, gain, grad, weights, token):
    shape = after.shape
    inputs = (spread, rows, after, gain, grad, weights)
    return call(
        back_kernel,
        "back",
        [whole(array) for array in inputs],
        [
            whole_out(shape, FULL),
            whole_out(shape, LOW),
            whole_out(shape, LOW),
            whole_out((1, shape[1]), FULL),
        ],
        token=token,
        vmem=16,
        us=0.01,
        far_in=(0, 2, 4, 5),
        prefetch=(at,),
    )


def mix_kernel(at_ref, pick_ref, rows_ref, gates_ref, after_ref, out_ref, peak_ref):
    top, tokens = gates_ref.shape
    blocks = rows_ref.shape[0]
    size = pick_ref.shape[0] // blocks
    total = after_ref[...]
    gates = [to_column(gates_ref[r : r + 1, :]) for r in range(top)]
    for block in range(blocks):
        rows = rows_ref[lax.rem(at_ref[3] + block, blocks), :size, :]
        for r in range(top):
            pick = pick_ref[pl.ds(block * size, size), pl.ds(r * tokens, tokens)]
            total = total + gates[r] * transpose_dot(pick, rows)
    out_ref[0] = total.astype(LOW)
    if rows_ref.shape[1] > size:
        peaks = [
            rows_ref[block, size:, :LANES].astype(FULL)
            + rows_ref[block, size:, LANES : 2 * LANES].astype(FULL)
            for block in range(blocks)
        ]
        peak_ref[...] = functools.reduce(jnp.maximum, peaks)


def mix(at, pick, rows, gates, after, token):
    (out, peak), token = call(
        mix_kernel,
        "mix",
        [whole(pick), whole(rows), whole(gates), whole(after)],
        [whole_out((1, *after.shape), LOW), whole_out((16, LANES), FULL)],
        token=token,
        us=0.01,
        far_in=(0, 3),
        prefetch=(at,),
    )
    return out, peak, token


def local(
    block_in,
    seg_ids,
    routes,
    gates,
    buckets,
    norm_attn,
    norm_ffn,
    w_query,
    w_key,
    w_value,
    w_out_attn,
    rel_bias,
    clip_level,
    w_in,
    w_down,
    cotangent,
):
    tokens, width = block_in.shape[1:]
    heads = width // HDIM
    n_ctx, experts, n_dp = (lax.axis_size(axis) for axis in ("ctx", "exp", "dp"))
    fast = (n_ctx, experts, n_dp) == (2, 4, 4)
    devices = n_ctx * experts * n_dp
    length = n_ctx * tokens
    y, z, x, core = place()
    place_all = (y * experts + z) * n_dp + lax.axis_index("dp")
    top_count = routes.shape[-1]
    capacity = tokens * top_count * 3 // (2 * experts)
    at = jnp.stack([y, x, core, z])

    (spread, pick, mask, rows_copy, *grad_out), token = front(
        at, routes[0].T, gates[0].T, cotangent[0], seg_ids, block_in[0], experts, capacity
    )
    backs = list(range(n_ctx - 1, 0, -1))
    earlier = [
        lax.ppermute(block_in[0], "ctx", [(i, (i + back) % n_ctx) for i in range(n_ctx)])
        for back in backs
    ]
    grad_blocks = to_experts(grad_out)
    (bucket_hot, bias, w_key_near, w_value_near), _ = bias_tiles(
        buckets.reshape(1, length), rel_bias.reshape(NB, heads), tokens, (w_key, w_value)
    )

    own_rows = block_in[0].astype(FULL)
    normed_own = rms_norm(own_rows, norm_attn).astype(LOW)
    normed_all = jnp.concatenate(
        [rms_norm(rows.astype(FULL), norm_attn).astype(LOW) for rows in earlier] + [normed_own],
        axis=0,
    )
    queries = dot_rows(normed_own, w_query).astype(LOW)
    keys = dot_rows(normed_all, w_key_near).astype(LOW)
    values = dot_rows(normed_all, w_value_near).astype(LOW)
    attended, probs, peak_lanes, w_out_near = attention(
        queries, keys, values, bias, mask, (w_out_attn,)
    )
    after, sent = after_attention(
        attended, w_out_near, rows_copy, norm_ffn.reshape(1, width), spread, experts
    )

    row_blocks = to_experts(sent)
    own_gain, own_table = width // devices, NB * heads // devices
    if fast:
        expert_grad, token = side_by_side(grad_blocks, token)
        parts = (normed_all, attended)
        parts = parts + tuple(swapped(part, "dp", 1) for part in parts)
        left, token = turn(at, parts, token)
        peak, token = larger(peak_lanes, swapped(peak_lanes, "dp", 1), token)
        peak, token = larger(peak, swapped(peak, "dp", 2), token)
        peak, token = larger(peak, swapped(peak, "ctx", 1), token)
        expert_rows, token = side_by_side(row_blocks, token)
        both_rows = expert_rows, swapped(expert_rows, "dp", 1)
        both_grads = expert_grad, swapped(expert_grad, "dp", 1)
        outs, token = expert_halves(at, both_rows, both_grads, w_in, w_down, token)
        back_keep, back_send, dgate, dup, rows_turned, hid, down_w, *down = outs
        back_got = swapped(back_send, "dp", 1)
        down = swapped(down[0], "dp", 2), down[1], to_down_plane(down[2]), down[2]
        back_rows, token = join(at, back_keep, back_got, experts, token)
        back_home = over_experts(back_rows)
        first, token = in_terms(at, rows_turned, dgate, dup, token)
        first = plane_first(first)
        out_keep, out_send, token = expert_results(hid, down_w, token)
    else:
        expert_rows = jnp.concatenate(row_blocks, axis=0)
        expert_grad = jnp.concatenate(grad_blocks, axis=0)
        (out_rows, back_rows, dgate, dup, hid_turned, rows_turned), token = expert(
            expert_rows, expert_grad, w_in, w_down, token
        )
        expert_first, expert_second = (
            lax.psum_scatter(grads, ("ctx", "dp"), scatter_dimension=0, tiled=True)[None]
            for grads in (
                dot_rows(rows_turned, jnp.concatenate([dgate, dup], axis=1)),
                dot_rows(hid_turned, expert_grad),
            )
        )
        back_home, out_home = (
            jnp.stack(from_experts(list(rows.reshape(experts, capacity, width))))
            for rows in (back_rows, out_rows)
        )

    home = at if fast else jnp.zeros_like(at)
    (grad_after, grad_branch, grad_attended, grad_gain_ffn), token = back_to_attention(
        home, spread, back_home, after, norm_ffn.reshape(1, width), cotangent[0], w_out_attn, token
    )
    if fast:
        packed, token = attention_back(
            queries, keys, values, probs, grad_attended, token,
            (grad_branch, bucket_hot, grad_gain_ffn, devices),
        )
        packed_got = swapped(packed, "dp", 1)
        down_a, down_b, token = down_second(at, down, token, 20)
        plane_2, token = shared_terms(at, left, packed, packed_got, experts, token)
        plane_2 = plane_first(plane_2)
        out_send, = hold(token, out_send)
        out_got = swapped(out_send, "dp", 1)
        out_rows, token = join_peak(at, out_keep, out_got, peak, experts, token)
        out_home = over_experts(out_rows)
        normed_own_grad, normed_other_grad, token = normed_grads(
            packed, (w_query, w_key, w_value), tokens, token
        )
        in_a, in_b, token = plane_second(first, token)
        down_a, down_b = hold(token, down_a, down_b)
        down_a, down_b = to_down_plane(down_a), in_down_plane(down_b)
    else:
        dq, dk, dv, lines, token = attention_back(
            queries, keys, values, probs, grad_attended, token
        )
        lines = lines[:, :GROUP, :].reshape(heads, length + tokens)
        grad_table = lax.dot_general(
            bucket_hot, lines, (((1,), (1,)), ((), ())), precision=FULL_PRECISION
        ).reshape(-1)
        mixed, _, _ = mix(home, pick, out_home, gates[0].T, after, token)
        peak = jnp.max(peak_lanes[:, :GROUP, :], axis=-1).reshape(heads)
        peak = lax.pmax(peak, ("ctx", "exp", "dp"))
        peak = jnp.broadcast_to(peak[:, None], (heads, LANES))
        clipped, _ = clip(w_query, w_key, peak, clip_level, token)

        grad_normed = dot_back(dk, w_key) + dot_back(dv, w_value)
        grad_normed_own = grad_normed[length - tokens :] + dot_back(dq, w_query)
        for block, back in enumerate(backs):
            term = grad_normed[block * tokens : (block + 1) * tokens].astype(LOW)
            returned = lax.ppermute(term, "ctx", [((i + back) % n_ctx, i) for i in range(n_ctx)])
            grad_normed_own = grad_normed_own + returned.astype(FULL)
        _, norm_pull = jax.vjp(lambda rows: rms_norm(rows, norm_attn), own_rows)
        grad_input = (grad_after + norm_pull(grad_normed_own)[0])[None]

    if fast:
        shared_a, shared_b, token = plane_second(plane_2, token, (normed_other_grad,))
        shared_a, shared_b = swapped(shared_a, "ctx", 1), swapped(shared_b, "dp", 2)
        mixed, peak, token = mix(at, pick, out_home, gates[0].T, after, token)
        down_keep, down_send, token = down_last(at, down, down_a, down_b, token)
        down_got = swapped(down_send, "dp", 1)
        half_b, token = plane_sum(plane_2[2], plane_2[3], shared_b, token)
        in_a, in_b = hold(token, in_a, in_b)
        in_a, in_b = swapped(in_a, "ctx", 1), swapped(in_b, "dp", 2)
        plane, token = pair_last(plane_2[0], plane_2[1], shared_a, half_b, experts, token)
        plane = over_experts(plane)
        clipped, token = clip(w_query, w_key, peak, clip_level, token)
        expert_second, token = choose(at, down_keep, down_got, token)
        grad_input, token = input_grads(
            block_in[0], norm_attn.reshape(1, width), normed_own_grad, shared_a, grad_after, token
        )
        in_keep, in_send, token = in_last(at, first, in_a, in_b, token)
        in_got = swapped(in_send, "dp", 1)
        outs, token = last_rows(
            place_all, plane, own_gain, (w_query, w_key, w_value), norm_attn, token
        )
        expert_first, token = in_end(at, in_keep, in_got, token)
        shared_q, shared_k, shared_v, shared_o = outs[:4]
        small_attn, small_ffn = outs[4][0, :own_gain], outs[5][0, :own_gain]
        small_table = outs[6][0, :own_table]
    else:
        shared_q, shared_k, shared_v, shared_o = (
            lax.psum_scatter(grads, ("ctx", "exp", "dp"), scatter_dimension=0, tiled=True)
            for grads in (
                transpose_dot(normed_own, dq),
                transpose_dot(normed_all, dk),
                transpose_dot(normed_all, dv),
                transpose_dot(attended, grad_branch),
            )
        )
        small_ffn, small_table = (
            lax.dynamic_slice_in_dim(lax.psum(array, ("ctx", "exp", "dp")), place_all * own, own)
            for array, own in ((grad_gain_ffn[0], own_gain), (grad_table, own_table))
        )
        pairs = ((shared_q, w_query), (shared_k, w_key), (shared_v, w_value))
        row_sums = sum(
            jnp.sum(
                grads * lax.dynamic_slice_in_dim(weights, place_all * own_gain, own_gain).astype(FULL),
                axis=1,
            )
            for grads, weights in pairs
        )
        small_attn = row_sums / lax.dynamic_slice_in_dim(norm_attn, place_all * own_gain, own_gain)

    return (
        mixed,
        grad_input,
        small_attn,
        small_ffn,
        shared_q,
        shared_k,
        shared_v,
        shared_o,
        small_table,
        expert_first,
        expert_second,
        clipped[0],
        clipped[1],
        clipped[2][:, 0],
    )


def solution(mesh):
    tokens = P(("exp", "dp"), "ctx", None)
    everywhere = P(("ctx", "exp", "dp"))
    by_rows = P(("ctx", "exp", "dp"), None)
    by_expert = P("exp", None, None)
    expert_rows = P("exp", ("ctx", "dp"), None)
    in_specs = (tokens, P(("exp", "dp"), None), tokens, tokens) + (P(),) * 9
    in_specs = in_specs + (by_expert, by_expert, tokens)
    out_specs = (tokens, tokens, everywhere, everywhere) + (by_rows,) * 4
    out_specs = out_specs + (everywhere, expert_rows, expert_rows, P(), P(), P())
    return jax.shard_map(local, mesh=mesh, in_specs=in_specs, out_specs=out_specs, check_vma=False)
```

time: 273 us -> 225 us (0.82)
  waiting for transfers between devices: 60.1 us -> 36 us
  other arithmetic: 19.3 us -> 0.59 us
  Pallas kernels: 108 us -> 125 us
  local copies, waits for them, and re-layouts: 17.4 us -> 7.17 us
  matrix products: 11 us -> 1.87 us
    all_to_all x5 -> x3, waiting for transfers between devices: 27.6 us -> 9.48 us  [over_experts(): lax.all_to_all(blocks, 'exp', split_axis=0, concat_axis=0, tiled=True)]
    pallas_call x25 -> x32, Pallas kernels: 108 us -> 125 us  [call(): pl.pallas_call(kernel, out_shape=shapes + [pltpu.HBM((8, LANES), FULL)],...]
    ppermute x1 -> x6, starting transfers between devices: 1.23 us -> 11.7 us  [shifted(): lax.ppermute(array, axis, [(i, (i + shift) % size) for i in range(size)])]
    ppermute x26 -> x21, starting transfers between devices: 23.1 us -> 14.5 us  [swapped(): return lax.ppermute(array, axis, [(i, i ^ bit) for i in range(size)])]
    dot_general x3 -> x0, matrix products: 7.26 us -> none  [dot_back(): lax.dot_general(left, right, (((1,), (1,)), ((), ())), preferred_element_...]
    unnamed x120 -> x48, local copies, waits for them, and re-layouts: 11 us -> 4.74 us
    mul x1 -> x0, other arithmetic: 6.22 us -> none  [local(): clipped_key = w_key.astype(FULL) * column_scale[None, :]]
    ppermute x26 -> x21, waiting for transfers between devices: 27.8 us -> 22.8 us  [swapped(): return lax.ppermute(array, axis, [(i, i ^ bit) for i in range(size)])]
  transfers between devices with their start and end apart: 36 -> 34, of which waited for: 12 -> 12; matrix products, arithmetic and copies ran while one was open for 13% -> 2% of each run, Pallas kernels for 30% -> 44%
where the time goes in v2:
time: 225 us; the launch traced here: 224 us
  Pallas kernels  125 us (56%)
  starting transfers between devices  52.6 us (23%)
  waiting for transfers between devices  36 us (16%)
  local copies, waits for them, and re-layouts  7.17 us (3%)
    pallas_call x32, Pallas kernels, call(): pl.pallas_call(kernel, out_shape=shapes + [pltpu.HBM((8, LANES), FULL)],...  125 us
    ppermute x21, waiting for transfers between devices, swapped(): return lax.ppermute(array, axis, [(i, i ^ bit) for i in range(size)])  22.8 us
    all_to_all x3, starting transfers between devices, over_experts(): lax.all_to_all(blocks, 'exp', split_axis=0, concat_axis=0, tiled=True)  17.1 us
    ppermute x21, starting transfers between devices, swapped(): return lax.ppermute(array, axis, [(i, i ^ bit) for i in range(size)])  14.5 us
    ppermute x6, starting transfers between devices, shifted(): lax.ppermute(array, axis, [(i, (i + shift) % size) for i in range(size)])  11.7 us
    all_to_all x3, waiting for transfers between devices, over_experts(): lax.all_to_all(blocks, 'exp', split_axis=0, concat_axis=0, tiled=True)  9.48 us
    unnamed x48, local copies, waits for them, and re-layouts  4.74 us
  transfers between devices with their start and end apart: 34, of which 12 were waited for; matrix products, arithmetic and copies ran while one was open for 2% of the time, Pallas kernels for 44%

profile of v2, /device:TPU:0, one launch (start us, length us, event | category | flops | bytes accessed | tf_op | source)
XLA Modules:
  0.0 224.0 jit_solution(8137292834335004503)
XLA Ops:
  0.6 3.0 %collective-permute-start = (bf16[128,1024]{1,0:T(8,128)(2,1)}, bf16[128,1024]{1,0:T(8,128)(2,1)S(1)}, u32[]{:S(2)}, u32[]{:S(2)}) collective-permute-start(bf16[128,1024]{1,0:T(8,128)(2,1)} %bitcast.37), channel_id=1, source_target_pairs={{0,16},{16,0},{1,17},{17,1},{2,18},{18,2},{3,19},{19,3},{4,20},{20... | collective-permute-start | bytes 786440 | tf_op jit(solution)/shard_map/ppermute | solution.py:1503
  3.8 2.7 %front.1 = (bf16[384,128]{1,0:T(8,128)(2,1)S(1)}, bf16[384,256]{1,0:T(8,128)(2,1)}, f32[128,256]{1,0:T(8,128)S(1)}, bf16[128,1024]{1,0:T(8,128)(2,1)S(1)}, bf16[...) custom-call(s32[4]{0:T(128)S(1)} %pad_add_fusion.refs_0_, ...), custom_call_target="tpu_custom_call" | custom-call | flops 1724999936 | bytes 1 | tf_op jit(solution)/shard_map/front/pallas_call | solution.py:159
  6.5 1.6 collective-permute-start.7
  8.1 2.6 %collective-permute-start.8 = (bf16[96,1024]{1,0:T(8,128)(2,1)S(1)}, bf16[96,1024]{1,0:T(8,128)(2,1)S(1)}, u32[]{:S(2)}, u32[]{:S(2)}) collective-permute-start(bf16[96,1024]{1,0:T(8,128)(2,1)S(1)} %get-tuple-element.145), channel_id=1, source_target_pairs={{0,8},{4,12},{8,0},{12,4},{1,9},{5,13},{9,1},{13,5},{2,10},{6,14},... | collective-permute-start | bytes 589832 | tf_op jit(solution)/shard_map/ppermute | solution.py:46
  12.3 4.1 %bias_tiles.1 = (f32[32,384]{1,0:T(8,128)S(1)}, f32[16,128,256]{2,1,0:T(8,128)S(1)}, bf16[1024,1024]{1,0:T(8,128)(2,1)S(1)}, bf16[1024,1024]{1,0:T(8,128)(2,1)S(1)}, f32[8,128]{1,0:T(8,128)}) custom-call(s32[1,256]{1,0:T(1,128)S(1)} %bitcast.36, f32[32,16]{1,0:T(8,128)S(1)} %reshape.66.refs_1_, bf16[1024,1024]{1,0:T(8,128)(2,1)} %refs_3_.5, ...), custom_call_target="tpu_custom_call" | custom-call | flops 2875000064 | bytes 1 | tf_op jit(solution)/shard_map/bias_tiles/pallas_call | solution.py:159
  19.1 4.6 %attention.1 = (bf16[128,1024]{1,0:T(8,128)(2,1)S(1)}, bf16[16,128,256]{2,1,0:T(8,128)(2,1)}, f32[4,8,128]{2,1,0:T(8,128)S(1)}, bf16[1024,1024]{1,0:T(8,128)(2,1)S(1)}, f32[8,128]{1,0:T(8,128)}) custom-call(bf16[128,1024]{1,0:T(8,128)(2,1)S(1)} %convolution_convert_fusion.2.refs_0_, bf16[256,1024]{1,0:T(8,128)(2,1)S(1)} %convolution_convert_fusion.1.refs_1_, ...), custom_call_target="tpu_custom_call" | custom-call | flops 5175000064 | bytes 1 | tf_op jit(solution)/shard_map/attention/pallas_call | solution.py:159
  26.6 3.7 %collective-permute-start.1 = (bf16[96,1024]{1,0:T(8,128)(2,1)S(1)}, bf16[96,1024]{1,0:T(8,128)(2,1)S(1)}, u32[]{:S(2)}, u32[]{:S(2)}) collective-permute-start(bf16[96,1024]{1,0:T(8,128)(2,1)S(1)} %get-tuple-element.139), channel_id=1, source_target_pairs={{0,4},{4,8},{8,12},{12,0},{1,5},{5,9},{9,13},{13,1},{2,6},{6,10},{... | collective-permute-start | bytes 589832 | tf_op jit(solution)/shard_map/ppermute | solution.py:46
  30.3 1.6 collective-permute-start.2
  32.7 1.9 turn.1
  36.3 2.2 collective-permute-done.10.refs_1_
  39.0 3.2 %collective-permute-done.11.refs_1_ = f32[4,8,128]{2,1,0:T(8,128)S(1)} collective-permute-done((f32[4,8,128]{2,1,0:T(8,128)S(1)}, f32[4,8,128]{2,1,0:T(8,128)S(1)}, u32[]{:S(2)}, u32[]{:S(2)}) %collective-permute-start.11) | collective-permute-done | bytes 16416 | tf_op jit(solution)/shard_map/ppermute | solution.py:41
  42.3 2.7 %collective-permute-done.2.refs_2_ = bf16[96,1024]{1,0:T(8,128)(2,1)S(1)} collective-permute-done((bf16[96,1024]{1,0:T(8,128)(2,1)S(1)}, bf16[96,1024]{1,0:T(8,128)(2,1)S(1)}, u32[]{:S(2)}, u32[]{:S(2)}) %collective-permute-start.2) | collective-permute-done | bytes 196640 | tf_op jit(solution)/shard_map/ppermute | solution.py:46
  45.1 2.3 %collective-permute-done.12.refs_2_ = bf16[384,1024]{1,0:T(8,128)(2,1)S(1)} collective-permute-done((bf16[384,1024]{1,0:T(8,128)(2,1)S(1)}, bf16[384,1024]{1,0:T(8,128)(2,1)S(1)}, u32[]{:S(2)}, u32[]{:S(2)}) %collective-permute-start.12) | collective-permute-done | bytes 786464 | tf_op jit(solution)/shard_map/ppermute | solution.py:41
  47.3 21.8 %expert_halves.1 = (f32[384,1024]{1,0:T(8,128)S(1)}, bf16[384,1024]{1,0:T(8,128)(2,1)S(1)}, bf16[768,1408]{1,0:T(8,128)(2,1)}, bf16[768,1408]{1,0:T(8,128)(2,1)}...) custom-call(s32[4]{0:T(128)S(1)} %pad_add_fusion.refs_0_, ...), custom_call_target="tpu_custom_call" | custom-call | flops 23000000512 | bytes 1 | tf_op jit(solution)/shard_map/expert_halves/pallas_call | solution.py:159
  69.3 2.1 collective-permute-done.14.refs_2_
  71.5 1.6 join.1
  73.0 6.7 %all-to-all-start = ((bf16[4,96,1024]{2,1,0:T(8,128)(2,1)}), bf16[4,96,1024]{2,1,0:T(8,128)(2,1)S(1)}, u32[]{:S(2)}, u32[]{:S(2)}) async-start(bf16[4,96,1024]{2,1,0:T(8,128)(2,1)} %get-tuple-element.171), calls=%async_computation | async-start | bytes 1572864 | tf_op jit(solution)/shard_map/all_to_all | solution.py:58
  81.3 1.6 collective-permute-start.16
  82.9 9.2 %in_terms.1 = (bf16[2,256,1408]{2,1,0:T(8,128)(2,1)}, bf16[2,256,1408]{2,1,0:T(8,128)(2,1)}, bf16[2,256,1408]{2,1,0:T(8,128)(2,1)}, bf16[2,256,1408]{2,1,0:T(8,128)(2,1)}, f32[8,128]{1,0:T(8,128)}) custom-call(s32[4]{0:T(128)S(1)} %pad_add_fusion.refs_0_, bf16[1024,768]{1,0:T(8,128)(2,1)} %get-tuple-element.160.refs_1_, ...), custom_call_target="tpu_custom_call" | custom-call | flops 11500000 | bytes 1 | tf_op jit(solution)/shard_map/in_terms/pallas_call | solution.py:159
  92.7 3.5 %collective-permute-start.22 = (bf16[2,256,1408]{2,1,0:T(8,128)(2,1)}, bf16[2,256,1408]{2,1,0:T(8,128)(2,1)}, u32[]{:S(2)}, u32[]{:S(2)}) collective-permute-start(bf16[2,256,1408]{2,1,0:T(8,128)(2,1)} %get-tuple-element.197), channel_id=1, source_target_pairs={{0,16},{16,0},{1,17},{17,1},{2,18},{18,2},{3,19},{19,3},{4,20},{20... | collective-permute-start | bytes 4325384 | tf_op jit(solution)/shard_map/ppermute | solution.py:41
  96.2 6.2 %expert_results.1 = (bf16[384,1024]{1,0:T(8,128)(2,1)}, bf16[384,1024]{1,0:T(8,128)(2,1)}, f32[8,128]{1,0:T(8,128)}) custom-call(bf16[768,1408]{1,0:T(8,128)(2,1)} %get-tuple-element.158.refs_0_, bf16[1408,1024]{1,0:T(8,128)(2,1)} %get-tuple-element.159.refs_1_, f32[8,128]{1,0:T(8,128)} %get-tuple-element.167.refs_2_), custom_call_target="tpu_custom_call" | custom-call | flops 11500000 | bytes 1 | tf_op jit(solution)/shard_map/expert_results/pallas_call | solution.py:159
  102.5 3.8 %back.1 = (f32[128,1024]{1,0:T(8,128)S(1)}, bf16[128,1024]{1,0:T(8,128)(2,1)S(1)}, bf16[128,1024]{1,0:T(8,128)(2,1)S(1)}, f32[1,1024]{1,0:T(1,128)S(1)}, f32[8,128]{1,0:T(8,128)}) custom-call(s32[4]{0:T(128)S(1)} %pad_add_fusion.refs_0_, bf16[384,128]{1,0:T(8,128)(2,1)} %copy-done.3, bf16[4,96,1024]{2,1,0:T(8,128)(2,1)S(1)} %all-to-all-done.refs_2_, ...), custom_call_target="tpu_custom_call" | custom-call | flops 11500000 | bytes 1 | tf_op jit(solution)/shard_map/back/pallas_call | solution.py:159
  107.1 8.6 %attention_back.1 = (bf16[800,1024]{1,0:T(8,128)(2,1)S(1)}, f32[4,8,384]{2,1,0:T(8,128)}, f32[8,128]{1,0:T(8,128)}) custom-call(bf16[128,1024]{1,0:T(8,128)(2,1)} %copy-done.2, bf16[256,1024]{1,0:T(8,128)(2,1)} %copy-done.11, bf16[256,1024]{1,0:T(8,128)(2,1)} %copy-done.12, bf16[16,128,256]{2,1,0:T(8,128)(2,1)} %get-tuple-element.170.refs_3_, ...), custom_call_target="tpu_custom_call" | custom-call | flops 8049999872 | bytes 1 | tf_op jit(solution)/shard_map/attention_back/pallas_call | solution.py:159
  115.8 3.4 %down_second.1 = (bf16[704,512]{1,0:T(8,128)(2,1)}, bf16[704,512]{1,0:T(8,128)(2,1)}, f32[8,128]{1,0:T(8,128)}) custom-call(s32[4]{0:T(128)S(1)} %pad_add_fusion.refs_0_, bf16[704,512]{1,0:T(8,128)(2,1)} %collective-permute-done.16.refs_1_, bf16[704,512]{1,0:T(8,128)(2,1)S(1)} %copy-done.14, bf16[1408,512]{1,0:T(8,128)(2,1)} %collective-permute-done.17.refs_3_, ...), custom_call_target="tpu_custom_call" | custom-call | flops 23000000512 | bytes 1 | tf_op jit(solution)/shard_map/down_second/pallas_call | solution.py:159
  119.3 6.1 %shared_terms.1 = (bf16[2,272,1024]{2,1,0:T(8,128)(2,1)}, bf16[2,272,1024]{2,1,0:T(8,128)(2,1)}, bf16[2,256,1024]{2,1,0:T(8,128)(2,1)}, bf16[2,256,1024]{2,1,0:T(8,128)(2,1)}, f32[8,128]{1,0:T(8,128)}) custom-call(s32[4]{0:T(128)S(1)} %pad_add_fusion.refs_0_, bf16[512,768]{1,0:T(8,128)(2,1)} %get-tuple-element.169.refs_1_, ...), custom_call_target="tpu_custom_call" | custom-call | flops 11500000 | bytes 1 | tf_op jit(solution)/shard_map/shared_terms/pallas_call | solution.py:159
  127.9 2.9 %join_peak.1 = (bf16[4,112,1024]{2,1,0:T(8,128)(2,1)}, f32[8,128]{1,0:T(8,128)}) custom-call(s32[4]{0:T(128)S(1)} %pad_add_fusion.refs_0_, bf16[384,1024]{1,0:T(8,128)(2,1)} %get-tuple-element.168.refs_1_, bf16[384,1024]{1,0:T(8,128)(2,1)S(1)} %collective-permute-done.18.refs_2_, f32[4,8,128]{2,1,0:T(8,128)S(1)} %get-tuple-element.187.refs_3_, ...), custom_call_target="tpu_custom_call" | custom-call | flops 11500000 | bytes 1 | tf_op jit(solution)/shard_map/join_peak/pallas_call | solution.py:159
  130.9 5.1 %all-to-all-start.1 = ((bf16[4,112,1024]{2,1,0:T(8,128)(2,1)}), bf16[4,112,1024]{2,1,0:T(8,128)(2,1)S(1)}, u32[]{:S(2)}, u32[]{:S(2)}) async-start(bf16[4,112,1024]{2,1,0:T(8,128)(2,1)} %get-tuple-element.188), calls=%async_computation.1 | async-start | bytes 1835008 | tf_op jit(solution)/shard_map/all_to_all | solution.py:58
  136.0 6.6 %normed_grads.1 = (f32[128,1024]{1,0:T(8,128)}, bf16[128,1024]{1,0:T(8,128)(2,1)}, f32[8,128]{1,0:T(8,128)}) custom-call(bf16[800,1024]{1,0:T(8,128)(2,1)} %copy-done, bf16[1024,1024]{1,0:T(8,128)(2,1)} %refs_2_.5, bf16[1024,1024]{1,0:T(8,128)(2,1)} %refs_3_.5, bf16[1024,1024]{1,0:T(8,128)(2,1)} %refs_4_.3, f32[8,128]{1,0:T(8,128)} %get-tuple-element.193.refs_4_), custom_call_target="tpu_custom_call" | custom-call | flops 11500000 | bytes 1 | tf_op jit(solution)/shard_map/normed_grads/pallas_call | solution.py:159
  142.6 3.2 %second_terms.2 = (bf16[256,1408]{1,0:T(8,128)(2,1)}, bf16[256,1408]{1,0:T(8,128)(2,1)}, f32[8,128]{1,0:T(8,128)}) custom-call(bf16[2,256,1408]{2,1,0:T(8,128)(2,1)} %collective-permute-done.21.refs_0_.refs_1_, bf16[2,256,1408]{2,1,0:T(8,128)(2,1)} %get-tuple-element.196.refs_1_.refs_2_, bf16[2,256,1408]{2,1,0:T(8,128)(2,1)} %collective-permute-done.22.refs_2_.refs_3_, ...), custom_call_target="tpu_custom_call" | custom-call | flops 17250000896 | bytes 1 | tf_op jit(solution)/shard_map/second_terms/pallas_call | solution.py:159
  147.1 3.4 %collective-permute-start.25 = (bf16[704,512]{1,0:T(8,128)(2,1)}, bf16[704,512]{1,0:T(8,128)(2,1)}, u32[]{:S(2)}, u32[]{:S(2)}) collective-permute-start(bf16[704,512]{1,0:T(8,128)(2,1)} %get-tuple-element.209), channel_id=1, source_target_pairs={{0,2},{2,0},{17,19},{19,17},{4,6},{6,4},{21,23},{23,21},{8,10},{10... | collective-permute-start | bytes 2162696 | tf_op jit(solution)/shard_map/ppermute | solution.py:855
  150.5 3.6 %collective-permute-done.20.refs_2_.refs_0_ = bf16[2,256,1024]{2,1,0:T(8,128)(2,1)} collective-permute-done((bf16[2,256,1024]{2,1,0:T(8,128)(2,1)}, bf16[2,256,1024]{2,1,0:T(8,128)(2,1)}, u32[]{:S(2)}, u32[]{:S(2)}) %collective-permute-start.20) | collective-permute-done | bytes 1048608 | tf_op jit(solution)/shard_map/ppermute | solution.py:41
  154.7 2.9 %second_terms.3 = (bf16[400,1024]{1,0:T(8,128)(2,1)}, bf16[256,1024]{1,0:T(8,128)(2,1)}, f32[8,128]{1,0:T(8,128)}) custom-call(bf16[2,272,1024]{2,1,0:T(8,128)(2,1)} %collective-permute-done.19.refs_0_, bf16[2,272,1024]{2,1,0:T(8,128)(2,1)} %get-tuple-element.190.refs_1_, bf16[2,256,1024]{2,1,0:T(8,128)(2,1)} %collective-permute-done.20.refs_2_.refs_0_, ...), custom_call_target="tpu_custom_call" | custom-call | flops 17250000896 | bytes 1 | tf_op jit(solution)/shard_map/second_terms/pallas_call | solution.py:159
  157.6 1.6 collective-permute-start.27
  159.8 3.2 %mix.1 = (bf16[1,128,1024]{2,1,0:T(8,128)(2,1)}, f32[16,128]{1,0:T(8,128)S(1)}, f32[8,128]{1,0:T(8,128)}) custom-call(s32[4]{0:T(128)S(1)} %pad_add_fusion.refs_0_, bf16[384,256]{1,0:T(8,128)(2,1)} %get-tuple-element.129.refs_1_, bf16[4,112,1024]{2,1,0:T(8,128)(2,1)S(1)} %all-to-all-done.1.refs_2_, f32[2,128]{1,0:T(2,128)S(1)} %bitcast.35, ...), custom_call_target="tpu_custom_call" | custom-call | flops 11500000 | bytes 1 | tf_op jit(solution)/shard_map/mix/pallas_call | solution.py:159
  165.2 3.4 %down_last.1 = (f32[352,1024]{1,0:T(8,128)}, bf16[352,1024]{1,0:T(8,128)(2,1)}, f32[8,128]{1,0:T(8,128)}) custom-call(s32[4]{0:T(128)S(1)} %pad_add_fusion.refs_0_, bf16[704,512]{1,0:T(8,128)(2,1)} %collective-permute-done.16.refs_1_, bf16[704,512]{1,0:T(8,128)(2,1)S(1)} %copy-done.15, bf16[1408,512]{1,0:T(8,128)(2,1)} %collective-permute-done.17.refs_3_, ...), custom_call_target="tpu_custom_call" | custom-call | flops 17250000896 | bytes 1 | tf_op jit(solution)/shard_map/down_last/pallas_call | solution.py:159
  168.6 5.6 %collective-permute-done.27.refs_2_ = bf16[256,1024]{1,0:T(8,128)(2,1)} collective-permute-done((bf16[256,1024]{1,0:T(8,128)(2,1)}, bf16[256,1024]{1,0:T(8,128)(2,1)}, u32[]{:S(2)}, u32[]{:S(2)}) %collective-permute-start.27) | collective-permute-done | bytes 524320 | tf_op jit(solution)/shard_map/ppermute | solution.py:41
  174.2 2.4 %plane_sum.1 = (bf16[256,1024]{1,0:T(8,128)(2,1)}, f32[8,128]{1,0:T(8,128)}) custom-call(bf16[2,256,1024]{2,1,0:T(8,128)(2,1)} %collective-permute-done.20.refs_2_.refs_0_, bf16[2,256,1024]{2,1,0:T(8,128)(2,1)} %get-tuple-element.192.refs_3_.refs_1_, bf16[256,1024]{1,0:T(8,128)(2,1)} %collective-permute-done.27.refs_2_, f32[8,128]{1,0:T(8,128)} %get-tuple-element.215.refs_3_), custom_call_target="tpu_custom_call" | custom-call | flops 17250000896 | bytes 1 | tf_op jit(solution)/shard_map/plane_sum/pallas_call | solution.py:159
  176.7 1.6 collective-permute-start.29
  178.3 2.3 %collective-permute-done.23.refs_2_.refs_3_ = bf16[400,1024]{1,0:T(8,128)(2,1)} collective-permute-done((bf16[400,1024]{1,0:T(8,128)(2,1)}, bf16[400,1024]{1,0:T(8,128)(2,1)}, u32[]{:S(2)}, u32[]{:S(2)}) %collective-permute-start.23) | collective-permute-done | bytes 819232 | tf_op jit(solution)/shard_map/ppermute | solution.py:41
  180.6 2.9 %pair_last.1 = (bf16[4,144,1024]{2,1,0:T(8,128)(2,1)}, f32[8,128]{1,0:T(8,128)}) custom-call(bf16[2,272,1024]{2,1,0:T(8,128)(2,1)} %collective-permute-done.19.refs_0_, bf16[2,272,1024]{2,1,0:T(8,128)(2,1)} %get-tuple-element.190.refs_1_, bf16[400,1024]{1,0:T(8,128)(2,1)} %collective-permute-done.23.refs_2_.refs_3_, ...), custom_call_target="tpu_custom_call" | custom-call | flops 17250000896 | bytes 1 | tf_op jit(solution)/shard_map/pair_last/pallas_call | solution.py:159
  183.5 5.3 %all-to-all-start.2 = ((bf16[4,144,1024]{2,1,0:T(8,128)(2,1)}), bf16[4,144,1024]{2,1,0:T(8,128)(2,1)S(1)}, u32[]{:S(2)}, u32[]{:S(2)}) async-start(bf16[4,144,1024]{2,1,0:T(8,128)(2,1)} %get-tuple-element.222), calls=%async_computation.2 | async-start | bytes 2359296 | tf_op jit(solution)/shard_map/all_to_all | solution.py:58
  188.8 6.1 %clip.1 = (f32[1024,1024]{1,0:T(8,128)}, f32[1024,1024]{1,0:T(8,128)}, f32[16,128]{1,0:T(8,128)}, f32[8,128]{1,0:T(8,128)}) custom-call(bf16[1024,1024]{1,0:T(8,128)(2,1)} %refs_2_.5, bf16[1024,1024]{1,0:T(8,128)(2,1)} %refs_3_.5, f32[16,128]{1,0:T(8,128)} %copy-done.6, f32[1,16]{1,0:T(1,128)} %bitcast.42, f32[8,128]{1,0:T(8,128)} %get-tuple-element.218.refs_4_), custom_call_target="tpu_custom_call" | custom-call | flops 11500000 | bytes 1 | tf_op jit(solution)/shard_map/clip/pallas_call | solution.py:159
  196.2 3.0 %choose.1 = (f32[1,352,1024]{2,1,0:T(8,128)}, f32[8,128]{1,0:T(8,128)}) custom-call(s32[4]{0:T(128)S(1)} %pad_add_fusion.refs_0_, f32[352,1024]{1,0:T(8,128)} %get-tuple-element.211.refs_1_, bf16[352,1024]{1,0:T(8,128)(2,1)} %collective-permute-done.26.refs_2_, f32[8,128]{1,0:T(8,128)} %get-tuple-element.219.refs_3_), custom_call_target="tpu_custom_call" | custom-call | flops 17250000896 | bytes 1 | tf_op jit(solution)/shard_map/choose/pallas_call | solution.py:159
  199.2 2.5 %input_grads.1 = (f32[1,128,1024]{2,1,0:T(8,128)}, f32[8,128]{1,0:T(8,128)}) custom-call(bf16[128,1024]{1,0:T(8,128)(2,1)} %bitcast.39, f32[1,1024]{1,0:T(1,128)} %bitcast.30, f32[128,1024]{1,0:T(8,128)} %get-tuple-element.203.refs_2_, bf16[400,1024]{1,0:T(8,128)(2,1)} %collective-permute-done.23.refs_2_.refs_3_, f32[128,1024]{1,0:T(8,128)} %copy-done.1, ...), custom_call_target="tpu_custom_call" | custom-call | flops 11500000 | bytes 1 | tf_op jit(solution)/shard_map/input_grads/pallas_call | solution.py:159
  202.8 4.4 %in_last.1 = (f32[2,128,1408]{2,1,0:T(8,128)}, bf16[2,128,1408]{2,1,0:T(8,128)(2,1)}, f32[8,128]{1,0:T(8,128)}) custom-call(s32[4]{0:T(128)S(1)} %pad_add_fusion.refs_0_, bf16[2,256,1408]{2,1,0:T(8,128)(2,1)} %collective-permute-done.21.refs_0_.refs_1_, bf16[2,256,1408]{2,1,0:T(8,128)(2,1)} %get-tuple-element.196.refs_1_.refs_2_, ...), custom_call_target="tpu_custom_call" | custom-call | flops 17250000896 | bytes 1 | tf_op jit(solution)/shard_map/in_last/pallas_call | solution.py:159
  207.3 9.5 %all-to-all-done.2.refs_1_ = bf16[4,144,1024]{2,1,0:T(8,128)(2,1)S(1)} async-done(((bf16[4,144,1024]{2,1,0:T(8,128)(2,1)}), bf16[4,144,1024]{2,1,0:T(8,128)(2,1)S(1)}, u32[]{:S(2)}, u32[]{:S(2)}) %all-to-all-start.2) | async-done | bytes 1179680 | tf_op jit(solution)/shard_map/all_to_all | solution.py:58
  216.7 1.9 last_rows.1
  220.6 3.4 %in_end.1 = (f32[1,128,5632]{2,1,0:T(8,128)}, f32[8,128]{1,0:T(8,128)}) custom-call(s32[4]{0:T(128)S(1)} %pad_add_fusion.refs_0_, f32[2,128,1408]{2,1,0:T(8,128)} %get-tuple-element.236.refs_1_, bf16[2,128,1408]{2,1,0:T(8,128)(2,1)} %copy-done.23, f32[8,128]{1,0:T(8,128)} %get-tuple-element.238.refs_3_), custom_call_target="tpu_custom_call" | custom-call | flops 17250000896 | bytes 1 | tf_op jit(solution)/shard_map/in_end/pallas_call | solution.py:159
  (117 shorter events, 25.1 us)
Async XLA Ops:
  0.6 15.8 %collective-permute-start = (bf16[128,1024]{1,0:T(8,128)(2,1)}, bf16[128,1024]{1,0:T(8,128)(2,1)S(1)}, u32[]{:S(2)}, u32[]{:S(2)}) collective-permute-start(bf16[128,1024]{1,0:T(8,128)(2,1)} %bitcast.37), channel_id=1, source_target_pairs={{0,16},{16,0},{1,17},{17,1},{2,18},{18,2},{3,19},{19,3},{4,20},{20... | collective-permute-start | bytes 786440 | tf_op jit(solution)/shard_map/ppermute | solution.py:1503
  3.8 8.3 %copy-start.17 = (bf16[1,128,1024]{2,1,0:T(8,128)(2,1)S(1)}, bf16[1,128,1024]{2,1,0:T(8,128)(2,1)}, u32[]{:S(2)}) copy-start(bf16[1,128,1024]{2,1,0:T(8,128)(2,1)} %param.16) | copy-start | bytes 786436
  3.8 8.5 %copy-start.18 = (f32[512]{0:T(512)S(1)}, f32[512]{0:T(512)}, u32[]{:S(2)}) copy-start(f32[512]{0:T(512)} %param.27) | copy-start | bytes 6148
  3.8 8.5 %copy-start.10 = (s32[256]{0:T(256)S(1)}, s32[256]{0:T(256)}, u32[]{:S(2)}) copy-start(s32[256]{0:T(256)} %param.20) | copy-start | bytes 3076
  6.5 18.0 %copy-start.3 = (bf16[384,128]{1,0:T(8,128)(2,1)}, bf16[384,128]{1,0:T(8,128)(2,1)S(1)}, u32[]{:S(2)}) copy-start(bf16[384,128]{1,0:T(8,128)(2,1)S(1)} %get-tuple-element.137.refs_4_.refs_1_) | copy-start | bytes 294916
  6.5 17.8 %collective-permute-start.7 = (bf16[96,1024]{1,0:T(8,128)(2,1)S(1)}, bf16[96,1024]{1,0:T(8,128)(2,1)S(1)}, u32[]{:S(2)}, u32[]{:S(2)}) collective-permute-start(bf16[96,1024]{1,0:T(8,128)(2,1)S(1)} %get-tuple-element.144), channel_id=1, source_target_pairs={{0,4},{4,8},{8,12},{12,0},{1,5},{5,9},{9,13},{13,1},{2,6},{6,10},{... | collective-permute-start | bytes 589832 | tf_op jit(solution)/shard_map/ppermute | solution.py:46
  8.1 16.2 %collective-permute-start.8 = (bf16[96,1024]{1,0:T(8,128)(2,1)S(1)}, bf16[96,1024]{1,0:T(8,128)(2,1)S(1)}, u32[]{:S(2)}, u32[]{:S(2)}) collective-permute-start(bf16[96,1024]{1,0:T(8,128)(2,1)S(1)} %get-tuple-element.145), channel_id=1, source_target_pairs={{0,8},{4,12},{8,0},{12,4},{1,9},{5,13},{9,1},{13,5},{2,10},{6,14},... | collective-permute-start | bytes 589832 | tf_op jit(solution)/shard_map/ppermute | solution.py:46
  10.7 13.6 %collective-permute-start.9 = (bf16[96,1024]{1,0:T(8,128)(2,1)S(1)}, bf16[96,1024]{1,0:T(8,128)(2,1)S(1)}, u32[]{:S(2)}, u32[]{:S(2)}) collective-permute-start(bf16[96,1024]{1,0:T(8,128)(2,1)S(1)} %get-tuple-element.146), channel_id=1, source_target_pairs={{0,12},{4,0},{8,4},{12,8},{1,13},{5,1},{9,5},{13,9},{2,14},{6,2},{... | collective-permute-start | bytes 589832 | tf_op jit(solution)/shard_map/ppermute | solution.py:46
  12.3 4.3 %copy-start.4 = (f32[1024]{0:T(1024)S(1)}, f32[1024]{0:T(1024)}, u32[]{:S(2)}) copy-start(f32[1024]{0:T(1024)} %param.21) | copy-start | bytes 12292
  12.3 4.8 %copy-start.16 = (bf16[1024,1024]{1,0:T(8,128)(2,1)S(1)}, bf16[1024,1024]{1,0:T(8,128)(2,1)}, u32[]{:S(2)}) copy-start(bf16[1024,1024]{1,0:T(8,128)(2,1)} %refs_2_.5) | copy-start | bytes 6291460
  17.6 15.2 %collective-permute-start.5 = (bf16[256,1024]{1,0:T(8,128)(2,1)S(1)}, bf16[256,1024]{1,0:T(8,128)(2,1)S(1)}, u32[]{:S(2)}, u32[]{:S(2)}) collective-permute-start(bf16[256,1024]{1,0:T(8,128)(2,1)S(1)} %pad_maximum_fusion.refs_1_), channel_id=1, source_target_pairs={{0,1},{1,0},{2,3},{3,2},{4,5},{5,4},{6,7},{7,6},{8,9},{9,8},{10,11... | collective-permute-start | bytes 1572872 | tf_op jit(solution)/shard_map/ppermute | solution.py:41
  18.4 5.4 %copy-start.11 = (bf16[256,1024]{1,0:T(8,128)(2,1)}, bf16[256,1024]{1,0:T(8,128)(2,1)S(1)}, u32[]{:S(2)}) copy-start(bf16[256,1024]{1,0:T(8,128)(2,1)S(1)} %convolution_convert_fusion.1.refs_1_) | copy-start | bytes 1572868
  19.1 4.6 %copy-start.12 = (bf16[256,1024]{1,0:T(8,128)(2,1)}, bf16[256,1024]{1,0:T(8,128)(2,1)S(1)}, u32[]{:S(2)}) copy-start(bf16[256,1024]{1,0:T(8,128)(2,1)S(1)} %convolution_convert_fusion.refs_2_) | copy-start | bytes 1572868
  23.7 8.2 %collective-permute-start.6 = (bf16[128,1024]{1,0:T(8,128)(2,1)S(1)}, bf16[128,1024]{1,0:T(8,128)(2,1)S(1)}, u32[]{:S(2)}, u32[]{:S(2)}) collective-permute-start(bf16[128,1024]{1,0:T(8,128)(2,1)S(1)} %get-tuple-element.134.refs_0_.refs_2_), channel_id=1, source_target_pairs={{0,1},{1,0},{2,3},{3,2},{4,5},{5,4},{6,7},{7,6},{8,9},{9,8},{10,11... | collective-permute-start | bytes 786440 | tf_op jit(solution)/shard_map/ppermute | solution.py:41
  24.4 10.3 %collective-permute-start.4 = (f32[4,8,128]{2,1,0:T(8,128)S(1)}, f32[4,8,128]{2,1,0:T(8,128)S(1)}, u32[]{:S(2)}, u32[]{:S(2)}) collective-permute-start(f32[4,8,128]{2,1,0:T(8,128)S(1)} %get-tuple-element.142.refs_0_), channel_id=1, source_target_pairs={{0,1},{1,0},{2,3},{3,2},{4,5},{5,4},{6,7},{7,6},{8,9},{9,8},{10,11... | collective-permute-start | bytes 49160 | tf_op jit(solution)/shard_map/ppermute | solution.py:41
  26.6 15.7 %collective-permute-start.1 = (bf16[96,1024]{1,0:T(8,128)(2,1)S(1)}, bf16[96,1024]{1,0:T(8,128)(2,1)S(1)}, u32[]{:S(2)}, u32[]{:S(2)}) collective-permute-start(bf16[96,1024]{1,0:T(8,128)(2,1)S(1)} %get-tuple-element.139), channel_id=1, source_target_pairs={{0,4},{4,8},{8,12},{12,0},{1,5},{5,9},{9,13},{13,1},{2,6},{6,10},{... | collective-permute-start | bytes 589832 | tf_op jit(solution)/shard_map/ppermute | solution.py:46
  30.3 14.6 %collective-permute-start.2 = (bf16[96,1024]{1,0:T(8,128)(2,1)S(1)}, bf16[96,1024]{1,0:T(8,128)(2,1)S(1)}, u32[]{:S(2)}, u32[]{:S(2)}) collective-permute-start(bf16[96,1024]{1,0:T(8,128)(2,1)S(1)} %get-tuple-element.140), channel_id=1, source_target_pairs={{0,8},{4,12},{8,0},{12,4},{1,9},{5,13},{9,1},{13,5},{2,10},{6,14},... | collective-permute-start | bytes 589832 | tf_op jit(solution)/shard_map/ppermute | solution.py:46
  31.9 13.0 %collective-permute-start.3 = (bf16[96,1024]{1,0:T(8,128)(2,1)S(1)}, bf16[96,1024]{1,0:T(8,128)(2,1)S(1)}, u32[]{:S(2)}, u32[]{:S(2)}) collective-permute-start(bf16[96,1024]{1,0:T(8,128)(2,1)S(1)} %get-tuple-element.141), channel_id=1, source_target_pairs={{0,12},{4,0},{8,4},{12,8},{1,13},{5,1},{9,5},{13,9},{2,14},{6,2},{... | collective-permute-start | bytes 589832 | tf_op jit(solution)/shard_map/ppermute | solution.py:46
  34.7 3.8 %collective-permute-start.10 = (f32[4,8,128]{2,1,0:T(8,128)S(1)}, f32[4,8,128]{2,1,0:T(8,128)S(1)}, u32[]{:S(2)}, u32[]{:S(2)}) collective-permute-start(f32[4,8,128]{2,1,0:T(8,128)S(1)} %get-tuple-element.150.refs_0_), channel_id=1, source_target_pairs={{0,2},{1,3},{2,0},{3,1},{4,6},{5,7},{6,4},{7,5},{8,10},{9,11},{10,... | collective-permute-start | bytes 49160 | tf_op jit(solution)/shard_map/ppermute | solution.py:41
  38.5 3.7 %collective-permute-start.11 = (f32[4,8,128]{2,1,0:T(8,128)S(1)}, f32[4,8,128]{2,1,0:T(8,128)S(1)}, u32[]{:S(2)}, u32[]{:S(2)}) collective-permute-start(f32[4,8,128]{2,1,0:T(8,128)S(1)} %get-tuple-element.152.refs_0_), channel_id=1, source_target_pairs={{0,16},{16,0},{1,17},{17,1},{2,18},{18,2},{3,19},{19,3},{4,20},{20... | collective-permute-start | bytes 49160 | tf_op jit(solution)/shard_map/ppermute | solution.py:41
  39.0 6.0 %collective-permute-start.13 = (bf16[384,1024]{1,0:T(8,128)(2,1)S(1)}, bf16[384,1024]{1,0:T(8,128)(2,1)S(1)}, u32[]{:S(2)}, u32[]{:S(2)}) collective-permute-start(bf16[384,1024]{1,0:T(8,128)(2,1)S(1)} %get-tuple-element.156.refs_3_), channel_id=1, source_target_pairs={{0,1},{1,0},{2,3},{3,2},{4,5},{5,4},{6,7},{7,6},{8,9},{9,8},{10,11... | collective-permute-start | bytes 2359304 | tf_op jit(solution)/shard_map/ppermute | solution.py:41
  45.0 2.4 %collective-permute-start.12 = (bf16[384,1024]{1,0:T(8,128)(2,1)S(1)}, bf16[384,1024]{1,0:T(8,128)(2,1)S(1)}, u32[]{:S(2)}, u32[]{:S(2)}) collective-permute-start(bf16[384,1024]{1,0:T(8,128)(2,1)S(1)} %get-tuple-element.155.refs_1_), channel_id=1, source_target_pairs={{0,1},{1,0},{2,3},{3,2},{4,5},{5,4},{6,7},{7,6},{8,9},{9,8},{10,11... | collective-permute-start | bytes 2359304 | tf_op jit(solution)/shard_map/ppermute | solution.py:41
  69.1 2.4 %collective-permute-start.14 = (bf16[384,1024]{1,0:T(8,128)(2,1)S(1)}, bf16[384,1024]{1,0:T(8,128)(2,1)S(1)}, u32[]{:S(2)}, u32[]{:S(2)}) collective-permute-start(bf16[384,1024]{1,0:T(8,128)(2,1)S(1)} %get-tuple-element.164), channel_id=1, source_target_pairs={{0,1},{1,0},{2,3},{3,2},{4,5},{5,4},{6,7},{7,6},{8,9},{9,8},{10,11... | collective-permute-start | bytes 2359304 | tf_op jit(solution)/shard_map/ppermute | solution.py:41
  71.5 8.3 %copy-start.9 = (bf16[1408,512]{1,0:T(8,128)(2,1)S(1)}, bf16[1408,512]{1,0:T(8,128)(2,1)}, u32[]{:S(2)}) copy-start(bf16[1408,512]{1,0:T(8,128)(2,1)} %get-tuple-element.182.refs_4_) | copy-start | bytes 4325380
  71.5 9.8 %copy-start.19 = (bf16[704,512]{1,0:T(8,128)(2,1)S(1)}, bf16[704,512]{1,0:T(8,128)(2,1)}, u32[]{:S(2)}) copy-start(bf16[704,512]{1,0:T(8,128)(2,1)} %get-tuple-element.180) | copy-start | bytes 2162692
  73.0 29.4 %all-to-all-start = ((bf16[4,96,1024]{2,1,0:T(8,128)(2,1)}), bf16[4,96,1024]{2,1,0:T(8,128)(2,1)S(1)}, u32[]{:S(2)}, u32[]{:S(2)}) async-start(bf16[4,96,1024]{2,1,0:T(8,128)(2,1)} %get-tuple-element.171), calls=%async_computation | async-start | bytes 1572864 | tf_op jit(solution)/shard_map/all_to_all | solution.py:58
  79.8 36.0 %collective-permute-start.17 = (bf16[1408,512]{1,0:T(8,128)(2,1)S(1)}, bf16[1408,512]{1,0:T(8,128)(2,1)}, u32[]{:S(2)}, u32[]{:S(2)}) collective-permute-start(bf16[1408,512]{1,0:T(8,128)(2,1)S(1)} %copy-done.9), channel_id=1, source_target_pairs={{16,0},{18,2},{1,17},{3,19},{20,4},{22,6},{5,21},{7,23},{24,8},{26... | collective-permute-start | bytes 4325384 | tf_op jit(solution)/shard_map/ppermute | solution.py:846
  81.3 34.5 %collective-permute-start.16 = (bf16[704,512]{1,0:T(8,128)(2,1)S(1)}, bf16[704,512]{1,0:T(8,128)(2,1)}, u32[]{:S(2)}, u32[]{:S(2)}) collective-permute-start(bf16[704,512]{1,0:T(8,128)(2,1)S(1)} %copy-done.19), channel_id=1, source_target_pairs={{0,2},{1,3},{2,0},{3,1},{4,6},{5,7},{6,4},{7,5},{8,10},{9,11},{10,... | collective-permute-start | bytes 2162696 | tf_op jit(solution)/shard_map/ppermute | solution.py:41
  92.1 50.5 %collective-permute-start.21 = (bf16[2,256,1408]{2,1,0:T(8,128)(2,1)}, bf16[2,256,1408]{2,1,0:T(8,128)(2,1)}, u32[]{:S(2)}, u32[]{:S(2)}) collective-permute-start(bf16[2,256,1408]{2,1,0:T(8,128)(2,1)} %get-tuple-element.195), channel_id=1, source_target_pairs={{0,2},{1,3},{2,0},{3,1},{4,6},{5,7},{6,4},{7,5},{8,10},{9,11},{10,... | collective-permute-start | bytes 4325384 | tf_op jit(solution)/shard_map/ppermute | solution.py:41
  92.7 49.9 %collective-permute-start.22 = (bf16[2,256,1408]{2,1,0:T(8,128)(2,1)}, bf16[2,256,1408]{2,1,0:T(8,128)(2,1)}, u32[]{:S(2)}, u32[]{:S(2)}) collective-permute-start(bf16[2,256,1408]{2,1,0:T(8,128)(2,1)} %get-tuple-element.197), channel_id=1, source_target_pairs={{0,16},{16,0},{1,17},{17,1},{2,18},{18,2},{3,19},{19,3},{4,20},{20... | collective-permute-start | bytes 4325384 | tf_op jit(solution)/shard_map/ppermute | solution.py:41
  107.1 8.7 %copy-start.14 = (bf16[704,512]{1,0:T(8,128)(2,1)S(1)}, bf16[704,512]{1,0:T(8,128)(2,1)}, u32[]{:S(2)}) copy-start(bf16[704,512]{1,0:T(8,128)(2,1)} %get-tuple-element.181.refs_2_) | copy-start | bytes 2162692
  115.7 3.6 %collective-permute-start.15 = (bf16[800,1024]{1,0:T(8,128)(2,1)S(1)}, bf16[800,1024]{1,0:T(8,128)(2,1)S(1)}, u32[]{:S(2)}, u32[]{:S(2)}) collective-permute-start(bf16[800,1024]{1,0:T(8,128)(2,1)S(1)} %get-tuple-element.179.refs_2_.refs_0_), channel_id=1, source_target_pairs={{0,1},{1,0},{2,3},{3,2},{4,5},{5,4},{6,7},{7,6},{8,9},{9,8},{10,11... | collective-permute-start | bytes 4915208 | tf_op jit(solution)/shard_map/ppermute | solution.py:41
  125.4 2.6 %collective-permute-start.18 = (bf16[384,1024]{1,0:T(8,128)(2,1)}, bf16[384,1024]{1,0:T(8,128)(2,1)S(1)}, u32[]{:S(2)}, u32[]{:S(2)}) collective-permute-start(bf16[384,1024]{1,0:T(8,128)(2,1)} %hold.3), channel_id=1, source_target_pairs={{0,1},{1,0},{2,3},{3,2},{4,5},{5,4},{6,7},{7,6},{8,9},{9,8},{10,11... | collective-permute-start | bytes 2359304 | tf_op jit(solution)/shard_map/ppermute | solution.py:41
  125.6 28.6 %collective-permute-start.20 = (bf16[2,256,1024]{2,1,0:T(8,128)(2,1)}, bf16[2,256,1024]{2,1,0:T(8,128)(2,1)}, u32[]{:S(2)}, u32[]{:S(2)}) collective-permute-start(bf16[2,256,1024]{2,1,0:T(8,128)(2,1)} %get-tuple-element.191), channel_id=1, source_target_pairs={{0,16},{16,0},{1,17},{17,1},{2,18},{18,2},{3,19},{19,3},{4,20},{20... | collective-permute-start | bytes 3145736 | tf_op jit(solution)/shard_map/ppermute | solution.py:41
  125.6 29.1 %collective-permute-start.19 = (bf16[2,272,1024]{2,1,0:T(8,128)(2,1)}, bf16[2,272,1024]{2,1,0:T(8,128)(2,1)}, u32[]{:S(2)}, u32[]{:S(2)}) collective-permute-start(bf16[2,272,1024]{2,1,0:T(8,128)(2,1)} %get-tuple-element.189), channel_id=1, source_target_pairs={{0,2},{1,3},{2,0},{3,1},{4,6},{5,7},{6,4},{7,5},{8,10},{9,11},{10,... | collective-permute-start | bytes 3342344 | tf_op jit(solution)/shard_map/ppermute | solution.py:41
  130.9 29.0 %all-to-all-start.1 = ((bf16[4,112,1024]{2,1,0:T(8,128)(2,1)}), bf16[4,112,1024]{2,1,0:T(8,128)(2,1)S(1)}, u32[]{:S(2)}, u32[]{:S(2)}) async-start(bf16[4,112,1024]{2,1,0:T(8,128)(2,1)} %get-tuple-element.188), calls=%async_computation.1 | async-start | bytes 1835008 | tf_op jit(solution)/shard_map/all_to_all | solution.py:58
  145.8 17.2 %collective-permute-start.24 = (bf16[704,512]{1,0:T(8,128)(2,1)}, bf16[704,512]{1,0:T(8,128)(2,1)S(1)}, u32[]{:S(2)}, u32[]{:S(2)}) collective-permute-start(bf16[704,512]{1,0:T(8,128)(2,1)} %get-tuple-element.208), channel_id=1, source_target_pairs={{16,0},{18,2},{1,17},{3,19},{20,4},{22,6},{5,21},{7,23},{24,8},{26... | collective-permute-start | bytes 2162696 | tf_op jit(solution)/shard_map/ppermute | solution.py:846
  147.1 17.0 %collective-permute-start.25 = (bf16[704,512]{1,0:T(8,128)(2,1)}, bf16[704,512]{1,0:T(8,128)(2,1)}, u32[]{:S(2)}, u32[]{:S(2)}) collective-permute-start(bf16[704,512]{1,0:T(8,128)(2,1)} %get-tuple-element.209), channel_id=1, source_target_pairs={{0,2},{2,0},{17,19},{19,17},{4,6},{6,4},{21,23},{23,21},{8,10},{10... | collective-permute-start | bytes 2162696 | tf_op jit(solution)/shard_map/ppermute | solution.py:855
  154.7 5.1 %copy-start.8 = (f32[1,128,2]{1,2,0:T(2,128)S(1)}, f32[1,128,2]{1,2,0:T(2,128)}, u32[]{:S(2)}) copy-start(f32[1,128,2]{1,2,0:T(2,128)} %param.19) | copy-start | bytes 3076
  157.6 16.6 %collective-permute-start.27 = (bf16[256,1024]{1,0:T(8,128)(2,1)}, bf16[256,1024]{1,0:T(8,128)(2,1)}, u32[]{:S(2)}, u32[]{:S(2)}) collective-permute-start(bf16[256,1024]{1,0:T(8,128)(2,1)} %get-tuple-element.214), channel_id=1, source_target_pairs={{0,2},{1,3},{2,0},{3,1},{4,6},{5,7},{6,4},{7,5},{8,10},{9,11},{10,... | collective-permute-start | bytes 1572872 | tf_op jit(solution)/shard_map/ppermute | solution.py:41
  159.2 21.4 %collective-permute-start.23 = (bf16[400,1024]{1,0:T(8,128)(2,1)}, bf16[400,1024]{1,0:T(8,128)(2,1)}, u32[]{:S(2)}, u32[]{:S(2)}) collective-permute-start(bf16[400,1024]{1,0:T(8,128)(2,1)} %get-tuple-element.204), channel_id=1, source_target_pairs={{0,16},{16,0},{1,17},{17,1},{2,18},{18,2},{3,19},{19,3},{4,20},{20... | collective-permute-start | bytes 2457608 | tf_op jit(solution)/shard_map/ppermute | solution.py:41
  163.0 5.6 %copy-start.6 = (f32[16,128]{1,0:T(8,128)}, f32[16,128]{1,0:T(8,128)S(1)}, u32[]{:S(2)}) copy-start(f32[16,128]{1,0:T(8,128)S(1)} %get-tuple-element.213.refs_2_) | copy-start | bytes 24580
  176.7 25.0 %collective-permute-start.28 = (bf16[256,1408]{1,0:T(8,128)(2,1)}, bf16[256,1408]{1,0:T(8,128)(2,1)S(1)}, u32[]{:S(2)}, u32[]{:S(2)}) collective-permute-start(bf16[256,1408]{1,0:T(8,128)(2,1)} %get-tuple-element.225), channel_id=1, source_target_pairs={{0,16},{16,0},{1,17},{17,1},{2,18},{18,2},{3,19},{19,3},{4,20},{20... | collective-permute-start | bytes 2162696 | tf_op jit(solution)/shard_map/ppermute | solution.py:41
  176.7 25.0 %collective-permute-start.29 = (bf16[256,1408]{1,0:T(8,128)(2,1)}, bf16[256,1408]{1,0:T(8,128)(2,1)S(1)}, u32[]{:S(2)}, u32[]{:S(2)}) collective-permute-start(bf16[256,1408]{1,0:T(8,128)(2,1)} %get-tuple-element.226), channel_id=1, source_target_pairs={{0,2},{1,3},{2,0},{3,1},{4,6},{5,7},{6,4},{7,5},{8,10},{9,11},{10,... | collective-permute-start | bytes 2162696 | tf_op jit(solution)/shard_map/ppermute | solution.py:41
  178.3 17.9 %collective-permute-start.26 = (bf16[352,1024]{1,0:T(8,128)(2,1)S(1)}, bf16[352,1024]{1,0:T(8,128)(2,1)}, u32[]{:S(2)}, u32[]{:S(2)}) collective-permute-start(bf16[352,1024]{1,0:T(8,128)(2,1)S(1)} %copy-done.22), channel_id=1, source_target_pairs={{0,1},{1,0},{2,3},{3,2},{4,5},{5,4},{6,7},{7,6},{8,9},{9,8},{10,11... | collective-permute-start | bytes 2162696 | tf_op jit(solution)/shard_map/ppermute | solution.py:41
  183.5 33.2 %all-to-all-start.2 = ((bf16[4,144,1024]{2,1,0:T(8,128)(2,1)}), bf16[4,144,1024]{2,1,0:T(8,128)(2,1)S(1)}, u32[]{:S(2)}, u32[]{:S(2)}) async-start(bf16[4,144,1024]{2,1,0:T(8,128)(2,1)} %get-tuple-element.222), calls=%async_computation.2 | async-start | bytes 2359296 | tf_op jit(solution)/shard_map/all_to_all | solution.py:58
  202.8 13.9 %copy-start.5 = (f32[1024]{0:T(1024)S(1)}, f32[1024]{0:T(1024)}, u32[]{:S(2)}) copy-start(f32[1024]{0:T(1024)} %param.21) | copy-start | bytes 12292
  207.2 12.5 %collective-permute-start.30 = (bf16[2,128,1408]{2,1,0:T(8,128)(2,1)}, bf16[2,128,1408]{2,1,0:T(8,128)(2,1)S(1)}, u32[]{:S(2)}, u32[]{:S(2)}) collective-permute-start(bf16[2,128,1408]{2,1,0:T(8,128)(2,1)} %get-tuple-element.237), channel_id=1, source_target_pairs={{0,1},{1,0},{2,3},{3,2},{4,5},{5,4},{6,7},{7,6},{8,9},{9,8},{10,11... | collective-permute-start | bytes 2162696 | tf_op jit(solution)/shard_map/ppermute | solution.py:41
  (10 other events, 15.4 us)
